TPU v7x, 128 devices: a whole 4x4x4 slice. The times are simulated.
128 devices in a mesh: comp: 2 (over x_lo), tile: 64 (over z, x_hi, y, core).
Axes of the slice: x: 4 (x_hi: 2, x_lo: 2; x = x_hi * 2 + x_lo), y: 4, z: 4, core: 2. Of those that a mesh axis runs over, the one named last changes fastest.
Arguments:
- atm_state: bfloat16 [256, 4096, 256], P(None, ('comp', 'tile')), may hold values from -6 to 6
- atm_sea: int32 [4096, 256], P(('comp', 'tile')), may hold values 0 or 1
- zonal_courant: float32 [256], replicated, may hold values from 0.05 to 0.45
- atm_vertical: bfloat16 [256, 256], replicated, may hold values from -1 to 1
- ocean_state: float32 [160, 2048, 128], P(None, ('comp', 'tile')), may hold values from -6 to 6
- ocean_sea: int32 [2048, 128], P(('comp', 'tile')), may hold values 0 or 1
- flux_in: float32 [2, 2048, 128], P(None, ('comp', 'tile')), may hold values from -6 to 6
- ocean_vertical: float32 [160, 160], replicated, may hold values from -1 to 1
- remap_owner: int32 [8192, 4], P(('comp', 'tile')), may hold values from 0 to 127, all different within a row; in each aligned block of 64 rows (0 to 63, 64 to 127, ...) at most 4 rows name the same one
- remap_block: int32 [8192, 4], P(('comp', 'tile')), may hold values from 0 to 15
- remap_weight: bfloat16 [8192, 4, 128, 128], P(('comp', 'tile')), may hold values from 0 to 0.00390625
Outputs:
- atm_next: bfloat16 [256, 4096, 256], P(None, ('comp', 'tile'))
- ocean_next: float32 [160, 2048, 128], P(None, ('comp', 'tile'))
- ocean_flux: float32 [2, 2048, 128], P(None, ('comp', 'tile'))
Inputs may be any that keep to these rules, and one draw needn't show every extreme that they name: `remap_owner`: in each row 4 different owners; among the 64 rows of one device no owner appears more than 4 times, a bound that some block reaches.
All inputs are finite; a program needn't handle non-finite values. No bound on the sum of `atm_sea` or of `ocean_sea` on one device may be relied on, other than what follows from the above.
Results may differ from a plain program's by a relative error of at most 0.0056.
Values may be sent and summed in bfloat16 or wider, within the bound.
No kernel may reach another device: no remote copies, remote signals or barrier semaphores. Data moves between devices by JAX's collectives and lax.ppermute only.
A program may use at most 128 MiB of HBM per device.

v0:
```python
import functools

import jax
import jax.numpy as jnp
from jax import lax
from jax.experimental import pallas as pl
from jax.experimental.pallas import tpu as pltpu
from jax.sharding import PartitionSpec as P

ATM_DIFFUSION = 0.1
OCEAN_DIFFUSION = 0.15
EXCHANGE_RATE = 0.3
FLUX_GAIN = 0.5

F32 = jnp.float32
BF16 = jnp.bfloat16
VM = pltpu.VMEM
BOTH = ("comp", "tile")
HEAD = 24


def call(kernel, outs, *args, scratch=(), spaces=None, flops=0, touched=0, limit=48):
    spaces = spaces or [VM] * len(args)
    return pl.pallas_call(
        kernel,
        out_shape=outs,
        in_specs=[pl.BlockSpec(memory_space=s) for s in spaces],
        out_specs=jax.tree.map(lambda _: pl.BlockSpec(memory_space=VM), outs),
        scratch_shapes=list(scratch),
        compiler_params=pltpu.CompilerParams(vmem_limit_bytes=limit << 20),
        cost_estimate=pl.CostEstimate(flops=flops, bytes_accessed=touched, transcendentals=0),
    )(*args)


def shape(dims, dtype):
    return jax.ShapeDtypeStruct(dims, dtype)


def iota(dims, axis):
    return lax.broadcasted_iota(jnp.int32, dims, axis)


def columns(ref):
    return jnp.concatenate([ref[:, k : k + 1] for k in range(ref.shape[1])], axis=0)


def plan_kernel(owner_ref, block_ref, surface_ref, head_ref, place_ref, slot_rows):
    devices = head_ref.shape[0]
    owner, block = columns(owner_ref), columns(block_ref)
    pairs = owner.shape[0]
    hits = (owner == iota((pairs, devices), 1)).astype(F32)
    earlier = (iota((pairs, pairs), 1) < iota((pairs, pairs), 0)).astype(F32)
    before = jnp.dot(earlier.astype(BF16), hits.astype(BF16), preferred_element_type=F32)
    slot = jnp.sum(before * hits, axis=1, keepdims=True)
    marked = jnp.where(
        slot == iota((pairs, 128), 1).astype(F32), (block + 1).astype(F32), 0.0
    )
    wanted = jnp.dot(
        jnp.transpose(hits).astype(BF16), marked.astype(BF16), preferred_element_type=F32
    )
    place = owner.astype(F32) * 8.0 + slot
    spread = jnp.transpose(jnp.broadcast_to(place, (pairs, 128)))
    place_ref[...] = spread[:8].astype(jnp.int32)
    slot_rows[...] = jnp.zeros_like(slot_rows)
    slot_rows[pl.ds(0, devices, stride=8), :] = wanted
    surface = surface_ref[...].astype(BF16)
    head_ref[:, 0:16, :] = jnp.broadcast_to(surface[None], (devices, 16, 128))
    head_ref[:, 16:24, :] = slot_rows[...].reshape(devices, 8, 128).astype(BF16)


def turn_kernel(state_ref, turned_ref, first_ref, last_ref):
    rows, cells = state_ref.shape[0], state_ref.shape[1]
    step = 16

    @pl.loop(0, rows // step)
    def _(i):
        at = pl.multiple_of(i * step, step)
        part = state_ref[pl.ds(at, step)].astype(F32)
        turned_ref[:, pl.ds(at, step), :] = jnp.swapaxes(part, 0, 1).astype(BF16)

    first_ref[...] = turned_ref[0]
    last_ref[...] = turned_ref[cells - 1]


def lateral_matrix(size):
    row, col = iota((size, size), 0), iota((size, size), 1)
    near = jnp.where(jnp.abs(row - col) == 1, 1.0, 0.0)
    edge = jnp.where((row == 0) | (row == size - 1), -3.0, -4.0)
    return (near + jnp.where(row == col, edge, 0.0)).astype(BF16)


def without_forced(vertical):
    height = vertical.shape[0]
    col = iota(vertical.shape, 1)
    keep = (col != height // 2 - 1) & (col != height - 1)
    return jnp.where(keep, vertical.astype(F32), 0.0).astype(BF16)


def stencil(west, center, east, lateral, courant):
    w, c, e = west.astype(F32), center.astype(F32), east.astype(F32)
    side = jnp.dot(center, lateral, preferred_element_type=F32)
    return c + courant * (w - c) + ATM_DIFFUSION * (w + e + side)


def first_step_kernel(
    turned_ref, left_ref, right_ref, courant_ref, vertical_ref,
    mixed_ref, first_ref, last_ref, upper_ref, lower_ref, upper_mix_ref, lower_mix_ref,
):
    cells, height = turned_ref.shape[0], turned_ref.shape[1]
    top, low = height // 2 - 1, height - 1
    lateral = lateral_matrix(turned_ref.shape[2])
    vertical = without_forced(vertical_ref[...])
    courant = courant_ref[...]

    def body(x, west, center, east):
        updated = stencil(west, center, east, lateral, courant)
        upper_ref[pl.ds(x, 1), :] = updated[top : top + 1]
        lower_ref[pl.ds(x, 1), :] = updated[low : low + 1]
        mixed = jnp.dot(vertical, updated.astype(BF16), preferred_element_type=F32)
        upper_mix_ref[pl.ds(x, 1), :] = mixed[top : top + 1]
        lower_mix_ref[pl.ds(x, 1), :] = mixed[low : low + 1]
        mixed_ref[x] = mixed.astype(BF16)

    body(0, left_ref[...], turned_ref[0], turned_ref[1])

    @pl.loop(1, cells - 1)
    def _(x):
        body(x, turned_ref[x - 1], turned_ref[x], turned_ref[x + 1])

    body(cells - 1, turned_ref[cells - 2], turned_ref[cells - 1], right_ref[...])
    first_ref[...] = mixed_ref[0]
    last_ref[...] = mixed_ref[cells - 1]


def ocean_kernel(ocean_ref, left_ref, right_ref, sea_ref, flux_ref, vertical_ref, out_ref):
    cells, width = sea_ref.shape
    height = ocean_ref.shape[0] // cells
    vertical = vertical_ref[...]
    high = vertical.astype(BF16)
    low = (vertical - high.astype(F32)).astype(BF16)
    lane = iota((height, width), 1)
    row = iota((height, width), 0)

    def column(x):
        if x < 0:
            return left_ref[...]
        if x >= cells:
            return right_ref[...]
        return ocean_ref[pl.ds(x, height, stride=cells), :]

    for x in range(cells):
        west, center, east = column(x - 1), column(x), column(x + 1)
        north = jnp.where(lane == width - 1, center, pltpu.roll(center, width - 1, 1))
        south = jnp.where(lane == 0, center, pltpu.roll(center, 1, 1))
        wet = sea_ref[x : x + 1, :].astype(F32)
        near = east + west + (north + south) - 4.0 * center
        heat = FLUX_GAIN * wet * flux_ref[0, x : x + 1, :]
        fresh = FLUX_GAIN * wet * flux_ref[1, x : x + 1, :]
        added = jnp.where(row == 0, heat, jnp.where(row == height // 2, fresh, 0.0))
        updated = (center + OCEAN_DIFFUSION * near) * wet + added
        upper = updated.astype(BF16)
        rest = (updated - upper.astype(F32)).astype(BF16)
        mixed = jnp.dot(high, upper, preferred_element_type=F32)
        mixed += jnp.dot(high, rest, preferred_element_type=F32)
        mixed += jnp.dot(low, upper, preferred_element_type=F32)
        out_ref[pl.ds(x, height, stride=cells), :] = mixed


def edges_kernel(ocean_ref, first_ref, last_ref):
    height = first_ref.shape[0]
    cells = ocean_ref.shape[0] // height
    first_ref[...] = ocean_ref[pl.ds(0, height, stride=cells), :]
    last_ref[...] = ocean_ref[pl.ds(cells - 1, height, stride=cells), :]


PARTS = 8


def weight_copies(weight_ref, held, sems):
    step = weight_ref.shape[0] // PARTS
    return [
        pltpu.make_async_copy(
            weight_ref.at[pl.ds(i * step, step)], held.at[pl.ds(i * step, step)], sems.at[i]
        )
        for i in range(PARTS)
    ]


def pull_kernel(
    head_ref, owner_ref, block_ref, weight_ref, sea_ref, upper_ref, lower_ref,
    temp_ref, upper_forced_ref, lower_forced_ref, first_ref, last_ref, slots_ref,
    held, sems, slot_rows, by_block,
):
    copies = weight_copies(weight_ref, held, sems)
    for c in copies:
        c.start()
    devices = head_ref.shape[0]
    surface = head_ref[:, 0:16, :].reshape(devices * 16, 128)
    slot_rows[...] = head_ref[:, 16:24, :].astype(F32).reshape(devices * 8, 128)
    slots_ref[...] = jnp.transpose(slot_rows[pl.ds(0, devices, stride=8), :])[:8]
    blocks, sources = owner_ref.shape
    goal = columns(owner_ref) * 16 + columns(block_ref)
    pick = (goal == iota((blocks * sources, devices * 16), 1)).astype(F32).astype(BF16)
    fetched = jnp.dot(pick, surface, preferred_element_type=F32)
    wanted = jnp.concatenate(
        [jnp.transpose(fetched[k * blocks : (k + 1) * blocks]) for k in range(sources)], axis=0
    ).astype(BF16)
    lane = iota((128, blocks), 1)
    step = blocks // PARTS

    def add(j, total):
        rows = jnp.concatenate([held[j, k] for k in range(sources)], axis=1)
        product = jnp.dot(rows, wanted, preferred_element_type=F32)
        return jnp.where(lane == j, product, total)

    total = jnp.zeros((128, blocks), F32)
    for i, c in enumerate(copies):
        c.wait()
        total = lax.fori_loop(i * step, (i + 1) * step, add, total, unroll=True)
    by_block[...] = jnp.transpose(total)
    half = blocks // 2
    temp = jnp.concatenate(
        [by_block[pl.ds(h, half, stride=2), :] for h in range(2)], axis=1
    )
    temp_ref[...] = temp
    exchange = EXCHANGE_RATE * sea_ref[...].astype(F32)
    upper, lower = upper_ref[...], lower_ref[...]
    upper = (upper + exchange * (temp - upper)).astype(BF16).astype(F32)
    lower = (lower + exchange * (0.5 * temp - lower)).astype(BF16).astype(F32)
    upper_forced_ref[...] = upper
    lower_forced_ref[...] = lower
    two = iota((8, upper.shape[1]), 0) == 0
    first_ref[...] = jnp.where(two, upper[0:1], lower[0:1])
    last_ref[...] = jnp.where(two, upper[half - 1 : half], lower[half - 1 : half])


def push_kernel(
    place_ref, weight_ref, sea_ref, temp_ref, upper_ref, lower_ref,
    upper_forced_ref, lower_forced_ref, upper_mix_ref, lower_mix_ref,
    left_forced_ref, right_forced_ref, left_mix_ref, right_mix_ref,
    courant_ref, vertical_ref, out_ref,
    held, sems, flux_rows, shares,
):
    copies = weight_copies(weight_ref, held, sems)
    for c in copies:
        c.start()
    height = vertical_ref.shape[0]
    top, low = height // 2 - 1, height - 1
    cells, width = sea_ref.shape
    sub, lane = iota((cells, width), 0), iota((cells, width), 1)

    def row_of(r, mix, upper, lower):
        a = vertical_ref[pl.ds(r - 7, 8), :].astype(F32)[7:8]
        kept = mix.astype(BF16).astype(F32)
        return (kept + a[:, top : top + 1] * upper + a[:, low : low + 1] * lower).astype(BF16).astype(F32)

    def updated(r, mix_ref):
        center = row_of(r, mix_ref[...], upper_forced_ref[...], lower_forced_ref[...])
        sides = [
            row_of(r, m[pl.ds(r - 7, 8), :].astype(F32)[7:8], f[0:1], f[1:2])
            for m, f in ((left_mix_ref, left_forced_ref), (right_mix_ref, right_forced_ref))
        ]
        west = jnp.where(sub == 0, sides[0], pltpu.roll(center, 1, 0))
        east = jnp.where(sub == cells - 1, sides[1], pltpu.roll(center, cells - 1, 0))
        north = jnp.where(lane == width - 1, center, pltpu.roll(center, width - 1, 1))
        south = jnp.where(lane == 0, center, pltpu.roll(center, 1, 1))
        near = east + west + (north + south) - 4.0 * center
        courant = courant_ref[pl.ds(r - 7, 8), :][7:8]
        return center - courant * (center - west) + ATM_DIFFUSION * near

    exchange = EXCHANGE_RATE * sea_ref[...].astype(F32)
    temp = temp_ref[...]
    heat = 0.5 * (exchange * (temp - upper_ref[...])) + 0.5 * (
        exchange * (temp - updated(top, upper_mix_ref))
    )
    moist = 0.5 * (exchange * (0.5 * temp - lower_ref[...])) + 0.5 * (
        exchange * (0.5 * temp - updated(low, lower_mix_ref))
    )
    flux_rows[...] = jnp.zeros_like(flux_rows)
    for v, flux in enumerate((heat, moist)):
        for h in range(2):
            flux_rows[pl.ds(h * 8 + v, cells, stride=16), :] = flux[:, h * 128 : (h + 1) * 128]
    blocks, sources = held.shape[0], held.shape[1]
    step = blocks // PARTS

    for i, c in enumerate(copies):
        c.wait()

        @pl.loop(i * step, (i + 1) * step, unroll=True)
        def _(j):
            rows = flux_rows[pl.ds(pl.multiple_of(j * 8, 8), 8), :].astype(BF16)
            for k in range(sources):
                got = jnp.dot(rows, held[j, k], preferred_element_type=F32)
                shares[pl.ds(pl.multiple_of((k * blocks + j) * 8, 8), 8), :] = got

    pairs = blocks * sources
    place = place_ref[0:1, :]
    rows = iota((out_ref.shape[0], pairs), 0)
    total = jnp.zeros(out_ref.shape, F32)
    for v in range(2):
        pick = (rows == place + 4 * v).astype(F32).astype(BF16)
        share = shares[pl.ds(v, pairs, stride=8), :].astype(BF16)
        total += jnp.dot(pick, share, preferred_element_type=F32)
    out_ref[...] = total.astype(BF16)


def second_step_kernel(
    mixed_ref, left_ref, right_ref, courant_ref, vertical_ref, sea_ref, temp_ref,
    upper_forced_ref, lower_forced_ref, left_forced_ref, right_forced_ref,
    out_ref, state, result,
):
    cells, height = mixed_ref.shape[0], mixed_ref.shape[1]
    top, low = height // 2 - 1, height - 1
    lateral = lateral_matrix(mixed_ref.shape[2])
    vertical = vertical_ref[...]
    upper_column = vertical[:, top : top + 1].astype(F32)
    lower_column = vertical[:, low : low + 1].astype(F32)
    courant = courant_ref[...]

    def complete(mixed, upper, lower):
        return (mixed.astype(F32) + upper_column * upper + lower_column * lower).astype(BF16)

    state[0] = complete(left_ref[...], left_forced_ref[0:1], left_forced_ref[1:2])
    state[cells + 1] = complete(right_ref[...], right_forced_ref[0:1], right_forced_ref[1:2])

    @pl.loop(0, cells)
    def _(x):
        state[x + 1] = complete(
            mixed_ref[x], upper_forced_ref[pl.ds(x, 1), :], lower_forced_ref[pl.ds(x, 1), :]
        )

    last = iota((8, mixed_ref.shape[2]), 0) == 7

    @pl.loop(0, cells)
    def _(x):
        updated = stencil(state[x], state[x + 1], state[x + 2], lateral, courant)
        exchange = EXCHANGE_RATE * sea_ref[pl.ds(x, 1), :].astype(F32)
        temp = temp_ref[pl.ds(x, 1), :]
        upper = updated[top - 7 : top + 1]
        lower = updated[low - 7 : low + 1]
        upper = jnp.where(last, upper + exchange * (temp - upper), upper)
        lower = jnp.where(last, lower + exchange * (0.5 * temp - lower), lower)
        forced = jnp.concatenate(
            [updated[: top - 7], upper, updated[top + 1 : low - 7], lower], axis=0
        ).astype(BF16)
        result[x] = jnp.dot(vertical, forced, preferred_element_type=F32).astype(BF16)

    step = 16

    @pl.loop(0, height // step)
    def _(i):
        at = pl.multiple_of(i * step, step)
        part = result[:, pl.ds(at, step), :].astype(F32)
        out_ref[pl.ds(at, step)] = jnp.swapaxes(part, 0, 1).astype(BF16)


def land_kernel(incoming_ref, slots_ref, sea_ref, out_ref, wide):
    devices = slots_ref.shape[1]
    cells = sea_ref.shape[0]
    wide[...] = incoming_ref[...].astype(F32)
    wet = sea_ref[...].astype(F32)
    here = (iota((cells, devices), 0) + 1).astype(F32)
    picks = [(slots_ref[s : s + 1, :] == here).astype(F32).astype(BF16) for s in range(4)]
    for v in range(2):
        total = jnp.zeros((cells, 128), F32)
        for s in range(4):
            part = wide[pl.ds(v * 4 + s, devices, stride=8), :].astype(BF16)
            total += jnp.dot(picks[s], part, preferred_element_type=F32)
        out_ref[v] = total * wet


def swap(first, last):
    peers = lax.axis_size(BOTH)
    up = [(i, (i + 1) % peers) for i in range(peers)]
    down = [(j, i) for i, j in up]
    return lax.ppermute(last, BOTH, up), lax.ppermute(first, BOTH, down)


def per_device(
    atm_state, atm_sea, zonal_courant, atm_vertical, ocean_state, ocean_sea,
    flux_in, ocean_vertical, remap_owner, remap_block, remap_weight,
):
    devices = lax.axis_size(BOTH)
    height, cells, width = atm_state.shape
    blocks, sources = remap_owner.shape
    pairs = blocks * sources
    courant = zonal_courant.reshape(height, 1)
    layers, ocean_cells, ocean_width = ocean_state.shape
    ocean_rows = ocean_state.reshape(layers * ocean_cells, ocean_width)

    head, place = call(
        plan_kernel,
        (shape((devices, HEAD, 128), BF16), shape((8, pairs), jnp.int32)),
        remap_owner, remap_block, ocean_state[0],
        scratch=[pltpu.VMEM((devices * 8, 128), F32)],
        touched=1 << 20,
    )
    gathered = lax.all_to_all(head, BOTH, split_axis=0, concat_axis=0, tiled=True)

    column = shape((height, width), BF16)
    turned, first, last = call(
        turn_kernel,
        (shape((cells, height, width), BF16), column, column),
        atm_state,
        touched=12 << 20,
    )
    left, right = swap(first, last)
    ocean_first, ocean_last = call(
        edges_kernel,
        (shape((layers, ocean_width), F32),) * 2,
        ocean_rows,
        touched=2 << 20,
    )
    ocean_left, ocean_right = swap(ocean_first, ocean_last)
    row = shape((cells, width), F32)
    mixed, mixed_first, mixed_last, upper, lower, upper_mix, lower_mix = call(
        first_step_kernel,
        (shape((cells, height, width), BF16), column, column, row, row, row, row),
        turned, left, right, courant, atm_vertical,
        touched=16 << 20,
    )
    mixed_left, mixed_right = swap(mixed_first, mixed_last)
    new_ocean = call(
        ocean_kernel,
        shape(ocean_rows.shape, F32),
        ocean_rows, ocean_left, ocean_right, ocean_sea, flux_in, ocean_vertical,
        touched=8 << 20,
    )

    small = shape((8, width), F32)
    held = [pltpu.VMEM(remap_weight.shape, BF16), pltpu.SemaphoreType.DMA((PARTS,))]
    temp, upper_forced, lower_forced, forced_first, forced_last, slots = call(
        pull_kernel,
        (row, row, row, small, small, shape((8, devices), F32)),
        gathered, remap_owner, remap_block, remap_weight, atm_sea, upper, lower,
        spaces=[VM, VM, VM, pl.ANY, VM, VM, VM],
        scratch=[*held, pltpu.VMEM((devices * 8, 128), F32), pltpu.VMEM((blocks, 128), F32)],
        touched=12 << 20,
    )
    forced_left, forced_right = swap(forced_first, forced_last)
    outgoing = call(
        push_kernel,
        shape((devices * 8, 128), BF16),
        place, remap_weight, atm_sea, temp, upper, lower,
        upper_forced, lower_forced, upper_mix, lower_mix,
        forced_left, forced_right, mixed_left, mixed_right, courant, atm_vertical,
        spaces=[VM, pl.ANY] + [VM] * 14,
        scratch=[*held, pltpu.VMEM((blocks * 8, 128), F32), pltpu.VMEM((pairs * 8, 128), F32)],
        touched=12 << 20,
    )
    incoming = lax.all_to_all(
        outgoing.reshape(devices, 8, 128), BOTH, split_axis=0, concat_axis=0, tiled=True
    )
    state = call(
        second_step_kernel,
        shape(atm_state.shape, BF16),
        mixed, mixed_left, mixed_right, courant, atm_vertical, atm_sea, temp,
        upper_forced, lower_forced, forced_left, forced_right,
        scratch=[
            pltpu.VMEM((cells + 2, height, width), BF16),
            pltpu.VMEM((cells, height, width), BF16),
        ],
        touched=24 << 20,
    )
    ocean_flux = call(
        land_kernel,
        shape((2, ocean_cells, ocean_width), F32),
        incoming.reshape(devices * 8, 128), slots, ocean_sea,
        scratch=[pltpu.VMEM((devices * 8, 128), F32)],
        touched=1 << 20,
    )
    return state, new_ocean.reshape(ocean_state.shape), ocean_flux


def solution(mesh):
    return jax.shard_map(
        per_device,
        mesh=mesh,
        in_specs=(
            P(None, BOTH, None), P(BOTH, None), P(), P(), P(None, BOTH, None), P(BOTH, None),
            P(None, BOTH, None), P(), P(BOTH, None), P(BOTH, None), P(BOTH, None, None, None),
        ),
        out_specs=(P(None, BOTH, None), P(None, BOTH, None), P(None, BOTH, None)),
        check_vma=False,
    )
```

profile of v0, /device:TPU:0, one launch (start us, length us, event | category | flops | bytes accessed | tf_op | source)
XLA Modules:
  0.0 120.3 jit_solution(8477158221658924961)
XLA Ops:
  0.7 0.8 copy.19.owner_ref
  1.5 0.8 copy.20.block_ref
  2.2 0.7 slice_bitcast_fusion.surface_ref
  2.9 1.5 %shard_map.132 = (bf16[128,24,128]{2,1,0:T(8,128)(2,1)}, s32[8,256]{1,0:T(8,128)S(1)}) custom-call(s32[64,4]{1,0:T(8,128)S(1)} %copy.19.owner_ref, s32[64,4]{1,0:T(8,128)S(1)} %copy.20.block_ref, f32[16,128]{1,0:T(8,128)S(1)} %slice_bitcast_fusion.surface_ref), custom_call_target="tpu_custom_call" | custom-call | bytes 1048576 | tf_op jit(solution)/shard_map/pallas_call | solution.py:24
  4.4 11.1 %all-to-all-start = ((bf16[128,24,128]{2,1,0:T(8,128)(2,1)}), bf16[128,24,128]{2,1,0:T(8,128)(2,1)S(1)}, u32[]{:S(2)}, u32[]{:S(2)}) async-start(bf16[128,24,128]{2,1,0:T(8,128)(2,1)} %get-tuple-element.29), calls=%async_computation | async-start | bytes 1572864 | tf_op jit(solution)/shard_map/all_to_all | solution.py:398
  15.6 0.0 copy-start.5
  15.6 4.2 %shard_map.130 = (bf16[32,256,256]{2,1,0:T(8,128)(2,1)S(1)}, bf16[256,256]{1,0:T(8,128)(2,1)S(1)}, bf16[256,256]{1,0:T(8,128)(2,1)S(1)}) custom-call(bf16[256,32,256]{2,1,0:T(8,128)(2,1)} %state_ref.1), custom_call_target="tpu_custom_call" | custom-call | bytes 12582912 | tf_op jit(solution)/shard_map/pallas_call | solution.py:24
  19.8 0.0 copy-start.1
  19.8 2.0 %copy-done.1 = bf16[32,256,256]{2,1,0:T(8,128)(2,1)} copy-done((bf16[32,256,256]{2,1,0:T(8,128)(2,1)}, bf16[32,256,256]{2,1,0:T(8,128)(2,1)S(1)}, u32[]{:S(2)}) %copy-start.1) | copy-done | bytes 4194328
  21.8 7.2 %collective-permute-start.1 = (bf16[256,256]{1,0:T(8,128)(2,1)S(1)}, bf16[256,256]{1,0:T(8,128)(2,1)S(1)}, u32[]{:S(2)}, u32[]{:S(2)}) collective-permute-start(bf16[256,256]{1,0:T(8,128)(2,1)S(1)} %get-tuple-element.25), channel_id=1, source_target_pairs={{1,0},{2,1},{3,2},{4,3},{5,4},{6,5},{7,6},{8,7},{9,8},{10,9},{11,1... | collective-permute-start | bytes 393224 | tf_op jit(solution)/shard_map/ppermute | solution.py:376
  29.0 0.1 copy.18.courant_ref
  29.1 3.9 %collective-permute-done.left_ref = bf16[256,256]{1,0:T(8,128)(2,1)S(1)} collective-permute-done((bf16[256,256]{1,0:T(8,128)(2,1)S(1)}, bf16[256,256]{1,0:T(8,128)(2,1)S(1)}, u32[]{:S(2)}, u32[]{:S(2)}) %collective-permute-start) | collective-permute-done | bytes 131104 | tf_op jit(solution)/shard_map/ppermute | solution.py:376
  33.0 15.1 %shard_map.131 = (bf16[32,256,256]{2,1,0:T(8,128)(2,1)S(1)}, bf16[256,256]{1,0:T(8,128)(2,1)S(1)}, bf16[256,256]{1,0:T(8,128)(2,1)S(1)}, f32[32,256]{1,0:T(8,128...) custom-call(bf16[32,256,256]{2,1,0:T(8,128)(2,1)} %copy-done.1, ...), custom_call_target="tpu_custom_call" | custom-call | bytes 16777216 | tf_op jit(solution)/shard_map/pallas_call | solution.py:24
  48.2 0.0 copy-start.2
  48.2 2.0 %copy-done.2 = bf16[32,256,256]{2,1,0:T(8,128)(2,1)} copy-done((bf16[32,256,256]{2,1,0:T(8,128)(2,1)}, bf16[32,256,256]{2,1,0:T(8,128)(2,1)S(1)}, u32[]{:S(2)}) %copy-start.2) | copy-done | bytes 4194328
  50.2 7.2 %collective-permute-start.3 = (bf16[256,256]{1,0:T(8,128)(2,1)S(1)}, bf16[256,256]{1,0:T(8,128)(2,1)S(1)}, u32[]{:S(2)}, u32[]{:S(2)}) collective-permute-start(bf16[256,256]{1,0:T(8,128)(2,1)S(1)} %get-tuple-element.28), channel_id=1, source_target_pairs={{1,0},{2,1},{3,2},{4,3},{5,4},{6,5},{7,6},{8,7},{9,8},{10,9},{11,1... | collective-permute-start | bytes 393224 | tf_op jit(solution)/shard_map/ppermute | solution.py:376
  57.4 5.4 %shard_map.133 = (f32[32,256]{1,0:T(8,128)S(1)}, f32[32,256]{1,0:T(8,128)S(1)}, f32[32,256]{1,0:T(8,128)S(1)}, f32[8,256]{1,0:T(8,128)S(1)}, f32[8,256]{1,0:T(8,128)S(1)}, /*index=5*/f32[8,128]{1,0:T(8,128)S(1)}) custom-call(bf16[128,24,128]{2,1,0:T(8,128)(2,1)S(1)} %all-to-all-done.head_ref, s32[64,4]{1,0:T(8,128)S(1)} %copy.19.owner_ref, ...), custom_call_target="tpu_custom_call" | custom-call | bytes 12582912 | tf_op jit(solution)/shard_map/pallas_call | solution.py:24
  62.8 0.1 collective-permute-start.4
  62.8 7.2 %collective-permute-start.5 = (f32[8,256]{1,0:T(8,128)S(1)}, f32[8,256]{1,0:T(8,128)S(1)}, u32[]{:S(2)}, u32[]{:S(2)}) collective-permute-start(f32[8,256]{1,0:T(8,128)S(1)} %get-tuple-element.36), channel_id=1, source_target_pairs={{1,0},{2,1},{3,2},{4,3},{5,4},{6,5},{7,6},{8,7},{9,8},{10,9},{11,1... | collective-permute-start | bytes 24584 | tf_op jit(solution)/shard_map/ppermute | solution.py:376
  70.0 0.0 collective-permute-done.2.left_ref.left_mix_ref
  70.0 1.3 %collective-permute-done.4.left_forced_ref = f32[8,256]{1,0:T(8,128)S(1)} collective-permute-done((f32[8,256]{1,0:T(8,128)S(1)}, f32[8,256]{1,0:T(8,128)S(1)}, u32[]{:S(2)}, u32[]{:S(2)}) %collective-permute-start.4) | collective-permute-done | bytes 8224 | tf_op jit(solution)/shard_map/ppermute | solution.py:376
  71.3 0.0 collective-permute-done.5.right_forced_ref
  71.4 5.7 %shard_map.137 = bf16[1024,128]{1,0:T(8,128)(2,1)} custom-call(s32[8,256]{1,0:T(8,128)S(1)} %get-tuple-element.39.place_ref, bf16[64,4,128,128]{3,2,1,0:T(8,128)(2,1)} %weight_ref.3, s32[32,256]{1,0:T(8,128)S(1)} %copy-done.5, f32[32,256]{1,0:T(8,128)S(1)} %get-tuple-element.32.temp_ref, f32[32,256]{1,0:T(8,128)S(1)} %get-tuple-element.30.upper_ref, ...), custom_call_target="tpu_custom_call" | custom-call | bytes 12582912 | tf_op jit(solution)/shard_map/pallas_call | solution.py:24
  77.1 9.1 %all-to-all-start.1 = ((bf16[128,8,128]{2,1,0:T(8,128)(2,1)}), bf16[128,8,128]{2,1,0:T(8,128)(2,1)S(1)}, u32[]{:S(2)}, u32[]{:S(2)}) async-start(bf16[128,8,128]{2,1,0:T(8,128)(2,1)} %bitcast.4), calls=%async_computation.1 | async-start | bytes 524288 | tf_op jit(solution)/shard_map/all_to_all | solution.py:451
  86.2 0.0 copy-start.3
  86.2 0.1 shard_map.135
  86.3 0.1 collective-permute-start.6
  86.4 7.3 %collective-permute-start.7 = (f32[160,128]{1,0:T(8,128)S(1)}, f32[160,128]{1,0:T(8,128)S(1)}, u32[]{:S(2)}, u32[]{:S(2)}) collective-permute-start(f32[160,128]{1,0:T(8,128)S(1)} %get-tuple-element.38), channel_id=1, source_target_pairs={{1,0},{2,1},{3,2},{4,3},{5,4},{6,5},{7,6},{8,7},{9,8},{10,9},{11,1... | collective-permute-start | bytes 245768 | tf_op jit(solution)/shard_map/ppermute | solution.py:376
  93.7 3.8 %collective-permute-done.6.left_ref = f32[160,128]{1,0:T(8,128)S(1)} collective-permute-done((f32[160,128]{1,0:T(8,128)S(1)}, f32[160,128]{1,0:T(8,128)S(1)}, u32[]{:S(2)}, u32[]{:S(2)}) %collective-permute-start.6) | collective-permute-done | bytes 81952 | tf_op jit(solution)/shard_map/ppermute | solution.py:376
  97.5 3.1 %shard_map.136 = f32[2560,128]{1,0:T(8,128)} custom-call(f32[2560,128]{1,0:T(8,128)S(1)} %bitcast.8, f32[160,128]{1,0:T(8,128)S(1)} %collective-permute-done.6.left_ref, f32[160,128]{1,0:T(8,128)S(1)} %collective-permute-done.7.right_ref, s32[16,128]{1,0:T(8,128)S(1)} %copy-done.7, f32[2,16,128]{2,1,0:T(8,128)S(1)} %copy-done.8, f32[160,160]{1,0:T(8,128)S(1)} %copy-done.6), custom_call_target="tpu_custom_call" | custom-call | bytes 8388608 | tf_op jit(solution)/shard_map/pallas_call | solution.py:24
  100.6 18.9 %shard_map.134 = bf16[256,32,256]{2,1,0:T(8,128)(2,1)} custom-call(bf16[32,256,256]{2,1,0:T(8,128)(2,1)S(1)} %copy-done.3, bf16[256,256]{1,0:T(8,128)(2,1)S(1)} %collective-permute-done.2.left_ref.left_mix_ref, bf16[256,256]{1,0:T(8,128)(2,1)S(1)} %collective-permute-done.3.right_ref.right_mix_ref, f32[256,1]{1,0:T(8,128)S(1)} %copy.18.courant_ref, ...), custom_call_target="tpu_custom_call" | custom-call | bytes 25165824 | tf_op jit(solution)/shard_map/pallas_call | solution.py:24
  119.5 0.8 shard_map.138
  (21 shorter events, 0.0 us)
Async XLA Ops:
  0.6 28.3 %copy-start.9 = (f32[256]{0:T(256)S(1)}, f32[256]{0:T(256)}, u32[]{:S(2)}) copy-start(f32[256]{0:T(256)} %param.13) | copy-start | bytes 3076
  0.6 32.4 %copy-start.4 = (bf16[256,256]{1,0:T(8,128)(2,1)S(1)}, bf16[256,256]{1,0:T(8,128)(2,1)}, u32[]{:S(2)}) copy-start(bf16[256,256]{1,0:T(8,128)(2,1)} %vertical_ref.7) | copy-start | bytes 393220
  4.4 52.9 %all-to-all-start = ((bf16[128,24,128]{2,1,0:T(8,128)(2,1)}), bf16[128,24,128]{2,1,0:T(8,128)(2,1)S(1)}, u32[]{:S(2)}, u32[]{:S(2)}) async-start(bf16[128,24,128]{2,1,0:T(8,128)(2,1)} %get-tuple-element.29), calls=%async_computation | async-start | bytes 1572864 | tf_op jit(solution)/shard_map/all_to_all | solution.py:398
  15.6 41.8 %copy-start.5 = (s32[32,256]{1,0:T(8,128)S(1)}, s32[32,256]{1,0:T(8,128)}, u32[]{:S(2)}) copy-start(s32[32,256]{1,0:T(8,128)} %sea_ref.8) | copy-start | bytes 98308
  19.8 2.0 %copy-start.1 = (bf16[32,256,256]{2,1,0:T(8,128)(2,1)}, bf16[32,256,256]{2,1,0:T(8,128)(2,1)S(1)}, u32[]{:S(2)}) copy-start(bf16[32,256,256]{2,1,0:T(8,128)(2,1)S(1)} %get-tuple-element.23.turned_ref) | copy-start | bytes 12582916
  21.8 11.2 %collective-permute-start = (bf16[256,256]{1,0:T(8,128)(2,1)S(1)}, bf16[256,256]{1,0:T(8,128)(2,1)S(1)}, u32[]{:S(2)}, u32[]{:S(2)}) collective-permute-start(bf16[256,256]{1,0:T(8,128)(2,1)S(1)} %get-tuple-element.24), channel_id=1, source_target_pairs={{0,1},{1,2},{2,3},{3,4},{4,5},{5,6},{6,7},{7,8},{8,9},{9,10},{10,1... | collective-permute-start | bytes 393224 | tf_op jit(solution)/shard_map/ppermute | solution.py:376
  21.8 11.2 %collective-permute-start.1 = (bf16[256,256]{1,0:T(8,128)(2,1)S(1)}, bf16[256,256]{1,0:T(8,128)(2,1)S(1)}, u32[]{:S(2)}, u32[]{:S(2)}) collective-permute-start(bf16[256,256]{1,0:T(8,128)(2,1)S(1)} %get-tuple-element.25), channel_id=1, source_target_pairs={{1,0},{2,1},{3,2},{4,3},{5,4},{6,5},{7,6},{8,7},{9,8},{10,9},{11,1... | collective-permute-start | bytes 393224 | tf_op jit(solution)/shard_map/ppermute | solution.py:376
  48.2 2.0 %copy-start.2 = (bf16[32,256,256]{2,1,0:T(8,128)(2,1)}, bf16[32,256,256]{2,1,0:T(8,128)(2,1)S(1)}, u32[]{:S(2)}) copy-start(bf16[32,256,256]{2,1,0:T(8,128)(2,1)S(1)} %get-tuple-element.26.mixed_ref) | copy-start | bytes 12582916
  50.2 19.8 %collective-permute-start.2 = (bf16[256,256]{1,0:T(8,128)(2,1)S(1)}, bf16[256,256]{1,0:T(8,128)(2,1)S(1)}, u32[]{:S(2)}, u32[]{:S(2)}) collective-permute-start(bf16[256,256]{1,0:T(8,128)(2,1)S(1)} %get-tuple-element.27), channel_id=1, source_target_pairs={{0,1},{1,2},{2,3},{3,4},{4,5},{5,6},{6,7},{7,8},{8,9},{9,10},{10,1... | collective-permute-start | bytes 393224 | tf_op jit(solution)/shard_map/ppermute | solution.py:376
  50.2 19.8 %collective-permute-start.3 = (bf16[256,256]{1,0:T(8,128)(2,1)S(1)}, bf16[256,256]{1,0:T(8,128)(2,1)S(1)}, u32[]{:S(2)}, u32[]{:S(2)}) collective-permute-start(bf16[256,256]{1,0:T(8,128)(2,1)S(1)} %get-tuple-element.28), channel_id=1, source_target_pairs={{1,0},{2,1},{3,2},{4,3},{5,4},{6,5},{7,6},{8,7},{9,8},{10,9},{11,1... | collective-permute-start | bytes 393224 | tf_op jit(solution)/shard_map/ppermute | solution.py:376
  62.8 8.6 %collective-permute-start.4 = (f32[8,256]{1,0:T(8,128)S(1)}, f32[8,256]{1,0:T(8,128)S(1)}, u32[]{:S(2)}, u32[]{:S(2)}) collective-permute-start(f32[8,256]{1,0:T(8,128)S(1)} %get-tuple-element.35), channel_id=1, source_target_pairs={{0,1},{1,2},{2,3},{3,4},{4,5},{5,6},{6,7},{7,8},{8,9},{9,10},{10,1... | collective-permute-start | bytes 24584 | tf_op jit(solution)/shard_map/ppermute | solution.py:376
  62.8 8.5 %collective-permute-start.5 = (f32[8,256]{1,0:T(8,128)S(1)}, f32[8,256]{1,0:T(8,128)S(1)}, u32[]{:S(2)}, u32[]{:S(2)}) collective-permute-start(f32[8,256]{1,0:T(8,128)S(1)} %get-tuple-element.36), channel_id=1, source_target_pairs={{1,0},{2,1},{3,2},{4,3},{5,4},{6,5},{7,6},{8,7},{9,8},{10,9},{11,1... | collective-permute-start | bytes 24584 | tf_op jit(solution)/shard_map/ppermute | solution.py:376
  71.4 14.8 %copy-start = (f32[160,16,128]{2,1,0:T(8,128)S(1)}, f32[160,16,128]{2,1,0:T(8,128)}, u32[]{:S(2)}) copy-start(f32[160,16,128]{2,1,0:T(8,128)} %param.15) | copy-start | bytes 3932164
  71.4 26.2 %copy-start.6 = (f32[160,160]{1,0:T(8,128)S(1)}, f32[160,160]{1,0:T(8,128)}, u32[]{:S(2)}) copy-start(f32[160,160]{1,0:T(8,128)} %vertical_ref.6) | copy-start | bytes 307204
  71.4 26.2 %copy-start.7 = (s32[16,128]{1,0:T(8,128)S(1)}, s32[16,128]{1,0:T(8,128)}, u32[]{:S(2)}) copy-start(s32[16,128]{1,0:T(8,128)} %sea_ref.9) | copy-start | bytes 24580
  71.4 26.2 %copy-start.8 = (f32[2,16,128]{2,1,0:T(8,128)S(1)}, f32[2,16,128]{2,1,0:T(8,128)}, u32[]{:S(2)}) copy-start(f32[2,16,128]{2,1,0:T(8,128)} %flux_ref.1) | copy-start | bytes 49156
  77.1 42.3 %all-to-all-start.1 = ((bf16[128,8,128]{2,1,0:T(8,128)(2,1)}), bf16[128,8,128]{2,1,0:T(8,128)(2,1)S(1)}, u32[]{:S(2)}, u32[]{:S(2)}) async-start(bf16[128,8,128]{2,1,0:T(8,128)(2,1)} %bitcast.4), calls=%async_computation.1 | async-start | bytes 524288 | tf_op jit(solution)/shard_map/all_to_all | solution.py:451
  86.2 14.4 %copy-start.3 = (bf16[32,256,256]{2,1,0:T(8,128)(2,1)S(1)}, bf16[32,256,256]{2,1,0:T(8,128)(2,1)}, u32[]{:S(2)}) copy-start(bf16[32,256,256]{2,1,0:T(8,128)(2,1)} %copy-done.2) | copy-start | bytes 12582916
  86.3 11.2 %collective-permute-start.6 = (f32[160,128]{1,0:T(8,128)S(1)}, f32[160,128]{1,0:T(8,128)S(1)}, u32[]{:S(2)}, u32[]{:S(2)}) collective-permute-start(f32[160,128]{1,0:T(8,128)S(1)} %get-tuple-element.37), channel_id=1, source_target_pairs={{0,1},{1,2},{2,3},{3,4},{4,5},{5,6},{6,7},{7,8},{8,9},{9,10},{10,1... | collective-permute-start | bytes 245768 | tf_op jit(solution)/shard_map/ppermute | solution.py:376
  86.4 11.2 %collective-permute-start.7 = (f32[160,128]{1,0:T(8,128)S(1)}, f32[160,128]{1,0:T(8,128)S(1)}, u32[]{:S(2)}, u32[]{:S(2)}) collective-permute-start(f32[160,128]{1,0:T(8,128)S(1)} %get-tuple-element.38), channel_id=1, source_target_pairs={{1,0},{2,1},{3,2},{4,3},{5,4},{6,5},{7,6},{8,7},{9,8},{10,9},{11,1... | collective-permute-start | bytes 245768 | tf_op jit(solution)/shard_map/ppermute | solution.py:376
where the time goes:
time: 121 us; the launch traced here: 120 us
  Pallas kernels  54.7 us (45%)
  starting transfers between devices  49.2 us (41%)
  waiting for transfers between devices  9.15 us (8%)
  local copies, waits for them, and re-layouts  6.46 us (5%)
    pallas_call x9, Pallas kernels, call(): pl.pallas_call(kernel, out_shape=outs, in_specs=[pl.BlockSpec(memory_spac...  54.7 us
    ppermute x8, starting transfers between devices, swap(): return (lax.ppermute(last, BOTH, up), lax.ppermute(first, BOTH, down))  29 us
    all_to_all x1, starting transfers between devices, per_device(): lax.all_to_all(head, BOTH, split_axis=0, concat_axis=0, tiled=True)  11.1 us
    ppermute x8, waiting for transfers between devices, swap(): return (lax.ppermute(last, BOTH, up), lax.ppermute(first, BOTH, down))  9.14 us
    all_to_all x1, starting transfers between devices, per_device(): lax.all_to_all(outgoing.reshape(devices, 8, 128), BOTH, split_axis=0, con...  9.07 us
    unnamed x22, local copies, waits for them, and re-layouts  5.63 us
  transfers between devices with their start and end apart: 10, of which 3 were waited for; matrix products, arithmetic and copies ran while one was open for 0% of the time, Pallas kernels for 39%

commit v1 on v0

v1 whole, which is shorter than its diff:
```python
import functools

import jax
import jax.numpy as jnp
from jax import lax
from jax.experimental import pallas as pl
from jax.experimental.pallas import tpu as pltpu
from jax.sharding import PartitionSpec as P

ATM_DIFFUSION = 0.1
OCEAN_DIFFUSION = 0.15
EXCHANGE_RATE = 0.3
FLUX_GAIN = 0.5

F32 = jnp.float32
BF16 = jnp.bfloat16
VM = pltpu.VMEM
BOTH = ("comp", "tile")
HEAD = 24


def call(kernel, outs, *args, scratch=(), specs=None, out_specs=None, limit=50, touched=0, grid=()):
    specs, out_specs = specs or {}, out_specs or {}
    single = not isinstance(outs, tuple)
    placed = [
        out_specs.get(i, pl.BlockSpec(memory_space=VM)) for i in range(1 if single else len(outs))
    ]
    return pl.pallas_call(
        kernel,
        out_shape=outs,
        grid=grid,
        in_specs=[specs.get(i, pl.BlockSpec(memory_space=VM)) for i in range(len(args))],
        out_specs=placed[0] if single else tuple(placed),
        scratch_shapes=list(scratch),
        compiler_params=pltpu.CompilerParams(vmem_limit_bytes=limit << 20),
        cost_estimate=pl.CostEstimate(flops=0, bytes_accessed=touched, transcendentals=0),
    )(*args)


SCALAR = pl.BlockSpec(memory_space=pltpu.SMEM)
ANY = pl.BlockSpec(memory_space=pltpu.HBM)


def start_all(copies):
    for c in copies:
        c.start()
    return copies


def wait_all(copies):
    for c in copies:
        c.wait()


def shape(dims, dtype):
    return jax.ShapeDtypeStruct(dims, dtype)


def iota(dims, axis):
    return lax.broadcasted_iota(jnp.int32, dims, axis)


def columns(ref):
    count, rows = ref.shape
    wide = [jnp.broadcast_to(ref[k : k + 1, :], (128, rows)) for k in range(count)]
    return jnp.concatenate([jnp.transpose(w) for w in wide], axis=0)


def is_odd():
    return jnp.bitwise_and(lax.axis_index("tile"), 1).astype(jnp.int32).reshape(1)


def plan_kernel(
    owner_hbm, block_hbm, ocean_hbm, head_ref, place_ref, slot_rows, owner_ref, block_ref, surface_ref, sems
):
    copies = start_all([
        pltpu.make_async_copy(owner_hbm, owner_ref, sems.at[0]),
        pltpu.make_async_copy(block_hbm, block_ref, sems.at[1]),
        pltpu.make_async_copy(ocean_hbm.at[0], surface_ref, sems.at[2]),
    ])
    devices = head_ref.shape[0]
    slot_rows[...] = jnp.zeros_like(slot_rows)
    wait_all(copies)
    owner, block = columns(owner_ref), columns(block_ref)
    pairs = owner.shape[0]
    hits = (owner == iota((pairs, devices), 1)).astype(F32)
    earlier = (iota((pairs, pairs), 1) < iota((pairs, pairs), 0)).astype(F32)
    before = jnp.dot(earlier.astype(BF16), hits.astype(BF16), preferred_element_type=F32)
    slot = jnp.sum(before * hits, axis=1, keepdims=True)
    marked = jnp.where(
        slot == iota((pairs, 128), 1).astype(F32), (block + 1).astype(F32), 0.0
    )
    wanted = jnp.dot(
        jnp.transpose(hits).astype(BF16), marked.astype(BF16), preferred_element_type=F32
    )
    spread = jnp.transpose(owner.astype(F32) * 8.0 + slot)
    place_ref[...] = spread[:8].astype(jnp.int32)
    slot_rows[pl.ds(0, devices, stride=8), :] = wanted
    surface = surface_ref[...].astype(BF16)
    head_ref[:, 0:16, :] = jnp.broadcast_to(surface[None], (devices, 16, 128))
    head_ref[:, 16:24, :] = slot_rows[...].reshape(devices, 8, 128).astype(BF16)


def turn_kernel(odd_ref, state_ref, ocean_hbm, turned_ref, send_ref, ocean_send_ref, sems):
    i, odd = pl.program_id(0), odd_ref[0]
    rows, cells = state_ref.shape[0], state_ref.shape[1]
    copies = [
        pltpu.make_async_copy(ocean_hbm.at[:, x], ocean_send_ref.at[to], sems.at[n])
        for n, (x, to) in enumerate(((0, 1 - odd), (ocean_hbm.shape[1] - 1, odd)))
    ]
    pl.when(i == 0)(lambda: (start_all(copies), None)[1])
    step = 32
    for n in range(rows // step):
        turned_ref[:, n * step : (n + 1) * step, :] = jnp.swapaxes(
            state_ref[n * step : (n + 1) * step], 0, 1
        )
    at = pl.ds(pl.multiple_of(i * rows, rows), rows)
    send_ref[1 - odd, :, at, :] = turned_ref[0:2]
    send_ref[odd, :, at, :] = turned_ref[cells - 2 : cells]
    pl.when(i == pl.num_programs(0) - 1)(lambda: wait_all(copies))


def sides(odd_ref, within, across):
    odd = odd_ref[0] == 1
    return jnp.where(odd, within, across), jnp.where(odd, across, within)


def lateral_matrix(size):
    row, col = iota((size, size), 0), iota((size, size), 1)
    near = jnp.where(jnp.abs(row - col) == 1, 1.0, 0.0)
    edge = jnp.where((row == 0) | (row == size - 1), -3.0, -4.0)
    return (near + jnp.where(row == col, edge, 0.0)).astype(BF16)


def without_forced(vertical):
    height = vertical.shape[0]
    col = iota(vertical.shape, 1)
    keep = (col != height // 2 - 1) & (col != height - 1)
    return jnp.where(keep, vertical.astype(F32), 0.0).astype(BF16)


def stencil(west, center, east, lateral, courant):
    w, c, e = west.astype(F32), center.astype(F32), east.astype(F32)
    side = jnp.dot(center, lateral, preferred_element_type=F32)
    return c + courant * (w - c) + ATM_DIFFUSION * (w + e + side)


GROUP = 8


def groups(hbm, held, sems, out=False):
    copies = []
    for g in range(held.shape[0] // GROUP):
        at = pl.ds(g * GROUP, GROUP)
        ends = (held.at[at], hbm.at[at]) if out else (hbm.at[at], held.at[at])
        copies.append(pltpu.make_async_copy(*ends, sems.at[g]))
    return copies


def first_step_kernel(
    turned_hbm, courant_ref, vertical_ref, mixed_hbm, upper_ref, lower_ref, upper_mix_ref, lower_mix_ref,
    turned, mixed_out, in_sems, out_sems,
):
    coming = start_all(groups(turned_hbm, turned, in_sems))
    going = groups(mixed_hbm, mixed_out, out_sems, out=True)
    cells, height = turned.shape[0], turned.shape[1]
    top, low = height // 2 - 1, height - 1
    lateral = lateral_matrix(turned.shape[2])
    vertical = without_forced(vertical_ref[...])
    courant = courant_ref[...]

    def body(x):
        updated = stencil(turned[x - 1], turned[x], turned[x + 1], lateral, courant)
        upper_ref[x : x + 1, :] = updated[top : top + 1]
        lower_ref[x : x + 1, :] = updated[low : low + 1]
        mixed = jnp.dot(vertical, updated.astype(BF16), preferred_element_type=F32)
        upper_mix_ref[x : x + 1, :] = mixed[top : top + 1]
        lower_mix_ref[x : x + 1, :] = mixed[low : low + 1]
        mixed_out[x] = mixed.astype(BF16)

    for x in (0, cells - 1):
        mixed_out[x] = jnp.zeros_like(mixed_out[x])
        for ref in (upper_ref, lower_ref, upper_mix_ref, lower_mix_ref):
            ref[x : x + 1, :] = jnp.zeros_like(ref[x : x + 1, :])
    coming[0].wait()
    for g in range(cells // GROUP):
        if g + 1 < len(coming):
            coming[g + 1].wait()
        for x in range(max(1, g * GROUP), min(cells - 1, (g + 1) * GROUP)):
            body(x)
        going[g].start()
    wait_all(going)


def first_edges_kernel(
    odd_ref, within_ref, across_ref, own_ref, courant_ref, vertical_ref, _, __,
    mixed_ref, upper_ref, lower_ref, upper_mix_ref, lower_mix_ref,
):
    height = own_ref.shape[2]
    top, low = height // 2 - 1, height - 1
    lateral = lateral_matrix(own_ref.shape[3])
    vertical = without_forced(vertical_ref[...])
    courant = courant_ref[...]
    left, right = sides(odd_ref, within_ref[...], across_ref[...])
    first, last = sides(odd_ref, own_ref[0], own_ref[1])
    for ref in (upper_ref, lower_ref, upper_mix_ref, lower_mix_ref):
        ref[...] = jnp.zeros_like(ref)
    before = [left[0], left[1], first[0], first[1]]
    after = [last[0], last[1], right[0], right[1]]
    for i, columns_of in enumerate((before[:3], before[1:], after[:3], after[1:])):
        updated = stencil(*columns_of, lateral, courant)
        upper_ref[i : i + 1, :] = updated[top : top + 1]
        lower_ref[i : i + 1, :] = updated[low : low + 1]
        mixed = jnp.dot(vertical, updated.astype(BF16), preferred_element_type=F32)
        upper_mix_ref[i : i + 1, :] = mixed[top : top + 1]
        lower_mix_ref[i : i + 1, :] = mixed[low : low + 1]
        mixed_ref[i] = mixed.astype(BF16)


def with_edges(main, edges):
    cells = main.shape[0]
    at = iota(main.shape, 0)
    return jnp.where(at == 0, edges[1:2], jnp.where(at == cells - 1, edges[2:3], main))


def ocean_kernel(
    odd_ref, ocean_ref, within_ref, across_ref, sea_ref, flux_ref, vertical_ref, out_ref
):
    cells, width = sea_ref.shape
    height = ocean_ref.shape[0] // cells
    vertical = vertical_ref[...]
    high = vertical.astype(BF16)
    low = (vertical - high.astype(F32)).astype(BF16)
    both = jnp.concatenate([high, low], axis=0)
    left, right = sides(odd_ref, within_ref[...], across_ref[...])
    lane = iota((height, width), 1)
    row = iota((height, width), 0)

    def column(x):
        if x < 0:
            return left
        if x >= cells:
            return right
        return ocean_ref[pl.ds(x, height, stride=cells), :]

    parts = []
    for x in range(cells):
        west, center, east = column(x - 1), column(x), column(x + 1)
        north = jnp.where(lane == width - 1, center, pltpu.roll(center, width - 1, 1))
        south = jnp.where(lane == 0, center, pltpu.roll(center, 1, 1))
        wet = sea_ref[x : x + 1, :].astype(F32)
        near = east + west + (north + south) - 4.0 * center
        heat = FLUX_GAIN * wet * flux_ref[0, x : x + 1, :]
        fresh = FLUX_GAIN * wet * flux_ref[1, x : x + 1, :]
        added = jnp.where(row == 0, heat, jnp.where(row == height // 2, fresh, 0.0))
        updated = (center + OCEAN_DIFFUSION * near) * wet + added
        upper = updated.astype(BF16)
        rest = (updated - upper.astype(F32)).astype(BF16)
        parts.append((upper, rest))
        if x % 2 == 0:
            continue
        upper, rest = (jnp.concatenate(p, axis=1) for p in zip(*parts))
        parts = []
        mixed = jnp.dot(both, upper, preferred_element_type=F32)
        mixed = mixed[:height] + mixed[height:]
        mixed += jnp.dot(high, rest, preferred_element_type=F32)
        out_ref[pl.ds(x - 1, height, stride=cells), :] = mixed[:, :width]
        out_ref[pl.ds(x, height, stride=cells), :] = mixed[:, width:]


PARTS = 8


def weight_copies(weight_hbm, held, sems):
    step = weight_hbm.shape[0] // PARTS
    return start_all([
        pltpu.make_async_copy(
            weight_hbm.at[pl.ds(i * step, step)], held.at[pl.ds(i * step, step)], sems.at[i]
        )
        for i in range(PARTS)
    ])


def pull_kernel(
    odd_ref, head_ref, owner_ref, block_ref, weight_hbm, sea_ref,
    upper_ref, lower_ref, upper_edge_ref, lower_edge_ref,
    temp_ref, heat_ref, moist_ref, upper_forced_ref, lower_forced_ref, send_ref, slots_ref,
    slot_rows, by_block, held, sems,
):
    copies = weight_copies(weight_hbm, held, sems)
    devices = head_ref.shape[0]
    surface = head_ref[:, 0:16, :].reshape(devices * 16, 128)
    slot_rows[...] = head_ref[:, 16:24, :].astype(F32).reshape(devices * 8, 128)
    slots_ref[...] = jnp.transpose(slot_rows[pl.ds(0, devices, stride=8), :])[:8]
    sources, blocks = owner_ref.shape
    goal = (columns(owner_ref) * 16 + columns(block_ref))[:, :1]
    pick = (goal == iota((blocks * sources, devices * 16), 1)).astype(F32).astype(BF16)
    fetched = jnp.dot(pick, surface, preferred_element_type=F32)
    wanted = jnp.concatenate(
        [jnp.transpose(fetched[k * blocks : (k + 1) * blocks]) for k in range(sources)], axis=0
    ).astype(BF16)
    lane = iota((128, blocks), 1)

    def add(j, total):
        rows = jnp.concatenate([held[j, k] for k in range(sources)], axis=1)
        product = jnp.dot(rows, wanted, preferred_element_type=F32)
        return jnp.where(lane == j, product, total)

    total = jnp.zeros((128, blocks), F32)
    step = blocks // PARTS
    for i, c in enumerate(copies):
        c.wait()
        for j in range(i * step, (i + 1) * step):
            total = add(j, total)
    by_block[...] = jnp.transpose(total)
    half = blocks // 2
    temp = jnp.concatenate(
        [by_block[pl.ds(h, half, stride=2), :] for h in range(2)], axis=1
    )
    temp_ref[...] = temp
    exchange = EXCHANGE_RATE * sea_ref[...].astype(F32)
    upper = with_edges(upper_ref[...], upper_edge_ref[...])
    lower = with_edges(lower_ref[...], lower_edge_ref[...])
    heat, moist = exchange * (temp - upper), exchange * (0.5 * temp - lower)
    heat_ref[...] = heat
    moist_ref[...] = moist
    upper = (upper + heat).astype(BF16).astype(F32)
    lower = (lower + moist).astype(BF16).astype(F32)
    upper_forced_ref[...] = upper
    lower_forced_ref[...] = lower
    two = iota((8, upper.shape[1]), 0) == 0
    first = jnp.where(two, upper[0:1], lower[0:1])
    last = jnp.where(two, upper[half - 1 : half], lower[half - 1 : half])
    send_ref[0], send_ref[1] = sides(odd_ref, first, last)


def push_kernel(
    odd_ref, place_ref, weight_hbm, sea_ref, temp_ref, heat_ref, moist_ref,
    upper_forced_ref, lower_forced_ref, upper_mix_ref, lower_mix_ref,
    upper_mix_edge_ref, lower_mix_edge_ref, within_ref, across_ref,
    courant_ref, vertical_ref, out_ref,
    flux_rows, shares, held, sems,
):
    copies = weight_copies(weight_hbm, held, sems)
    height = vertical_ref.shape[0]
    top, low = height // 2 - 1, height - 1
    cells, width = sea_ref.shape
    sub, lane = iota((cells, width), 0), iota((cells, width), 1)

    left_forced, right_forced = sides(odd_ref, within_ref[...], across_ref[...])

    def row_of(r, mix, upper, lower):
        a = vertical_ref[pl.ds(r - 7, 8), :].astype(F32)[7:8]
        kept = mix.astype(BF16).astype(F32)
        return (kept + a[:, top : top + 1] * upper + a[:, low : low + 1] * lower).astype(BF16).astype(F32)

    def updated(r, mix_ref, edge_ref):
        edges = edge_ref[...]
        center = row_of(
            r, with_edges(mix_ref[...], edges), upper_forced_ref[...], lower_forced_ref[...]
        )
        before = row_of(r, edges[0:1], left_forced[0:1], left_forced[1:2])
        after = row_of(r, edges[3:4], right_forced[0:1], right_forced[1:2])
        west = jnp.where(sub == 0, before, pltpu.roll(center, 1, 0))
        east = jnp.where(sub == cells - 1, after, pltpu.roll(center, cells - 1, 0))
        north = jnp.where(lane == width - 1, center, pltpu.roll(center, width - 1, 1))
        south = jnp.where(lane == 0, center, pltpu.roll(center, 1, 1))
        near = east + west + (north + south) - 4.0 * center
        courant = courant_ref[pl.ds(r - 7, 8), :][7:8]
        return center - courant * (center - west) + ATM_DIFFUSION * near

    exchange = EXCHANGE_RATE * sea_ref[...].astype(F32)
    temp = temp_ref[...]
    heat = 0.5 * heat_ref[...] + 0.5 * (
        exchange * (temp - updated(top, upper_mix_ref, upper_mix_edge_ref))
    )
    moist = 0.5 * moist_ref[...] + 0.5 * (
        exchange * (0.5 * temp - updated(low, lower_mix_ref, lower_mix_edge_ref))
    )
    flux_rows[...] = jnp.zeros_like(flux_rows)
    for v, flux in enumerate((heat, moist)):
        for h in range(2):
            flux_rows[pl.ds(h * 8 + v, cells, stride=16), :] = flux[:, h * 128 : (h + 1) * 128]
    blocks, sources = held.shape[0], held.shape[1]
    step = blocks // PARTS
    for i, c in enumerate(copies):
        c.wait()
        for j in range(i * step, (i + 1) * step):
            rows = flux_rows[j * 8 : (j + 1) * 8, :].astype(BF16)
            for k in range(sources):
                got = jnp.dot(rows, held[j, k], preferred_element_type=F32)
                at = (k * blocks + j) * 8
                shares[at : at + 8, :] = got

    pairs = blocks * sources
    place = place_ref[0:1, :]
    rows = iota((out_ref.shape[0], pairs), 0)
    total = jnp.zeros(out_ref.shape, F32)
    for v in range(2):
        pick = (rows == place + 4 * v).astype(F32).astype(BF16)
        share = shares[pl.ds(v, pairs, stride=8), :].astype(BF16)
        total += jnp.dot(pick, share, preferred_element_type=F32)
    out_ref[...] = total.astype(BF16)


def second_step_kernel(
    odd_ref, mixed_hbm, edge_ref, courant_ref, vertical_ref, sea_ref, temp_ref,
    upper_forced_ref, lower_forced_ref, within_ref, across_ref,
    out_hbm, mixed_ref, state, result, out_ref, in_sems, out_sems,
):
    coming = start_all(groups(mixed_hbm, mixed_ref, in_sems))
    cells, height = mixed_ref.shape[0], mixed_ref.shape[1]
    top, low = height // 2 - 1, height - 1
    lateral = lateral_matrix(mixed_ref.shape[2])
    vertical = vertical_ref[...]
    upper_column = vertical[:, top : top + 1].astype(F32)
    lower_column = vertical[:, low : low + 1].astype(F32)
    courant = courant_ref[...]

    def complete(mixed, upper, lower):
        return (mixed.astype(F32) + upper_column * upper + lower_column * lower).astype(BF16)

    left, right = sides(odd_ref, within_ref[...], across_ref[...])
    state[0] = complete(edge_ref[0], left[0:1], left[1:2])
    state[1] = complete(edge_ref[1], upper_forced_ref[0:1, :], lower_forced_ref[0:1, :])
    state[cells] = complete(
        edge_ref[2], upper_forced_ref[cells - 1 : cells, :], lower_forced_ref[cells - 1 : cells, :]
    )
    state[cells + 1] = complete(edge_ref[3], right[0:1], right[1:2])

    for g, c in enumerate(coming):
        c.wait()
        for x in range(max(1, g * GROUP), min(cells - 1, (g + 1) * GROUP)):
            state[x + 1] = complete(
                mixed_ref[x], upper_forced_ref[x : x + 1, :], lower_forced_ref[x : x + 1, :]
            )

    last = iota((8, mixed_ref.shape[2]), 0) == 7

    @pl.loop(0, cells, unroll=GROUP)
    def _(x):
        updated = stencil(state[x], state[x + 1], state[x + 2], lateral, courant)
        exchange = EXCHANGE_RATE * sea_ref[pl.ds(x, 1), :].astype(F32)
        temp = temp_ref[pl.ds(x, 1), :]
        upper = updated[top - 7 : top + 1]
        lower = updated[low - 7 : low + 1]
        upper = jnp.where(last, upper + exchange * (temp - upper), upper)
        lower = jnp.where(last, lower + exchange * (0.5 * temp - lower), lower)
        forced = jnp.concatenate(
            [updated[: top - 7], upper, updated[top + 1 : low - 7], lower], axis=0
        ).astype(BF16)
        result[x] = jnp.dot(vertical, forced, preferred_element_type=F32).astype(BF16)

    step = 32
    going = []
    for i in range(height // step):
        at = pl.ds(i * step, step)
        out_ref[at] = jnp.swapaxes(result[:, i * step : (i + 1) * step, :], 0, 1)
        going.append(pltpu.make_async_copy(out_ref.at[at], out_hbm.at[at], out_sems.at[i]))
        going[-1].start()
    wait_all(going)


def land_kernel(incoming_ref, slots_ref, sea_ref, out_ref, wide):
    devices = slots_ref.shape[1]
    cells = sea_ref.shape[0]
    wide[...] = incoming_ref[...].astype(F32)
    wet = sea_ref[...].astype(F32)
    here = (iota((cells, devices), 0) + 1).astype(F32)
    picks = [(slots_ref[s : s + 1, :] == here).astype(F32).astype(BF16) for s in range(4)]
    for v in range(2):
        total = jnp.zeros((cells, 128), F32)
        for s in range(4):
            part = wide[pl.ds(v * 4 + s, devices, stride=8), :].astype(BF16)
            total += jnp.dot(picks[s], part, preferred_element_type=F32)
        out_ref[v] = total * wet


def swap(within, across):
    peers = lax.axis_size(BOTH)
    pair = [(i, i ^ 1) for i in range(peers)]
    other = [(i, ((i + 1) ^ 1) - 1) for i in range(peers)]
    other = [(i, j % peers) for i, j in other]
    return lax.ppermute(within, BOTH, pair), lax.ppermute(across, BOTH, other)


def per_device(
    atm_state, atm_sea, zonal_courant, atm_vertical, ocean_state, ocean_sea,
    flux_in, ocean_vertical, remap_owner, remap_block, remap_weight,
):
    devices = lax.axis_size(BOTH)
    height, cells, width = atm_state.shape
    blocks, sources = remap_owner.shape
    pairs = blocks * sources
    courant = zonal_courant.reshape(height, 1)
    layers, ocean_cells, ocean_width = ocean_state.shape
    ocean_rows = ocean_state.reshape(layers * ocean_cells, ocean_width)
    owner, block = remap_owner.T, remap_block.T
    odd = is_odd()
    dma = pltpu.SemaphoreType.DMA
    held = [pltpu.VMEM(remap_weight.shape, BF16), dma((PARTS,))]
    whole = pltpu.VMEM((cells, height, width), BF16)
    levels = 64

    head, place = call(
        plan_kernel,
        (shape((devices, HEAD, 128), BF16), shape((8, pairs), jnp.int32)),
        owner, block, ocean_state,
        specs={0: ANY, 1: ANY, 2: ANY},
        scratch=[
            pltpu.VMEM((devices * 8, 128), F32),
            pltpu.VMEM(owner.shape, jnp.int32),
            pltpu.VMEM(owner.shape, jnp.int32),
            pltpu.VMEM((ocean_cells, ocean_width), F32),
            dma((3,)),
        ],
        limit=58,
        touched=1 << 20,
    )
    gathered = lax.all_to_all(head, BOTH, split_axis=0, concat_axis=0, tiled=True)

    turned, send, ocean_send = call(
        turn_kernel,
        (
            shape((cells, height, width), BF16),
            shape((2, 2, height, width), BF16),
            shape((2, layers, ocean_width), F32),
        ),
        odd, atm_state, ocean_state,
        specs={0: SCALAR, 1: pl.BlockSpec((levels, cells, width), lambda i: (i, 0, 0)), 2: ANY},
        out_specs={
            0: pl.BlockSpec((cells, levels, width), lambda i: (0, i, 0)),
            1: pl.BlockSpec((2, 2, height, width), lambda i: (0, 0, 0, 0)),
            2: pl.BlockSpec((2, layers, ocean_width), lambda i: (0, 0, 0)),
        },
        scratch=[dma((2,))],
        grid=(height // levels,),
        limit=54,
        touched=12 << 20,
    )
    near = swap(send[0], send[1])
    ocean_near = swap(ocean_send[0], ocean_send[1])
    row, small = shape((cells, width), F32), shape((8, width), F32)
    mixed, upper, lower, upper_mix, lower_mix = call(
        first_step_kernel,
        (shape((cells, height, width), BF16), row, row, row, row),
        turned, courant, atm_vertical,
        specs={0: ANY},
        out_specs={0: ANY},
        scratch=[whole, whole, dma((cells // GROUP,)), dma((cells // GROUP,))],
        touched=16 << 20,
    )
    mixed_edge, upper_edge, lower_edge, upper_mix_edge, lower_mix_edge = call(
        first_edges_kernel,
        (shape((4, height, width), BF16), small, small, small, small),
        odd, *near, send, courant, atm_vertical, *ocean_near,
        specs={0: SCALAR},
        touched=2 << 20,
    )

    temp, heat, moist, upper_forced, lower_forced, forced_send, slots = call(
        pull_kernel,
        (row, row, row, row, row, shape((2, 8, width), F32), shape((8, devices), F32)),
        odd, gathered, owner, block, remap_weight, atm_sea, upper, lower, upper_edge, lower_edge,
        specs={0: SCALAR, 4: ANY},
        scratch=[pltpu.VMEM((devices * 8, 128), F32), pltpu.VMEM((blocks, 128), F32), *held],
        touched=12 << 20,
    )
    forced_near = swap(forced_send[0], forced_send[1])
    outgoing = call(
        push_kernel,
        shape((devices * 8, 128), BF16),
        odd, place, remap_weight, atm_sea, temp, heat, moist,
        upper_forced, lower_forced, upper_mix, lower_mix, upper_mix_edge, lower_mix_edge,
        *forced_near, courant, atm_vertical,
        specs={0: SCALAR, 2: ANY},
        scratch=[pltpu.VMEM((blocks * 8, 128), F32), pltpu.VMEM((pairs * 8, 128), F32), *held],
        touched=12 << 20,
    )
    incoming = lax.all_to_all(
        outgoing.reshape(devices, 8, 128), BOTH, split_axis=0, concat_axis=0, tiled=True
    )
    state = call(
        second_step_kernel,
        shape(atm_state.shape, BF16),
        odd, mixed, mixed_edge, courant, atm_vertical, atm_sea, temp,
        upper_forced, lower_forced, *forced_near,
        specs={0: SCALAR, 1: ANY},
        out_specs={0: ANY},
        scratch=[
            whole,
            pltpu.VMEM((cells + 2, height, width), BF16),
            whole,
            pltpu.VMEM(atm_state.shape, BF16),
            dma((cells // GROUP,)),
            dma((height // 32,)),
        ],
        touched=24 << 20,
    )
    new_ocean = call(
        ocean_kernel,
        shape(ocean_rows.shape, F32),
        odd, ocean_rows, *ocean_near, ocean_sea, flux_in, ocean_vertical,
        specs={0: SCALAR},
        touched=8 << 20,
    )
    ocean_flux = call(
        land_kernel,
        shape((2, ocean_cells, ocean_width), F32),
        incoming.reshape(devices * 8, 128), slots, ocean_sea,
        scratch=[pltpu.VMEM((devices * 8, 128), F32)],
        touched=1 << 20,
    )
    return state, new_ocean.reshape(ocean_state.shape), ocean_flux


def solution(mesh):
    return jax.shard_map(
        per_device,
        mesh=mesh,
        in_specs=(
            P(None, BOTH, None), P(BOTH, None), P(), P(), P(None, BOTH, None), P(BOTH, None),
            P(None, BOTH, None), P(), P(BOTH, None), P(BOTH, None), P(BOTH, None, None, None),
        ),
        out_specs=(P(None, BOTH, None), P(None, BOTH, None), P(None, BOTH, None)),
        check_vma=False,
    )
```

time: 121 us -> 80.1 us (0.66)
  the two profiles are of different devices: /device:TPU:0 before, /device:TPU:1 now
where the time goes in v1:
time: 80.1 us; the launch traced here: 79.7 us
  Pallas kernels  39.4 us (49%)
  starting transfers between devices  34.1 us (43%)
  waiting for transfers between devices  3.09 us (4%)
  local copies, waits for them, and re-layouts  2.25 us (3%)
  between operations  0.92 us (1%)
    pallas_call x9, Pallas kernels, call(): pl.pallas_call(kernel, out_shape=outs, grid=grid, in_specs=[specs.get(i,...  39.4 us
    all_to_all x1, starting transfers between devices, per_device(): lax.all_to_all(head, BOTH, split_axis=0, concat_axis=0, tiled=True)  11.5 us
    ppermute x6, starting transfers between devices, swap(): return (lax.ppermute(within, BOTH, pair), lax.ppermute(across, BOTH, other))  11.4 us
    all_to_all x1, starting transfers between devices, per_device(): lax.all_to_all(outgoing.reshape(devices, 8, 128), BOTH, split_axis=0, con...  11.1 us
    ppermute x6, waiting for transfers between devices, swap(): return (lax.ppermute(within, BOTH, pair), lax.ppermute(across, BOTH, other))  3.08 us
  transfers between devices with their start and end apart: 8, of which 2 were waited for; matrix products, arithmetic and copies ran while one was open for 3% of the time, Pallas kernels for 32%

profile of v1, /device:TPU:1, one launch (start us, length us, event | category | flops | bytes accessed | tf_op | source)
XLA Modules:
  0.0 79.7 jit_solution(11107231083477834846)
XLA Ops:
  0.6 2.2 %shard_map.133 = (bf16[128,24,128]{2,1,0:T(8,128)(2,1)}, s32[8,256]{1,0:T(8,128)}) custom-call(s32[4,64]{1,0:T(4,128)} %bitcast.22, s32[4,64]{1,0:T(4,128)} %bitcast.24, f32[160,16,128]{2,1,0:T(8,128)} %ocean_hbm.3), custom_call_target="tpu_custom_call" | custom-call | bytes 1048576 | tf_op jit(solution)/shard_map/pallas_call | solution.py:28
  2.9 0.0 copy-start.10
  2.9 0.0 copy-start.1
  2.9 11.5 %all-to-all-start = ((bf16[128,24,128]{2,1,0:T(8,128)(2,1)}), bf16[128,24,128]{2,1,0:T(8,128)(2,1)S(1)}, u32[]{:S(2)}, u32[]{:S(2)}) async-start(bf16[128,24,128]{2,1,0:T(8,128)(2,1)} %get-tuple-element.30), calls=%async_computation | async-start | bytes 1572864 | tf_op jit(solution)/shard_map/all_to_all | solution.py:520
  14.4 5.4 %shard_map.130 = (bf16[32,256,256]{2,1,0:T(8,128)(2,1)}, bf16[2,2,256,256]{3,2,1,0:T(8,128)(2,1)}, f32[2,160,128]{2,1,0:T(8,128)}) custom-call(s32[1]{0:T(128)} %bitcast.odd_ref, bf16[256,32,256]{2,1,0:T(8,128)(2,1)} %state_ref.1, f32[160,16,128]{2,1,0:T(8,128)} %ocean_hbm.3), custom_call_target="tpu_custom_call" | custom-call | bytes 12582912 | tf_op jit(solution)/shard_map/pallas_call | solution.py:28
  19.8 0.0 copy-start.3
  19.9 0.0 copy-start.7
  19.9 0.0 copy-start.8
  19.9 1.1 %slice_bitcast_fusion = (bf16[2,256,256]{2,1,0:T(8,128)(2,1)S(1)}, bf16[2,256,256]{2,1,0:T(8,128)(2,1)S(1)}) fusion(bf16[2,2,256,256]{3,2,1,0:T(8,128)(2,1)} %get-tuple-element.27.own_ref), kind=kLoop, calls=%fused_computation | loop fusion | bytes 1048576 | tf_op jit(solution)/shard_map/squeeze | solution.py:541
  21.0 1.1 %collective-permute-start = (bf16[2,256,256]{2,1,0:T(8,128)(2,1)S(1)}, bf16[2,256,256]{2,1,0:T(8,128)(2,1)S(1)}, u32[]{:S(2)}, u32[]{:S(2)}) collective-permute-start(bf16[2,256,256]{2,1,0:T(8,128)(2,1)S(1)} %get-tuple-element.48), channel_id=1, source_target_pairs={{0,1},{1,0},{2,3},{3,2},{4,5},{5,4},{6,7},{7,6},{8,9},{9,8},{10,11... | collective-permute-start | bytes 786440 | tf_op jit(solution)/shard_map/ppermute | solution.py:484
  22.1 0.7 collective-permute-start.1
  22.9 0.9 %slice_bitcast_fusion.2 = (f32[160,128]{1,0:T(8,128)S(1)}, f32[160,128]{1,0:T(8,128)S(1)}) fusion(f32[2,160,128]{2,1,0:T(8,128)} %get-tuple-element.28), kind=kLoop, calls=%fused_computation.2 | loop fusion | bytes 327680 | tf_op jit(solution)/shard_map/squeeze | solution.py:542
  23.8 6.8 %collective-permute-start.2 = (f32[160,128]{1,0:T(8,128)S(1)}, f32[160,128]{1,0:T(8,128)S(1)}, u32[]{:S(2)}, u32[]{:S(2)}) collective-permute-start(f32[160,128]{1,0:T(8,128)S(1)} %get-tuple-element.50), channel_id=1, source_target_pairs={{0,1},{1,0},{2,3},{3,2},{4,5},{5,4},{6,7},{7,6},{8,9},{9,8},{10,11... | collective-permute-start | bytes 245768 | tf_op jit(solution)/shard_map/ppermute | solution.py:484
  30.6 0.0 collective-permute-start.3
  30.6 0.1 copy.14.courant_ref
  30.7 6.5 %shard_map.131 = (bf16[32,256,256]{2,1,0:T(8,128)(2,1)}, f32[32,256]{1,0:T(8,128)S(1)}, f32[32,256]{1,0:T(8,128)S(1)}, f32[32,256]{1,0:T(8,128)S(1)}, f32[32,256]{1,0:T(8,128)S(1)}) custom-call(bf16[32,256,256]{2,1,0:T(8,128)(2,1)} %get-tuple-element.25.turned_hbm, f32[256,1]{1,0:T(8,128)S(1)} %copy.14.courant_ref, bf16[256,256]{1,0:T(8,128)(2,1)S(1)} %copy-done.1), custom_call_target="tpu_custom_call" | custom-call | bytes 16777216 | tf_op jit(solution)/shard_map/pallas_call | solution.py:28
  37.2 0.0 collective-permute-done.3.__.across_ref
  37.2 0.0 collective-permute-done.within_ref
  37.3 0.7 shard_map.132
  38.0 0.0 all-to-all-done.head_ref
  38.0 0.0 copy-start.9
  38.1 5.5 %shard_map.134 = (f32[32,256]{1,0:T(8,128)S(1)}, f32[32,256]{1,0:T(8,128)S(1)}, f32[32,256]{1,0:T(8,128)S(1)}, f32[32,256]{1,0:T(8,128)S(1)}, f32[32,256]{1,0:T(...) custom-call(s32[1]{0:T(128)} %bitcast.odd_ref, bf16[128,24,128]{2,1,0:T(8,128)(2,1)S(1)} %all-to-all-done.head_ref, ...), custom_call_target="tpu_custom_call" | custom-call | bytes 12582912 | tf_op jit(solution)/shard_map/pallas_call | solution.py:28
  43.6 2.8 %collective-permute-start.4 = (f32[8,256]{1,0:T(8,128)S(1)}, f32[8,256]{1,0:T(8,128)S(1)}, u32[]{:S(2)}, u32[]{:S(2)}) collective-permute-start(f32[8,256]{1,0:T(8,128)S(1)} %get-tuple-element.52), channel_id=1, source_target_pairs={{0,1},{1,0},{2,3},{3,2},{4,5},{5,4},{6,7},{7,6},{8,9},{9,8},{10,11... | collective-permute-start | bytes 24584 | tf_op jit(solution)/shard_map/ppermute | solution.py:484
  46.4 0.0 collective-permute-start.5
  46.4 0.8 %collective-permute-done.4.within_ref = f32[8,256]{1,0:T(8,128)S(1)} collective-permute-done((f32[8,256]{1,0:T(8,128)S(1)}, f32[8,256]{1,0:T(8,128)S(1)}, u32[]{:S(2)}, u32[]{:S(2)}) %collective-permute-start.4) | collective-permute-done | bytes 8224 | tf_op jit(solution)/shard_map/ppermute | solution.py:484
  47.2 2.2 %collective-permute-done.5.across_ref = f32[8,256]{1,0:T(8,128)S(1)} collective-permute-done((f32[8,256]{1,0:T(8,128)S(1)}, f32[8,256]{1,0:T(8,128)S(1)}, u32[]{:S(2)}, u32[]{:S(2)}) %collective-permute-start.5) | collective-permute-done | bytes 8224 | tf_op jit(solution)/shard_map/ppermute | solution.py:484
  49.5 0.0 copy-start.6
  49.5 5.6 %shard_map.137 = bf16[1024,128]{1,0:T(8,128)(2,1)} custom-call(s32[1]{0:T(128)} %bitcast.odd_ref, s32[8,256]{1,0:T(8,128)S(1)} %copy-done.9, bf16[64,4,128,128]{3,2,1,0:T(8,128)(2,1)} %weight_hbm.3, s32[32,256]{1,0:T(8,128)S(1)} %copy-done.3, f32[32,256]{1,0:T(8,128)S(1)} %get-tuple-element.35.temp_ref, f32[32,256]{1,0:T(8,128)S(1)} %get-tuple-element.40.heat_ref, ...), custom_call_target="tpu_custom_call" | custom-call | bytes 12582912 | tf_op jit(solution)/shard_map/pallas_call | solution.py:28
  55.1 11.1 %all-to-all-start.1 = ((bf16[128,8,128]{2,1,0:T(8,128)(2,1)}), bf16[128,8,128]{2,1,0:T(8,128)(2,1)S(1)}, u32[]{:S(2)}, u32[]{:S(2)}) async-start(bf16[128,8,128]{2,1,0:T(8,128)(2,1)} %bitcast.12), calls=%async_computation.1 | async-start | bytes 524288 | tf_op jit(solution)/shard_map/all_to_all | solution.py:580
  66.3 2.9 %shard_map.136 = f32[2560,128]{1,0:T(8,128)} custom-call(s32[1]{0:T(128)} %bitcast.odd_ref, f32[2560,128]{1,0:T(8,128)S(1)} %bitcast.20, f32[160,128]{1,0:T(8,128)S(1)} %collective-permute-done.2._.within_ref, f32[160,128]{1,0:T(8,128)S(1)} %collective-permute-done.3.__.across_ref, s32[16,128]{1,0:T(8,128)S(1)} %copy-done.5, f32[2,16,128]{2,1,0:T(8,128)S(1)} %copy-done.6, ...), custom_call_target="tpu_custom_call" | custom-call | bytes 8388608 | tf_op jit(solution)/shard_map/pallas_call | solution.py:28
  69.2 9.7 %shard_map.135 = bf16[256,32,256]{2,1,0:T(8,128)(2,1)} custom-call(s32[1]{0:T(128)} %bitcast.odd_ref, bf16[32,256,256]{2,1,0:T(8,128)(2,1)} %get-tuple-element.26.mixed_hbm, bf16[4,256,256]{2,1,0:T(8,128)(2,1)S(1)} %get-tuple-element.29.edge_ref, f32[256,1]{1,0:T(8,128)S(1)} %copy.14.courant_ref, bf16[256,256]{1,0:T(8,128)(2,1)S(1)} %copy-done.1, ...), custom_call_target="tpu_custom_call" | custom-call | bytes 25165824 | tf_op jit(solution)/shard_map/pallas_call | solution.py:28
  78.9 0.8 %shard_map.138 = f32[2,16,128]{2,1,0:T(8,128)} custom-call(bf16[1024,128]{1,0:T(8,128)(2,1)S(1)} %bitcast.21, f32[8,128]{1,0:T(8,128)S(1)} %get-tuple-element.46.slots_ref, s32[16,128]{1,0:T(8,128)S(1)} %copy-done.5), custom_call_target="tpu_custom_call" | custom-call | bytes 1048576 | tf_op jit(solution)/shard_map/pallas_call | solution.py:28
  (19 shorter events, 0.0 us)
Async XLA Ops:
  2.9 27.7 %copy-start.10 = (f32[256]{0:T(256)S(1)}, f32[256]{0:T(256)}, u32[]{:S(2)}) copy-start(f32[256]{0:T(256)} %param.13) | copy-start | bytes 3076
  2.9 27.9 %copy-start.1 = (bf16[256,256]{1,0:T(8,128)(2,1)S(1)}, bf16[256,256]{1,0:T(8,128)(2,1)}, u32[]{:S(2)}) copy-start(bf16[256,256]{1,0:T(8,128)(2,1)} %vertical_ref.9) | copy-start | bytes 393220
  2.9 35.1 %all-to-all-start = ((bf16[128,24,128]{2,1,0:T(8,128)(2,1)}), bf16[128,24,128]{2,1,0:T(8,128)(2,1)S(1)}, u32[]{:S(2)}, u32[]{:S(2)}) async-start(bf16[128,24,128]{2,1,0:T(8,128)(2,1)} %get-tuple-element.30), calls=%async_computation | async-start | bytes 1572864 | tf_op jit(solution)/shard_map/all_to_all | solution.py:520
  19.8 17.4 %copy-start.2 = (bf16[2,2,256,256]{3,2,1,0:T(8,128)(2,1)S(1)}, bf16[2,2,256,256]{3,2,1,0:T(8,128)(2,1)}, u32[]{:S(2)}) copy-start(bf16[2,2,256,256]{3,2,1,0:T(8,128)(2,1)} %get-tuple-element.27.own_ref) | copy-start | bytes 1572868
  19.8 18.2 %copy-start.3 = (s32[32,256]{1,0:T(8,128)S(1)}, s32[32,256]{1,0:T(8,128)}, u32[]{:S(2)}) copy-start(s32[32,256]{1,0:T(8,128)} %sea_ref.8) | copy-start | bytes 98308
  19.9 18.2 %copy-start.7 = (s32[64,4]{0,1:T(4,128)S(1)}, s32[64,4]{0,1:T(4,128)}, u32[]{:S(2)}) copy-start(s32[64,4]{0,1:T(4,128)} %param.19) | copy-start | bytes 3076
  19.9 18.2 %copy-start.8 = (s32[64,4]{0,1:T(4,128)S(1)}, s32[64,4]{0,1:T(4,128)}, u32[]{:S(2)}) copy-start(s32[64,4]{0,1:T(4,128)} %param.20) | copy-start | bytes 3076
  21.0 16.2 %collective-permute-start = (bf16[2,256,256]{2,1,0:T(8,128)(2,1)S(1)}, bf16[2,256,256]{2,1,0:T(8,128)(2,1)S(1)}, u32[]{:S(2)}, u32[]{:S(2)}) collective-permute-start(bf16[2,256,256]{2,1,0:T(8,128)(2,1)S(1)} %get-tuple-element.48), channel_id=1, source_target_pairs={{0,1},{1,0},{2,3},{3,2},{4,5},{5,4},{6,7},{7,6},{8,9},{9,8},{10,11... | collective-permute-start | bytes 786440 | tf_op jit(solution)/shard_map/ppermute | solution.py:484
  22.1 15.1 %collective-permute-start.1 = (bf16[2,256,256]{2,1,0:T(8,128)(2,1)S(1)}, bf16[2,256,256]{2,1,0:T(8,128)(2,1)S(1)}, u32[]{:S(2)}, u32[]{:S(2)}) collective-permute-start(bf16[2,256,256]{2,1,0:T(8,128)(2,1)S(1)} %get-tuple-element.47), channel_id=1, source_target_pairs={{0,127},{1,2},{2,1},{3,4},{4,3},{5,6},{6,5},{7,8},{8,7},{9,10},{10... | collective-permute-start | bytes 786440 | tf_op jit(solution)/shard_map/ppermute | solution.py:484
  23.8 13.4 %collective-permute-start.2 = (f32[160,128]{1,0:T(8,128)S(1)}, f32[160,128]{1,0:T(8,128)S(1)}, u32[]{:S(2)}, u32[]{:S(2)}) collective-permute-start(f32[160,128]{1,0:T(8,128)S(1)} %get-tuple-element.50), channel_id=1, source_target_pairs={{0,1},{1,0},{2,3},{3,2},{4,5},{5,4},{6,7},{7,6},{8,9},{9,8},{10,11... | collective-permute-start | bytes 245768 | tf_op jit(solution)/shard_map/ppermute | solution.py:484
  30.6 6.7 %collective-permute-start.3 = (f32[160,128]{1,0:T(8,128)S(1)}, f32[160,128]{1,0:T(8,128)S(1)}, u32[]{:S(2)}, u32[]{:S(2)}) collective-permute-start(f32[160,128]{1,0:T(8,128)S(1)} %get-tuple-element.49), channel_id=1, source_target_pairs={{0,127},{1,2},{2,1},{3,4},{4,3},{5,6},{6,5},{7,8},{8,7},{9,10},{10... | collective-permute-start | bytes 245768 | tf_op jit(solution)/shard_map/ppermute | solution.py:484
  38.0 11.4 %copy-start.9 = (s32[8,256]{1,0:T(8,128)S(1)}, s32[8,256]{1,0:T(8,128)}, u32[]{:S(2)}) copy-start(s32[8,256]{1,0:T(8,128)} %get-tuple-element.39.place_ref) | copy-start | bytes 24580
  43.6 3.6 %collective-permute-start.4 = (f32[8,256]{1,0:T(8,128)S(1)}, f32[8,256]{1,0:T(8,128)S(1)}, u32[]{:S(2)}, u32[]{:S(2)}) collective-permute-start(f32[8,256]{1,0:T(8,128)S(1)} %get-tuple-element.52), channel_id=1, source_target_pairs={{0,1},{1,0},{2,3},{3,2},{4,5},{5,4},{6,7},{7,6},{8,9},{9,8},{10,11... | collective-permute-start | bytes 24584 | tf_op jit(solution)/shard_map/ppermute | solution.py:484
  46.4 3.1 %collective-permute-start.5 = (f32[8,256]{1,0:T(8,128)S(1)}, f32[8,256]{1,0:T(8,128)S(1)}, u32[]{:S(2)}, u32[]{:S(2)}) collective-permute-start(f32[8,256]{1,0:T(8,128)S(1)} %get-tuple-element.51), channel_id=1, source_target_pairs={{0,127},{1,2},{2,1},{3,4},{4,3},{5,6},{6,5},{7,8},{8,7},{9,10},{10... | collective-permute-start | bytes 24584 | tf_op jit(solution)/shard_map/ppermute | solution.py:484
  49.4 16.8 %copy-start = (f32[160,16,128]{2,1,0:T(8,128)S(1)}, f32[160,16,128]{2,1,0:T(8,128)}, u32[]{:S(2)}) copy-start(f32[160,16,128]{2,1,0:T(8,128)} %ocean_hbm.3) | copy-start | bytes 3932164
  49.4 16.8 %copy-start.4 = (f32[160,160]{1,0:T(8,128)S(1)}, f32[160,160]{1,0:T(8,128)}, u32[]{:S(2)}) copy-start(f32[160,160]{1,0:T(8,128)} %vertical_ref.8) | copy-start | bytes 307204
  49.5 16.8 %copy-start.5 = (s32[16,128]{1,0:T(8,128)S(1)}, s32[16,128]{1,0:T(8,128)}, u32[]{:S(2)}) copy-start(s32[16,128]{1,0:T(8,128)} %sea_ref.9) | copy-start | bytes 24580
  49.5 16.8 %copy-start.6 = (f32[2,16,128]{2,1,0:T(8,128)S(1)}, f32[2,16,128]{2,1,0:T(8,128)}, u32[]{:S(2)}) copy-start(f32[2,16,128]{2,1,0:T(8,128)} %flux_ref.1) | copy-start | bytes 49156
  55.1 23.7 %all-to-all-start.1 = ((bf16[128,8,128]{2,1,0:T(8,128)(2,1)}), bf16[128,8,128]{2,1,0:T(8,128)(2,1)S(1)}, u32[]{:S(2)}, u32[]{:S(2)}) async-start(bf16[128,8,128]{2,1,0:T(8,128)(2,1)} %bitcast.12), calls=%async_computation.1 | async-start | bytes 524288 | tf_op jit(solution)/shard_map/all_to_all | solution.py:580

commit v2 on v1

v2 whole, which is shorter than its diff:
```python
import functools

import jax
import jax.numpy as jnp
from jax import lax
from jax.experimental import pallas as pl
from jax.experimental.pallas import tpu as pltpu
from jax.sharding import PartitionSpec as P

ATM_DIFFUSION = 0.1
OCEAN_DIFFUSION = 0.15
EXCHANGE_RATE = 0.3
FLUX_GAIN = 0.5

F32 = jnp.float32
BF16 = jnp.bfloat16
VM = pltpu.VMEM
BOTH = ("comp", "tile")
HEAD = 24


def call(kernel, outs, *args, scratch=(), specs=None, out_specs=None, limit=50, touched=0, grid=()):
    specs, out_specs = specs or {}, out_specs or {}
    single = not isinstance(outs, tuple)
    placed = [
        out_specs.get(i, pl.BlockSpec(memory_space=VM)) for i in range(1 if single else len(outs))
    ]
    return pl.pallas_call(
        kernel,
        out_shape=outs,
        grid=grid,
        in_specs=[specs.get(i, pl.BlockSpec(memory_space=VM)) for i in range(len(args))],
        out_specs=placed[0] if single else tuple(placed),
        scratch_shapes=list(scratch),
        compiler_params=pltpu.CompilerParams(vmem_limit_bytes=limit << 20),
        cost_estimate=pl.CostEstimate(flops=0, bytes_accessed=touched, transcendentals=0),
    )(*args)


SCALAR = pl.BlockSpec(memory_space=pltpu.SMEM)
ANY = pl.BlockSpec(memory_space=pltpu.HBM)


def start_all(copies):
    for c in copies:
        c.start()
    return copies


def wait_all(copies):
    for c in copies:
        c.wait()


def shape(dims, dtype):
    return jax.ShapeDtypeStruct(dims, dtype)


def iota(dims, axis):
    return lax.broadcasted_iota(jnp.int32, dims, axis)


def columns(ref):
    count, rows = ref.shape
    wide = [jnp.broadcast_to(ref[k : k + 1, :], (128, rows)) for k in range(count)]
    return jnp.concatenate([jnp.transpose(w) for w in wide], axis=0)


def is_odd():
    return jnp.bitwise_and(lax.axis_index("tile"), 1).astype(jnp.int32).reshape(1)


def plan_kernel(
    owner_hbm, block_hbm, ocean_hbm, head_ref, place_ref, slot_rows, places, owner_ref, block_ref, surface_ref, sems
):
    copies = start_all([
        pltpu.make_async_copy(owner_hbm, owner_ref, sems.at[0]),
        pltpu.make_async_copy(block_hbm, block_ref, sems.at[1]),
        pltpu.make_async_copy(ocean_hbm.at[0], surface_ref, sems.at[2]),
    ])
    devices = head_ref.shape[0]
    slot_rows[...] = jnp.zeros_like(slot_rows)
    wait_all(copies)
    owner, block = columns(owner_ref), columns(block_ref)
    pairs = owner.shape[0]
    hits = (owner == iota((pairs, devices), 1)).astype(F32)
    earlier = (iota((pairs, pairs), 1) < iota((pairs, pairs), 0)).astype(F32)
    before = jnp.dot(earlier.astype(BF16), hits.astype(BF16), preferred_element_type=F32)
    slot = jnp.sum(before * hits, axis=1, keepdims=True)
    marked = jnp.where(
        slot == iota((pairs, 128), 1).astype(F32), (block + 1).astype(F32), 0.0
    )
    wanted = jnp.dot(
        jnp.transpose(hits).astype(BF16), marked.astype(BF16), preferred_element_type=F32
    )
    places[...] = owner.astype(F32) * 8.0 + slot
    spread = jnp.transpose(
        jnp.concatenate([places[pl.ds(h, pairs // 2, stride=2), :] for h in range(2)], axis=0)
    )
    place_ref[...] = spread[:8].astype(jnp.int32)
    slot_rows[pl.ds(0, devices, stride=8), :] = wanted
    surface = surface_ref[...].astype(BF16)
    head_ref[:, 0:16, :] = jnp.broadcast_to(surface[None], (devices, 16, 128))
    head_ref[:, 16:24, :] = slot_rows[...].reshape(devices, 8, 128).astype(BF16)


def edges_kernel(
    odd_ref, state_ref, ocean_hbm, weight_hbm, owner_ref, block_ref, sea_ref,
    state_a_ref, state_b_ref, weight_a_hbm, weight_b_hbm, pack_a_ref, pack_b_ref,
    ocean_first, ocean_last, sems,
):
    i, odd = pl.program_id(0), odd_ref[0]
    blocks = weight_hbm.shape[0]
    at_a = (1 - odd) * (blocks - 2)
    copies = [
        pltpu.make_async_copy(weight_hbm.at[pl.ds(at_a, 2)], weight_a_hbm, sems.at[0]),
        pltpu.make_async_copy(weight_hbm.at[pl.ds(blocks - 2 - at_a, 2)], weight_b_hbm, sems.at[1]),
        pltpu.make_async_copy(ocean_hbm.at[:, 0], ocean_first, sems.at[2]),
        pltpu.make_async_copy(ocean_hbm.at[:, ocean_hbm.shape[1] - 1], ocean_last, sems.at[3]),
    ]
    pl.when(i == 0)(lambda: (start_all(copies), None)[1])
    rows, cells = state_ref.shape[0], state_ref.shape[1]
    first = jnp.swapaxes(state_ref[:, 0:8, :], 0, 1)[0:2]
    last = jnp.swapaxes(state_ref[:, cells - 8 : cells, :], 0, 1)[6:8]
    at = pl.ds(pl.multiple_of(i * rows, rows), rows)
    state_a_ref[:, at, :], state_b_ref[:, at, :] = sides(odd_ref, first, last)

    @pl.when(i == pl.num_programs(0) - 1)
    def _():
        layers = ocean_first.shape[0]
        goal = (owner_ref[...] * 16 + block_ref[...]).astype(F32)
        sea = sea_ref[...].astype(F32)
        width = sea.shape[1] // 2
        wait_all(copies)
        ends = [ocean_first[...], ocean_last[...]], [sea[0:1], sea[cells - 1 : cells]]
        for ref, ocean, line in zip(
            (pack_a_ref, pack_b_ref), sides(odd_ref, *ends[0]), sides(odd_ref, *ends[1])
        ):
            ref[0:layers, :] = ocean
            ref[layers:, :] = jnp.zeros_like(ref[layers:, :])
            for h in range(2):
                ref[layers + h : layers + h + 1, :] = line[:, h * width : (h + 1) * width]
            ref[layers + 8 : layers + 8 + goal.shape[0], 0 : goal.shape[1]] = goal


def sides(odd_ref, within, across):
    odd = odd_ref[0] == 1
    return jnp.where(odd, within, across), jnp.where(odd, across, within)


def lateral_matrix(size):
    row, col = iota((size, size), 0), iota((size, size), 1)
    near = jnp.where(jnp.abs(row - col) == 1, 1.0, 0.0)
    edge = jnp.where((row == 0) | (row == size - 1), -3.0, -4.0)
    return (near + jnp.where(row == col, edge, 0.0)).astype(BF16)


def without_forced(vertical):
    height = vertical.shape[0]
    col = iota(vertical.shape, 1)
    keep = (col != height // 2 - 1) & (col != height - 1)
    return jnp.where(keep, vertical.astype(F32), 0.0).astype(BF16)


def stencil(west, center, east, lateral, courant):
    w, c, e = west.astype(F32), center.astype(F32), east.astype(F32)
    side = jnp.dot(center, lateral, preferred_element_type=F32)
    return c + courant * (w - c) + ATM_DIFFUSION * (w + e + side)


GROUP = 8
LEVEL_PARTS = 4


def groups(hbm, held, sems, out=False):
    copies = []
    for g in range(held.shape[0] // GROUP):
        at = pl.ds(g * GROUP, GROUP)
        ends = (held.at[at], hbm.at[at]) if out else (hbm.at[at], held.at[at])
        copies.append(pltpu.make_async_copy(*ends, sems.at[g]))
    return copies


def keep_rows(ref, x, updated, mixed):
    height = updated.shape[0]
    for n, (field, r) in enumerate(
        ((updated, height // 2), (updated, height), (mixed, height // 2), (mixed, height))
    ):
        ref[n, x : x + 1, :] = field[r - 1 : r]


def first_step_kernel(
    state_hbm, courant_ref, vertical_ref, mixed_hbm, rows_ref, state, turned, mixed_out, in_sems, out_sems,
):
    levels = state.shape[0] // LEVEL_PARTS
    coming = start_all([
        pltpu.make_async_copy(
            state_hbm.at[pl.ds(n * levels, levels)], state.at[pl.ds(n * levels, levels)], in_sems.at[n]
        )
        for n in range(LEVEL_PARTS)
    ])
    going = groups(mixed_hbm, mixed_out, out_sems, out=True)
    cells, height = turned.shape[0], turned.shape[1]
    lateral = lateral_matrix(turned.shape[2])
    vertical = without_forced(vertical_ref[...])
    courant = courant_ref[...]

    def body(x):
        updated = stencil(turned[x - 1], turned[x], turned[x + 1], lateral, courant)
        mixed = jnp.dot(vertical, updated.astype(BF16), preferred_element_type=F32)
        keep_rows(rows_ref, x, updated, mixed)
        mixed_out[x] = mixed.astype(BF16)

    for x in (0, cells - 1):
        mixed_out[x] = jnp.zeros_like(mixed_out[x])
        rows_ref[:, x : x + 1, :] = jnp.zeros_like(rows_ref[:, x : x + 1, :])
    step = 32
    for n, c in enumerate(coming):
        c.wait()
        for at in range(n * levels, (n + 1) * levels, step):
            turned[:, at : at + step, :] = jnp.swapaxes(state[at : at + step], 0, 1)
    for g in range(cells // GROUP):
        for x in range(max(1, g * GROUP), min(cells - 1, (g + 1) * GROUP)):
            body(x)
        going[g].start()
    wait_all(going)


def first_edges_kernel(
    odd_ref, within_ref, across_ref, own_a_ref, own_b_ref, courant_ref, vertical_ref, _, __,
    mixed_hbm, rows_ref, mixed_out, sem,
):
    height = own_a_ref.shape[1]
    lateral = lateral_matrix(own_a_ref.shape[2])
    vertical = without_forced(vertical_ref[...])
    courant = courant_ref[...]
    left, right = sides(odd_ref, within_ref[...], across_ref[...])
    first, last = sides(odd_ref, own_a_ref[...], own_b_ref[...])
    rows_ref[...] = jnp.zeros_like(rows_ref)
    before = [left[0], left[1], first[0], first[1]]
    after = [last[0], last[1], right[0], right[1]]
    for i, columns_of in enumerate((before[:3], before[1:], after[:3], after[1:])):
        updated = stencil(*columns_of, lateral, courant)
        mixed = jnp.dot(vertical, updated.astype(BF16), preferred_element_type=F32)
        keep_rows(rows_ref, i, updated, mixed)
        mixed_out[i] = mixed.astype(BF16)
    copy = pltpu.make_async_copy(mixed_out, mixed_hbm, sem)
    copy.start()
    copy.wait()


def with_edges(main, edges):
    cells = main.shape[0]
    at = iota(main.shape, 0)
    return jnp.where(at == 0, edges[1:2], jnp.where(at == cells - 1, edges[2:3], main))


def ocean_kernel(
    odd_ref, ocean_hbm, within_ref, across_ref, sea_ref, flux_ref, vertical_ref, out_hbm,
    ocean_ref, out_ref, sem,
):
    copy = pltpu.make_async_copy(ocean_hbm, ocean_ref, sem)
    copy.start()
    cells, width = sea_ref.shape
    height = ocean_ref.shape[0] // cells
    vertical = vertical_ref[...]
    high = vertical.astype(BF16)
    low = (vertical - high.astype(F32)).astype(BF16)
    both = jnp.concatenate([high, low], axis=0)
    left, right = sides(odd_ref, within_ref[0:height, :], across_ref[0:height, :])
    lane = iota((height, width), 1)
    row = iota((height, width), 0)

    copy.wait()

    def column(x):
        if x < 0:
            return left
        if x >= cells:
            return right
        return ocean_ref[pl.ds(x, height, stride=cells), :]

    parts = []
    for x in range(cells):
        west, center, east = column(x - 1), column(x), column(x + 1)
        north = jnp.where(lane == width - 1, center, pltpu.roll(center, width - 1, 1))
        south = jnp.where(lane == 0, center, pltpu.roll(center, 1, 1))
        wet = sea_ref[x : x + 1, :].astype(F32)
        near = east + west + (north + south) - 4.0 * center
        heat = FLUX_GAIN * wet * flux_ref[0, x : x + 1, :]
        fresh = FLUX_GAIN * wet * flux_ref[1, x : x + 1, :]
        added = jnp.where(row == 0, heat, jnp.where(row == height // 2, fresh, 0.0))
        updated = (center + OCEAN_DIFFUSION * near) * wet + added
        upper = updated.astype(BF16)
        rest = (updated - upper.astype(F32)).astype(BF16)
        parts.append((upper, rest))
        if x % 2 == 0:
            continue
        upper, rest = (jnp.concatenate(p, axis=1) for p in zip(*parts))
        parts = []
        mixed = jnp.dot(both, upper, preferred_element_type=F32)
        mixed = mixed[:height] + mixed[height:]
        mixed += jnp.dot(high, rest, preferred_element_type=F32)
        out_ref[pl.ds(x - 1, height, stride=cells), :] = mixed[:, :width]
        out_ref[pl.ds(x, height, stride=cells), :] = mixed[:, width:]
    copy = pltpu.make_async_copy(out_ref, out_hbm, sem)
    copy.start()
    copy.wait()


PARTS = 8


def weight_copies(weight_hbm, held, sems):
    step = weight_hbm.shape[0] // PARTS
    return start_all([
        pltpu.make_async_copy(
            weight_hbm.at[pl.ds(i * step, step)], held.at[pl.ds(i * step, step)], sems.at[i]
        )
        for i in range(PARTS)
    ])


def couple_kernel(
    odd_ref, head_ref, own_pack_ref, within_pack_ref, across_pack_ref,
    weight_hbm, within_weight_ref, across_weight_ref, sea_ref, place_ref,
    rows_ref, edges_ref, courant_ref, vertical_ref, coupled_ref, slots_ref, out_ref,
    slot_rows, by_block, flux_rows, shares, held, sems,
):
    copies = weight_copies(weight_hbm, held, sems)
    devices = head_ref.shape[0]
    blocks, sources = held.shape[0], held.shape[1]
    surface = head_ref[:, 0:16, :].reshape(devices * 16, 128)
    slot_rows[...] = head_ref[:, 16:24, :].astype(F32).reshape(devices * 8, 128)
    slots_ref[...] = jnp.transpose(slot_rows[pl.ds(0, devices, stride=8), :])[:8]

    layers = own_pack_ref.shape[0] - 16
    left_pack, right_pack = sides(
        odd_ref, within_pack_ref[layers:, :], across_pack_ref[layers:, :]
    )
    lane = iota((8, 128), 1)
    goals = jnp.where(
        lane < blocks,
        own_pack_ref[layers + 8 :, :],
        jnp.where(
            lane < blocks + 2,
            pltpu.roll(left_pack[8:], 2, 1),
            jnp.where(lane < blocks + 4, pltpu.roll(right_pack[8:], blocks + 2, 1), -1.0),
        ),
    )
    count = blocks + 8
    goal = jnp.concatenate(
        [
            jnp.transpose(jnp.broadcast_to(goals[k : k + 1], (128, 128)))[:count, :1]
            for k in range(sources)
        ],
        axis=0,
    ).astype(jnp.int32)
    pick = (goal == iota((sources * count, devices * 16), 1)).astype(F32).astype(BF16)
    fetched = jnp.dot(pick, surface, preferred_element_type=F32)
    empty = jnp.zeros((128 - count, 128), F32)
    wanted = jnp.concatenate(
        [
            jnp.transpose(jnp.concatenate([fetched[k * count : (k + 1) * count], empty], axis=0))
            for k in range(sources)
        ],
        axis=0,
    ).astype(BF16)
    lane = iota((128, 128), 1)

    def add(j, weights, total):
        rows = jnp.concatenate(weights, axis=1)
        return jnp.where(lane == j, jnp.dot(rows, wanted, preferred_element_type=F32), total)

    total = jnp.zeros((128, 128), F32)
    before, after = sides(odd_ref, within_weight_ref[...], across_weight_ref[...])
    for n, weights in enumerate((before[0], before[1], after[0], after[1])):
        total = add(blocks + n, [weights[k] for k in range(sources)], total)
    step = blocks // PARTS
    for i, c in enumerate(copies):
        c.wait()
        for j in range(i * step, (i + 1) * step):
            total = add(j, [held[j, k] for k in range(sources)], total)
    by_block[...] = jnp.transpose(total)

    half = blocks // 2
    temp = jnp.concatenate([by_block[pl.ds(h, half, stride=2), :] for h in range(2)], axis=1)
    coupled_ref[0:half, :] = temp
    exchange = EXCHANGE_RATE * sea_ref[...].astype(F32)
    upper = with_edges(rows_ref[0], edges_ref[0])
    lower = with_edges(rows_ref[1], edges_ref[1])
    heat, moist = exchange * (temp - upper), exchange * (0.5 * temp - lower)
    upper = (upper + heat).astype(BF16).astype(F32)
    lower = (lower + moist).astype(BF16).astype(F32)
    coupled_ref[half : 2 * half, :] = upper
    coupled_ref[2 * half : 3 * half, :] = lower
    halo = []
    for n, (edge, pack) in enumerate(((0, left_pack), (3, right_pack))):
        at = blocks + 2 * n
        warm = jnp.concatenate([by_block[at : at + 1, :], by_block[at + 1 : at + 2, :]], axis=1)
        rate = EXCHANGE_RATE * jnp.concatenate([pack[0:1], pack[1:2]], axis=1)
        u, w = edges_ref[0, edge : edge + 1, :], edges_ref[1, edge : edge + 1, :]
        halo.append((u + rate * (warm - u)).astype(BF16).astype(F32))
        halo.append((w + rate * (0.5 * warm - w)).astype(BF16).astype(F32))
    coupled_ref[3 * half :, :] = jnp.zeros_like(coupled_ref[3 * half :, :])
    for n, line in enumerate(halo):
        coupled_ref[3 * half + n : 3 * half + n + 1, :] = line

    height = vertical_ref.shape[0]
    top, low = height // 2 - 1, height - 1
    cells, width = sea_ref.shape
    sub, lane = iota((cells, width), 0), iota((cells, width), 1)

    def row_of(r, mix, upper, lower):
        a = vertical_ref[pl.ds(r - 7, 8), :].astype(F32)[7:8]
        kept = mix.astype(BF16).astype(F32)
        return (kept + a[:, top : top + 1] * upper + a[:, low : low + 1] * lower).astype(BF16).astype(F32)

    def updated(r, n):
        edges = edges_ref[n]
        center = row_of(r, with_edges(rows_ref[n], edges), upper, lower)
        left = row_of(r, edges[0:1], halo[0], halo[1])
        right = row_of(r, edges[3:4], halo[2], halo[3])
        west = jnp.where(sub == 0, left, pltpu.roll(center, 1, 0))
        east = jnp.where(sub == cells - 1, right, pltpu.roll(center, cells - 1, 0))
        north = jnp.where(lane == width - 1, center, pltpu.roll(center, width - 1, 1))
        south = jnp.where(lane == 0, center, pltpu.roll(center, 1, 1))
        near = east + west + (north + south) - 4.0 * center
        courant = courant_ref[pl.ds(r - 7, 8), :][7:8]
        return center - courant * (center - west) + ATM_DIFFUSION * near

    heat = 0.5 * heat + 0.5 * (exchange * (temp - updated(top, 2)))
    moist = 0.5 * moist + 0.5 * (
        exchange * (0.5 * temp - updated(low, 3))
    )
    flux_rows[...] = jnp.zeros_like(flux_rows)
    for v, flux in enumerate((heat, moist)):
        for h in range(2):
            flux_rows[pl.ds(h * 10 + v, cells, stride=16), :] = flux[:, h * 128 : (h + 1) * 128]
    for x in range(half):
        rows = jnp.concatenate(
            [flux_rows[(2 * x + h) * 8 : (2 * x + h + 1) * 8, :] for h in range(2)], axis=1
        ).astype(BF16)
        weights = jnp.concatenate(
            [
                jnp.concatenate([held[2 * x + h, k] for k in range(sources)], axis=1)
                for h in range(2)
            ],
            axis=0,
        )
        got = jnp.dot(rows, weights, preferred_element_type=F32)
        for k in range(sources):
            at = (k * half + x) * 8
            shares[at : at + 8, :] = got[:, k * 128 : (k + 1) * 128]

    pairs = blocks * sources
    place = place_ref[0:1, :]
    rows = iota((out_ref.shape[0], pairs), 0)
    total = jnp.zeros(out_ref.shape, F32)
    for v in range(2):
        pick = (rows == place + 4 * v).astype(F32).astype(BF16)
        share = jnp.concatenate(
            [shares[pl.ds(2 * h + v, pairs // 2, stride=8), :] for h in range(2)], axis=0
        ).astype(BF16)
        total += jnp.dot(pick, share, preferred_element_type=F32)
    out_ref[...] = total.astype(BF16)


def second_step_kernel(
    mixed_hbm, edge_hbm, courant_ref, vertical_ref, sea_ref, coupled_ref,
    out_hbm, mixed_ref, edge_ref, state, result, out_ref, in_sems, edge_sem, out_sems,
):
    edge_copy = pltpu.make_async_copy(edge_hbm, edge_ref, edge_sem)
    edge_copy.start()
    coming = start_all(groups(mixed_hbm, mixed_ref, in_sems))
    cells, height = mixed_ref.shape[0], mixed_ref.shape[1]
    top, low = height // 2 - 1, height - 1
    lateral = lateral_matrix(mixed_ref.shape[2])
    vertical = vertical_ref[...]
    upper_column = vertical[:, top : top + 1].astype(F32)
    lower_column = vertical[:, low : low + 1].astype(F32)
    courant = courant_ref[...]

    def complete(mixed, upper, lower):
        return (mixed.astype(F32) + upper_column * upper + lower_column * lower).astype(BF16)

    halo_ref = coupled_ref.at[3 * cells :]
    upper_forced_ref = coupled_ref.at[cells : 2 * cells]
    lower_forced_ref = coupled_ref.at[2 * cells : 3 * cells]
    edge_copy.wait()
    state[0] = complete(edge_ref[0], halo_ref[0:1, :], halo_ref[1:2, :])
    state[1] = complete(edge_ref[1], upper_forced_ref[0:1, :], lower_forced_ref[0:1, :])
    state[cells] = complete(
        edge_ref[2], upper_forced_ref[cells - 1 : cells, :], lower_forced_ref[cells - 1 : cells, :]
    )
    state[cells + 1] = complete(edge_ref[3], halo_ref[2:3, :], halo_ref[3:4, :])

    for g, c in enumerate(coming):
        c.wait()
        for x in range(max(1, g * GROUP), min(cells - 1, (g + 1) * GROUP)):
            state[x + 1] = complete(
                mixed_ref[x], upper_forced_ref[x : x + 1, :], lower_forced_ref[x : x + 1, :]
            )

    last = iota((8, mixed_ref.shape[2]), 0) == 7

    @pl.loop(0, cells, unroll=GROUP)
    def _(x):
        updated = stencil(state[x], state[x + 1], state[x + 2], lateral, courant)
        exchange = EXCHANGE_RATE * sea_ref[pl.ds(x, 1), :].astype(F32)
        temp = coupled_ref[pl.ds(x, 1), :]
        upper = updated[top - 7 : top + 1]
        lower = updated[low - 7 : low + 1]
        upper = jnp.where(last, upper + exchange * (temp - upper), upper)
        lower = jnp.where(last, lower + exchange * (0.5 * temp - lower), lower)
        forced = jnp.concatenate(
            [updated[: top - 7], upper, updated[top + 1 : low - 7], lower], axis=0
        ).astype(BF16)
        result[x] = jnp.dot(vertical, forced, preferred_element_type=F32).astype(BF16)

    step = 32
    going = []
    for i in range(height // step):
        at = pl.ds(i * step, step)
        out_ref[at] = jnp.swapaxes(result[:, i * step : (i + 1) * step, :], 0, 1)
        going.append(pltpu.make_async_copy(out_ref.at[at], out_hbm.at[at], out_sems.at[i]))
        going[-1].start()
    wait_all(going)


def land_kernel(incoming_ref, slots_ref, sea_ref, out_ref, wide):
    devices = slots_ref.shape[1]
    cells = sea_ref.shape[0]
    wide[...] = incoming_ref[...].astype(F32)
    wet = sea_ref[...].astype(F32)
    here = (iota((cells, devices), 0) + 1).astype(F32)
    picks = [(slots_ref[s : s + 1, :] == here).astype(F32).astype(BF16) for s in range(4)]
    for v in range(2):
        total = jnp.zeros((cells, 128), F32)
        for s in range(4):
            part = wide[pl.ds(v * 4 + s, devices, stride=8), :].astype(BF16)
            total += jnp.dot(picks[s], part, preferred_element_type=F32)
        out_ref[v] = total * wet


def swap(within, across):
    peers = lax.axis_size(BOTH)
    pair = [(i, i ^ 1) for i in range(peers)]
    other = [(i, ((i + 1) ^ 1) - 1) for i in range(peers)]
    other = [(i, j % peers) for i, j in other]
    return lax.ppermute(within, BOTH, pair), lax.ppermute(across, BOTH, other)


def per_device(
    atm_state, atm_sea, zonal_courant, atm_vertical, ocean_state, ocean_sea,
    flux_in, ocean_vertical, remap_owner, remap_block, remap_weight,
):
    devices = lax.axis_size(BOTH)
    height, cells, width = atm_state.shape
    blocks, sources = remap_owner.shape
    pairs = blocks * sources
    courant = zonal_courant.reshape(height, 1)
    layers, ocean_cells, ocean_width = ocean_state.shape
    ocean_rows = ocean_state.reshape(layers * ocean_cells, ocean_width)
    owner, block = remap_owner.T, remap_block.T
    odd = is_odd()
    dma = pltpu.SemaphoreType.DMA
    held = [pltpu.VMEM(remap_weight.shape, BF16), dma((PARTS,))]
    whole = pltpu.VMEM((cells, height, width), BF16)
    levels = 64

    head, place = call(
        plan_kernel,
        (shape((devices, HEAD, 128), BF16), shape((8, pairs), jnp.int32)),
        owner, block, ocean_state,
        specs={0: ANY, 1: ANY, 2: ANY},
        scratch=[
            pltpu.VMEM((devices * 8, 128), F32),
            pltpu.VMEM((pairs, 128), F32),
            pltpu.VMEM(owner.shape, jnp.int32),
            pltpu.VMEM(owner.shape, jnp.int32),
            pltpu.VMEM((ocean_cells, ocean_width), F32),
            dma((3,)),
        ],
        limit=58,
        touched=1 << 20,
    )
    gathered = lax.all_to_all(head, BOTH, split_axis=0, concat_axis=0, tiled=True)

    pair_of_columns = shape((2, height, width), BF16)
    pair_of_blocks = shape((2, *remap_weight.shape[1:]), BF16)
    pack = shape((layers + 16, ocean_width), F32)
    state_a, state_b, weight_a, weight_b, pack_a, pack_b = call(
        edges_kernel,
        (pair_of_columns, pair_of_columns, pair_of_blocks, pair_of_blocks, pack, pack),
        odd, atm_state, ocean_state, remap_weight, owner, block, atm_sea,
        specs={
            0: SCALAR,
            1: pl.BlockSpec((levels, cells, width), lambda i: (i, 0, 0)),
            2: ANY,
            3: ANY,
        },
        out_specs={2: ANY, 3: ANY},
        scratch=[pltpu.VMEM((layers, ocean_width), F32)] * 2 + [dma((4,))],
        grid=(height // levels,),
        limit=54,
        touched=6 << 20,
    )
    state_near = swap(state_a, state_b)
    pack_near = swap(pack_a, pack_b)
    weight_near = swap(weight_a, weight_b)
    mixed, rows = call(
        first_step_kernel,
        (shape((cells, height, width), BF16), shape((4, cells, width), F32)),
        atm_state, courant, atm_vertical,
        specs={0: ANY},
        out_specs={0: ANY},
        scratch=[
            pltpu.VMEM(atm_state.shape, BF16), whole, whole,
            dma((LEVEL_PARTS,)), dma((cells // GROUP,)),
        ],
        touched=16 << 20,
    )
    mixed_edge, edge_rows = call(
        first_edges_kernel,
        (shape((4, height, width), BF16), shape((4, 8, width), F32)),
        odd, *state_near, state_a, state_b, courant, atm_vertical, *pack_near,
        specs={0: SCALAR},
        out_specs={0: ANY},
        scratch=[pltpu.VMEM((4, height, width), BF16), dma],
        limit=50,
        touched=2 << 20,
    )

    coupled, slots, outgoing = call(
        couple_kernel,
        (
            shape((3 * cells + 8, width), F32),
            shape((8, devices), F32),
            shape((devices * 8, 128), BF16),
        ),
        odd, gathered, pack_a, *pack_near, remap_weight, *weight_near, atm_sea, place,
        rows, edge_rows, courant, atm_vertical,
        specs={0: SCALAR, 5: ANY},
        scratch=[
            pltpu.VMEM((devices * 8, 128), F32),
            pltpu.VMEM((128, 128), F32),
            pltpu.VMEM((blocks * 8, 128), F32),
            pltpu.VMEM((pairs * 4, 128), F32),
            *held,
        ],
        limit=50,
        touched=16 << 20,
    )
    incoming = lax.all_to_all(
        outgoing.reshape(devices, 8, 128), BOTH, split_axis=0, concat_axis=0, tiled=True
    )
    state = call(
        second_step_kernel,
        shape(atm_state.shape, BF16),
        mixed, mixed_edge, courant, atm_vertical, atm_sea, coupled,
        specs={0: ANY, 1: ANY},
        out_specs={0: ANY},
        scratch=[
            whole,
            pltpu.VMEM((4, height, width), BF16),
            pltpu.VMEM((cells + 2, height, width), BF16),
            whole,
            pltpu.VMEM(atm_state.shape, BF16),
            dma((cells // GROUP,)),
            dma,
            dma((height // 32,)),
        ],
        touched=24 << 20,
    )
    new_ocean = call(
        ocean_kernel,
        shape(ocean_rows.shape, F32),
        odd, ocean_rows, *pack_near, ocean_sea, flux_in, ocean_vertical,
        specs={0: SCALAR, 1: ANY},
        out_specs={0: ANY},
        scratch=[pltpu.VMEM(ocean_rows.shape, F32), pltpu.VMEM(ocean_rows.shape, F32), dma],
        limit=53,
        touched=8 << 20,
    )
    ocean_flux = call(
        land_kernel,
        shape((2, ocean_cells, ocean_width), F32),
        incoming.reshape(devices * 8, 128), slots, ocean_sea,
        scratch=[pltpu.VMEM((devices * 8, 128), F32)],
        touched=1 << 20,
    )
    return state, new_ocean.reshape(ocean_state.shape), ocean_flux


def solution(mesh):
    return jax.shard_map(
        per_device,
        mesh=mesh,
        in_specs=(
            P(None, BOTH, None), P(BOTH, None), P(), P(), P(None, BOTH, None), P(BOTH, None),
            P(None, BOTH, None), P(), P(BOTH, None), P(BOTH, None), P(BOTH, None, None, None),
        ),
        out_specs=(P(None, BOTH, None), P(None, BOTH, None), P(None, BOTH, None)),
        check_vma=False,
    )
```

time: 80.1 us -> 86 us (1.074)
  Pallas kernels: 39.4 us -> 51.2 us
  starting transfers between devices: 34.1 us -> 31.3 us
  waiting for transfers between devices: 3.09 us -> 1.16 us
  local copies, waits for them, and re-layouts: 2.25 us -> 1.06 us
    pallas_call x9 -> x8, Pallas kernels: 39.4 us -> 51.2 us  [call(): pl.pallas_call(kernel, out_shape=outs, grid=grid, in_specs=[specs.get(i,...]
    squeeze x3 -> x0, local copies, waits for them, and re-layouts: 2.06 us -> none  [the longest x1 1.12 us: per_device(): near = swap(send[0], send[1])]
    all_to_all x1, starting transfers between devices: 11.1 us -> 9.16 us  [per_device(): lax.all_to_all(outgoing.reshape(devices, 8, 128), BOTH, split_axis=0, con...]
    ppermute x6, waiting for transfers between devices: 3.08 us -> 1.16 us  [swap(): return (lax.ppermute(within, BOTH, pair), lax.ppermute(across, BOTH, other))]
    unnamed x22 -> x20, local copies, waits for them, and re-layouts: 0.06 us -> 0.93 us
  transfers between devices with their start and end apart: 8 -> 8, of which waited for: 2 -> 1; matrix products, arithmetic and copies ran while one was open for 3% -> 0% of each run, Pallas kernels for 32% -> 47%
where the time goes in v2:
time: 86 us; the launch traced here: 85.6 us
  Pallas kernels  51.2 us (60%)
  starting transfers between devices  31.3 us (36%)
  waiting for transfers between devices  1.16 us (1%)
  local copies, waits for them, and re-layouts  1.06 us (1%)
  between operations  0.89 us (1%)
    pallas_call x8, Pallas kernels, call(): pl.pallas_call(kernel, out_shape=outs, grid=grid, in_specs=[specs.get(i,...  51.2 us
    all_to_all x1, starting transfers between devices, per_device(): lax.all_to_all(head, BOTH, split_axis=0, concat_axis=0, tiled=True)  11.5 us
    ppermute x6, starting transfers between devices, swap(): return (lax.ppermute(within, BOTH, pair), lax.ppermute(across, BOTH, other))  10.7 us
    all_to_all x1, starting transfers between devices, per_device(): lax.all_to_all(outgoing.reshape(devices, 8, 128), BOTH, split_axis=0, con...  9.16 us
  transfers between devices with their start and end apart: 8, of which 1 were waited for; matrix products, arithmetic and copies ran while one was open for 0% of the time, Pallas kernels for 47%

profile of v2, /device:TPU:1, one launch (start us, length us, event | category | flops | bytes accessed | tf_op | source)
XLA Modules:
  0.0 85.6 jit_solution(8427813382586197255)
XLA Ops:
  0.6 2.2 %shard_map.133 = (bf16[128,24,128]{2,1,0:T(8,128)(2,1)}, s32[8,256]{1,0:T(8,128)}) custom-call(s32[4,64]{1,0:T(4,128)} %bitcast.11, s32[4,64]{1,0:T(4,128)} %bitcast.13, f32[160,16,128]{2,1,0:T(8,128)} %ocean_hbm.3), custom_call_target="tpu_custom_call" | custom-call | bytes 1048576 | tf_op jit(solution)/shard_map/pallas_call | solution.py:28
  2.9 11.5 %all-to-all-start = ((bf16[128,24,128]{2,1,0:T(8,128)(2,1)}), bf16[128,24,128]{2,1,0:T(8,128)(2,1)S(1)}, u32[]{:S(2)}, u32[]{:S(2)}) async-start(bf16[128,24,128]{2,1,0:T(8,128)(2,1)} %get-tuple-element.24), calls=%async_computation | async-start | bytes 1572864 | tf_op jit(solution)/shard_map/all_to_all | solution.py:588
  14.4 0.0 copy-start.9
  14.4 0.0 copy-start
  14.4 19.2 %shard_map.131 = (bf16[2,256,256]{2,1,0:T(8,128)(2,1)}, bf16[2,256,256]{2,1,0:T(8,128)(2,1)}, bf16[2,4,128,128]{3,2,1,0:T(8,128)(2,1)}, bf16[2,4,128,128]{3,2,1,...) custom-call(s32[1]{0:T(128)} %bitcast.1.odd_ref, bf16[256,32,256]{2,1,0:T(8,128)(2,1)} %state_ref.1, ...), custom_call_target="tpu_custom_call" | custom-call | bytes 6291456 | tf_op jit(solution)/shard_map/pallas_call | solution.py:28
  33.6 0.0 copy-start.2
  33.6 0.0 copy-start.3
  33.6 0.0 copy-start.1
  33.6 0.0 copy-start.8
  33.6 1.1 %collective-permute-start = (bf16[2,256,256]{2,1,0:T(8,128)(2,1)}, bf16[2,256,256]{2,1,0:T(8,128)(2,1)S(1)}, u32[]{:S(2)}, u32[]{:S(2)}) collective-permute-start(bf16[2,256,256]{2,1,0:T(8,128)(2,1)} %get-tuple-element.19.own_a_ref), channel_id=1, source_target_pairs={{0,1},{1,0},{2,3},{3,2},{4,5},{5,4},{6,7},{7,6},{8,9},{9,8},{10,11... | collective-permute-start | bytes 786440 | tf_op jit(solution)/shard_map/ppermute | solution.py:551
  34.8 0.7 collective-permute-start.1
  35.5 6.7 %collective-permute-start.4 = (bf16[2,4,128,128]{3,2,1,0:T(8,128)(2,1)}, bf16[2,4,128,128]{3,2,1,0:T(8,128)(2,1)S(1)}, u32[]{:S(2)}, u32[]{:S(2)}) collective-permute-start(bf16[2,4,128,128]{3,2,1,0:T(8,128)(2,1)} %get-tuple-element.25), channel_id=1, source_target_pairs={{0,1},{1,0},{2,3},{3,2},{4,5},{5,4},{6,7},{7,6},{8,9},{9,8},{10,11... | collective-permute-start | bytes 786440 | tf_op jit(solution)/shard_map/ppermute | solution.py:551
  42.2 0.0 collective-permute-start.5
  42.2 0.9 %collective-permute-start.2 = (f32[176,128]{1,0:T(8,128)}, f32[176,128]{1,0:T(8,128)S(1)}, u32[]{:S(2)}, u32[]{:S(2)}) collective-permute-start(f32[176,128]{1,0:T(8,128)} %get-tuple-element.21.own_pack_ref), channel_id=1, source_target_pairs={{0,1},{1,0},{2,3},{3,2},{4,5},{5,4},{6,7},{7,6},{8,9},{9,8},{10,11... | collective-permute-start | bytes 270344 | tf_op jit(solution)/shard_map/ppermute | solution.py:551
  43.1 1.1 %collective-permute-done.2._.within_pack_ref.within_ref = f32[176,128]{1,0:T(8,128)S(1)} collective-permute-done((f32[176,128]{1,0:T(8,128)}, f32[176,128]{1,0:T(8,128)S(1)}, u32[]{:S(2)}, u32[]{:S(2)}) %collective-permute-start.2) | collective-permute-done | bytes 90144 | tf_op jit(solution)/shard_map/ppermute | solution.py:551
  44.2 1.2 %collective-permute-start.3 = (f32[176,128]{1,0:T(8,128)}, f32[176,128]{1,0:T(8,128)S(1)}, u32[]{:S(2)}, u32[]{:S(2)}) collective-permute-start(f32[176,128]{1,0:T(8,128)} %get-tuple-element.22), channel_id=1, source_target_pairs={{0,127},{1,2},{2,1},{3,4},{4,3},{5,6},{6,5},{7,8},{8,7},{9,10},{10... | collective-permute-start | bytes 270344 | tf_op jit(solution)/shard_map/ppermute | solution.py:551
  45.4 0.1 copy.14.courant_ref
  45.6 6.6 %shard_map.130 = (bf16[32,256,256]{2,1,0:T(8,128)(2,1)}, f32[4,32,256]{2,1,0:T(8,128)S(1)}) custom-call(bf16[256,32,256]{2,1,0:T(8,128)(2,1)} %state_ref.1, f32[256,1]{1,0:T(8,128)S(1)} %copy.14.courant_ref, bf16[256,256]{1,0:T(8,128)(2,1)S(1)} %copy-done), custom_call_target="tpu_custom_call" | custom-call | bytes 16777216 | tf_op jit(solution)/shard_map/pallas_call | solution.py:28
  52.2 0.0 collective-permute-done.3.__.across_pack_ref.across_ref
  52.2 0.0 collective-permute-done.within_ref
  52.2 0.0 collective-permute-done.1.across_ref
  52.2 0.8 shard_map.132
  53.0 0.0 collective-permute-done.4.within_weight_ref
  53.0 0.0 collective-permute-done.5.across_weight_ref
  53.0 0.0 all-to-all-done.head_ref
  53.1 0.9 %copy-done.5 = f32[176,128]{1,0:T(8,128)S(1)} copy-done((f32[176,128]{1,0:T(8,128)S(1)}, f32[176,128]{1,0:T(8,128)}, u32[]{:S(2)}) %copy-start.5) | copy-done | bytes 90136
  54.0 7.8 %shard_map.134 = (f32[104,256]{1,0:T(8,128)S(1)}, f32[8,128]{1,0:T(8,128)S(1)}, bf16[1024,128]{1,0:T(8,128)(2,1)}) custom-call(s32[1]{0:T(128)} %bitcast.1.odd_ref, bf16[128,24,128]{2,1,0:T(8,128)(2,1)S(1)} %all-to-all-done.head_ref, f32[176,128]{1,0:T(8,128)S(1)} %copy-done.5, f32[176,128]{1,0:T(8,128)S(1)} %collective-permute-done.2._.within_pack_ref.within_ref, ...), custom_call_target="tpu_custom_call" | custom-call | bytes 16777216 | tf_op jit(solution)/shard_map/pallas_call | solution.py:28
  61.8 9.2 %all-to-all-start.1 = ((bf16[128,8,128]{2,1,0:T(8,128)(2,1)}), bf16[128,8,128]{2,1,0:T(8,128)(2,1)S(1)}, u32[]{:S(2)}, u32[]{:S(2)}) async-start(bf16[128,8,128]{2,1,0:T(8,128)(2,1)} %bitcast.6), calls=%async_computation.1 | async-start | bytes 524288 | tf_op jit(solution)/shard_map/all_to_all | solution.py:655
  71.0 4.0 %shard_map.136 = f32[2560,128]{1,0:T(8,128)} custom-call(s32[1]{0:T(128)} %bitcast.1.odd_ref, f32[2560,128]{1,0:T(8,128)} %bitcast.9, f32[176,128]{1,0:T(8,128)S(1)} %collective-permute-done.2._.within_pack_ref.within_ref, f32[176,128]{1,0:T(8,128)S(1)} %collective-permute-done.3.__.across_pack_ref.across_ref, s32[16,128]{1,0:T(8,128)S(1)} %copy-done.6, ...), custom_call_target="tpu_custom_call" | custom-call | bytes 8388608 | tf_op jit(solution)/shard_map/pallas_call | solution.py:28
  75.0 9.7 %shard_map.135 = bf16[256,32,256]{2,1,0:T(8,128)(2,1)} custom-call(bf16[32,256,256]{2,1,0:T(8,128)(2,1)} %get-tuple-element.18.mixed_hbm, bf16[4,256,256]{2,1,0:T(8,128)(2,1)S(1)} %get-tuple-element.23.edge_hbm, f32[256,1]{1,0:T(8,128)S(1)} %copy.14.courant_ref, bf16[256,256]{1,0:T(8,128)(2,1)S(1)} %copy-done, s32[32,256]{1,0:T(8,128)S(1)} %copy-done.1, ...), custom_call_target="tpu_custom_call" | custom-call | bytes 25165824 | tf_op jit(solution)/shard_map/pallas_call | solution.py:28
  84.8 0.0 all-to-all-done.1
  84.8 0.8 shard_map.137
  (13 shorter events, 0.0 us)
Async XLA Ops:
  2.9 50.2 %all-to-all-start = ((bf16[128,24,128]{2,1,0:T(8,128)(2,1)}), bf16[128,24,128]{2,1,0:T(8,128)(2,1)S(1)}, u32[]{:S(2)}, u32[]{:S(2)}) async-start(bf16[128,24,128]{2,1,0:T(8,128)(2,1)} %get-tuple-element.24), calls=%async_computation | async-start | bytes 1572864 | tf_op jit(solution)/shard_map/all_to_all | solution.py:588
  14.4 31.1 %copy-start.9 = (f32[256]{0:T(256)S(1)}, f32[256]{0:T(256)}, u32[]{:S(2)}) copy-start(f32[256]{0:T(256)} %param.13) | copy-start | bytes 3076
  14.4 31.2 %copy-start = (bf16[256,256]{1,0:T(8,128)(2,1)S(1)}, bf16[256,256]{1,0:T(8,128)(2,1)}, u32[]{:S(2)}) copy-start(bf16[256,256]{1,0:T(8,128)(2,1)} %vertical_ref.8) | copy-start | bytes 393220
  33.6 18.6 %copy-start.2 = (bf16[2,256,256]{2,1,0:T(8,128)(2,1)S(1)}, bf16[2,256,256]{2,1,0:T(8,128)(2,1)}, u32[]{:S(2)}) copy-start(bf16[2,256,256]{2,1,0:T(8,128)(2,1)} %get-tuple-element.19.own_a_ref) | copy-start | bytes 786436
  33.6 18.6 %copy-start.3 = (bf16[2,256,256]{2,1,0:T(8,128)(2,1)S(1)}, bf16[2,256,256]{2,1,0:T(8,128)(2,1)}, u32[]{:S(2)}) copy-start(bf16[2,256,256]{2,1,0:T(8,128)(2,1)} %get-tuple-element.20.own_b_ref) | copy-start | bytes 786436
  33.6 19.4 %copy-start.1 = (s32[32,256]{1,0:T(8,128)S(1)}, s32[32,256]{1,0:T(8,128)}, u32[]{:S(2)}) copy-start(s32[32,256]{1,0:T(8,128)} %sea_ref.7) | copy-start | bytes 98308
  33.6 19.4 %copy-start.8 = (s32[8,256]{1,0:T(8,128)S(1)}, s32[8,256]{1,0:T(8,128)}, u32[]{:S(2)}) copy-start(s32[8,256]{1,0:T(8,128)} %get-tuple-element.27.place_ref) | copy-start | bytes 24580
  33.6 18.5 %collective-permute-start = (bf16[2,256,256]{2,1,0:T(8,128)(2,1)}, bf16[2,256,256]{2,1,0:T(8,128)(2,1)S(1)}, u32[]{:S(2)}, u32[]{:S(2)}) collective-permute-start(bf16[2,256,256]{2,1,0:T(8,128)(2,1)} %get-tuple-element.19.own_a_ref), channel_id=1, source_target_pairs={{0,1},{1,0},{2,3},{3,2},{4,5},{5,4},{6,7},{7,6},{8,9},{9,8},{10,11... | collective-permute-start | bytes 786440 | tf_op jit(solution)/shard_map/ppermute | solution.py:551
  34.8 17.4 %collective-permute-start.1 = (bf16[2,256,256]{2,1,0:T(8,128)(2,1)}, bf16[2,256,256]{2,1,0:T(8,128)(2,1)S(1)}, u32[]{:S(2)}, u32[]{:S(2)}) collective-permute-start(bf16[2,256,256]{2,1,0:T(8,128)(2,1)} %get-tuple-element.20.own_b_ref), channel_id=1, source_target_pairs={{0,127},{1,2},{2,1},{3,4},{4,3},{5,6},{6,5},{7,8},{8,7},{9,10},{10... | collective-permute-start | bytes 786440 | tf_op jit(solution)/shard_map/ppermute | solution.py:551
  35.5 17.5 %collective-permute-start.4 = (bf16[2,4,128,128]{3,2,1,0:T(8,128)(2,1)}, bf16[2,4,128,128]{3,2,1,0:T(8,128)(2,1)S(1)}, u32[]{:S(2)}, u32[]{:S(2)}) collective-permute-start(bf16[2,4,128,128]{3,2,1,0:T(8,128)(2,1)} %get-tuple-element.25), channel_id=1, source_target_pairs={{0,1},{1,0},{2,3},{3,2},{4,5},{5,4},{6,7},{7,6},{8,9},{9,8},{10,11... | collective-permute-start | bytes 786440 | tf_op jit(solution)/shard_map/ppermute | solution.py:551
  42.2 10.8 %collective-permute-start.5 = (bf16[2,4,128,128]{3,2,1,0:T(8,128)(2,1)}, bf16[2,4,128,128]{3,2,1,0:T(8,128)(2,1)S(1)}, u32[]{:S(2)}, u32[]{:S(2)}) collective-permute-start(bf16[2,4,128,128]{3,2,1,0:T(8,128)(2,1)} %get-tuple-element.26), channel_id=1, source_target_pairs={{0,127},{1,2},{2,1},{3,4},{4,3},{5,6},{6,5},{7,8},{8,7},{9,10},{10... | collective-permute-start | bytes 786440 | tf_op jit(solution)/shard_map/ppermute | solution.py:551
  42.2 2.0 %collective-permute-start.2 = (f32[176,128]{1,0:T(8,128)}, f32[176,128]{1,0:T(8,128)S(1)}, u32[]{:S(2)}, u32[]{:S(2)}) collective-permute-start(f32[176,128]{1,0:T(8,128)} %get-tuple-element.21.own_pack_ref), channel_id=1, source_target_pairs={{0,1},{1,0},{2,3},{3,2},{4,5},{5,4},{6,7},{7,6},{8,9},{9,8},{10,11... | collective-permute-start | bytes 270344 | tf_op jit(solution)/shard_map/ppermute | solution.py:551
  44.2 7.9 %collective-permute-start.3 = (f32[176,128]{1,0:T(8,128)}, f32[176,128]{1,0:T(8,128)S(1)}, u32[]{:S(2)}, u32[]{:S(2)}) collective-permute-start(f32[176,128]{1,0:T(8,128)} %get-tuple-element.22), channel_id=1, source_target_pairs={{0,127},{1,2},{2,1},{3,4},{4,3},{5,6},{6,5},{7,8},{8,7},{9,10},{10... | collective-permute-start | bytes 270344 | tf_op jit(solution)/shard_map/ppermute | solution.py:551
  53.1 0.9 %copy-start.5 = (f32[176,128]{1,0:T(8,128)S(1)}, f32[176,128]{1,0:T(8,128)}, u32[]{:S(2)}) copy-start(f32[176,128]{1,0:T(8,128)} %get-tuple-element.21.own_pack_ref) | copy-start | bytes 270340
  54.0 17.0 %copy-start.4 = (f32[160,160]{1,0:T(8,128)S(1)}, f32[160,160]{1,0:T(8,128)}, u32[]{:S(2)}) copy-start(f32[160,160]{1,0:T(8,128)} %vertical_ref.9) | copy-start | bytes 307204
  54.0 17.0 %copy-start.6 = (s32[16,128]{1,0:T(8,128)S(1)}, s32[16,128]{1,0:T(8,128)}, u32[]{:S(2)}) copy-start(s32[16,128]{1,0:T(8,128)} %sea_ref.9) | copy-start | bytes 24580
  54.0 17.0 %copy-start.7 = (f32[2,16,128]{2,1,0:T(8,128)S(1)}, f32[2,16,128]{2,1,0:T(8,128)}, u32[]{:S(2)}) copy-start(f32[2,16,128]{2,1,0:T(8,128)} %flux_ref.1) | copy-start | bytes 49156
  61.8 23.0 %all-to-all-start.1 = ((bf16[128,8,128]{2,1,0:T(8,128)(2,1)}), bf16[128,8,128]{2,1,0:T(8,128)(2,1)S(1)}, u32[]{:S(2)}, u32[]{:S(2)}) async-start(bf16[128,8,128]{2,1,0:T(8,128)(2,1)} %bitcast.6), calls=%async_computation.1 | async-start | bytes 524288 | tf_op jit(solution)/shard_map/all_to_all | solution.py:655

commit v3 on v2

--- a/solution.py
+++ b/solution.py
@@ -104,17 +104,21 @@
     head_ref[:, 16:24, :] = slot_rows[...].reshape(devices, 8, 128).astype(BF16)
 
 
+PACK = 192
+
+
 def edges_kernel(
     odd_ref, state_ref, ocean_hbm, weight_hbm, owner_ref, block_ref, sea_ref,
-    state_a_ref, state_b_ref, weight_a_hbm, weight_b_hbm, pack_a_ref, pack_b_ref,
+    state_a_ref, state_b_ref, load_a_ref, load_b_ref, goal_ref,
     ocean_first, ocean_last, sems,
 ):
     i, odd = pl.program_id(0), odd_ref[0]
-    blocks = weight_hbm.shape[0]
-    at_a = (1 - odd) * (blocks - 2)
+    tiles = 2 * owner_ref.shape[0]
+    at_a = (1 - odd) * (weight_hbm.shape[0] - tiles)
+    at_b = odd * (weight_hbm.shape[0] - tiles)
     copies = [
-        pltpu.make_async_copy(weight_hbm.at[pl.ds(at_a, 2)], weight_a_hbm, sems.at[0]),
-        pltpu.make_async_copy(weight_hbm.at[pl.ds(blocks - 2 - at_a, 2)], weight_b_hbm, sems.at[1]),
+        pltpu.make_async_copy(weight_hbm.at[pl.ds(at_a, tiles)], load_a_ref.at[0:tiles], sems.at[0]),
+        pltpu.make_async_copy(weight_hbm.at[pl.ds(at_b, tiles)], load_b_ref.at[0:tiles], sems.at[1]),
         pltpu.make_async_copy(ocean_hbm.at[:, 0], ocean_first, sems.at[2]),
         pltpu.make_async_copy(ocean_hbm.at[:, ocean_hbm.shape[1] - 1], ocean_last, sems.at[3]),
     ]
@@ -129,18 +133,28 @@
     def _():
         layers = ocean_first.shape[0]
         goal = (owner_ref[...] * 16 + block_ref[...]).astype(F32)
+        goal_ref[...] = jnp.zeros_like(goal_ref)
+        goal_ref[0 : goal.shape[0], 0 : goal.shape[1]] = goal
         sea = sea_ref[...].astype(F32)
         width = sea.shape[1] // 2
+        row = iota((8, width), 0)
         wait_all(copies)
-        ends = [ocean_first[...], ocean_last[...]], [sea[0:1], sea[cells - 1 : cells]]
-        for ref, ocean, line in zip(
-            (pack_a_ref, pack_b_ref), sides(odd_ref, *ends[0]), sides(odd_ref, *ends[1])
-        ):
-            ref[0:layers, :] = ocean
-            ref[layers:, :] = jnp.zeros_like(ref[layers:, :])
-            for h in range(2):
-                ref[layers + h : layers + h + 1, :] = line[:, h * width : (h + 1) * width]
-            ref[layers + 8 : layers + 8 + goal.shape[0], 0 : goal.shape[1]] = goal
+        oceans = sides(odd_ref, ocean_first[...], ocean_last[...])
+        lines = sides(odd_ref, sea[0:1], sea[cells - 1 : cells])
+        for ref, ocean, line in zip((load_a_ref, load_b_ref), oceans, lines):
+            halves = jnp.where(row == 0, line[:, :width], jnp.where(row == 1, line[:, width:], 0.0))
+            empty = jnp.zeros((PACK - layers - 16, width), F32)
+            pack = jnp.concatenate([ocean, halves, goal_ref[...], empty], axis=0)
+            high = pack.astype(BF16)
+            low = (pack - high.astype(F32)).astype(BF16)
+            ref[tiles:] = jnp.concatenate([high, low], axis=0).reshape(
+                2 * PACK // width, width, width
+            )
+
+
+def unpack(load):
+    both = load.reshape(2 * PACK, load.shape[2]).astype(F32)
+    return both[:PACK] + both[PACK:]
 
 
 def sides(odd_ref, within, across):
@@ -227,7 +241,7 @@
 
 
 def first_edges_kernel(
-    odd_ref, within_ref, across_ref, own_a_ref, own_b_ref, courant_ref, vertical_ref, _, __,
+    odd_ref, within_ref, across_ref, own_a_ref, own_b_ref, courant_ref, vertical_ref,
     mixed_hbm, rows_ref, mixed_out, sem,
 ):
     height = own_a_ref.shape[1]
@@ -255,23 +269,15 @@
     return jnp.where(at == 0, edges[1:2], jnp.where(at == cells - 1, edges[2:3], main))
 
 
-def ocean_kernel(
-    odd_ref, ocean_hbm, within_ref, across_ref, sea_ref, flux_ref, vertical_ref, out_hbm,
-    ocean_ref, out_ref, sem,
-):
-    copy = pltpu.make_async_copy(ocean_hbm, ocean_ref, sem)
-    copy.start()
+def ocean_step(ocean_ref, left, right, sea_ref, flux_ref, vertical_ref, out_ref):
     cells, width = sea_ref.shape
     height = ocean_ref.shape[0] // cells
     vertical = vertical_ref[...]
     high = vertical.astype(BF16)
     low = (vertical - high.astype(F32)).astype(BF16)
     both = jnp.concatenate([high, low], axis=0)
-    left, right = sides(odd_ref, within_ref[0:height, :], across_ref[0:height, :])
     lane = iota((height, width), 1)
     row = iota((height, width), 0)
-
-    copy.wait()
 
     def column(x):
         if x < 0:
@@ -303,9 +309,6 @@
         mixed += jnp.dot(high, rest, preferred_element_type=F32)
         out_ref[pl.ds(x - 1, height, stride=cells), :] = mixed[:, :width]
         out_ref[pl.ds(x, height, stride=cells), :] = mixed[:, width:]
-    copy = pltpu.make_async_copy(out_ref, out_hbm, sem)
-    copy.start()
-    copy.wait()
 
 
 PARTS = 8
@@ -322,8 +325,8 @@
 
 
 def couple_kernel(
-    odd_ref, head_ref, own_pack_ref, within_pack_ref, across_pack_ref,
-    weight_hbm, within_weight_ref, across_weight_ref, sea_ref, place_ref,
+    layers,
+    odd_ref, head_ref, goal_ref, within_ref, across_ref, weight_hbm, sea_ref, place_ref,
     rows_ref, edges_ref, courant_ref, vertical_ref, coupled_ref, slots_ref, out_ref,
     slot_rows, by_block, flux_rows, shares, held, sems,
 ):
@@ -334,14 +337,15 @@
     slot_rows[...] = head_ref[:, 16:24, :].astype(F32).reshape(devices * 8, 128)
     slots_ref[...] = jnp.transpose(slot_rows[pl.ds(0, devices, stride=8), :])[:8]
 
-    layers = own_pack_ref.shape[0] - 16
-    left_pack, right_pack = sides(
-        odd_ref, within_pack_ref[layers:, :], across_pack_ref[layers:, :]
+    tiles = 2 * sources
+    left_pack, right_pack = (
+        p[layers : layers + 16]
+        for p in sides(odd_ref, unpack(within_ref[tiles:]), unpack(across_ref[tiles:]))
     )
     lane = iota((8, 128), 1)
     goals = jnp.where(
         lane < blocks,
-        own_pack_ref[layers + 8 :, :],
+        goal_ref[...],
         jnp.where(
             lane < blocks + 2,
             pltpu.roll(left_pack[8:], 2, 1),
@@ -373,9 +377,11 @@
         return jnp.where(lane == j, jnp.dot(rows, wanted, preferred_element_type=F32), total)
 
     total = jnp.zeros((128, 128), F32)
-    before, after = sides(odd_ref, within_weight_ref[...], across_weight_ref[...])
-    for n, weights in enumerate((before[0], before[1], after[0], after[1])):
-        total = add(blocks + n, [weights[k] for k in range(sources)], total)
+    for n, weights in enumerate(sides(odd_ref, within_ref[0:tiles], across_ref[0:tiles])):
+        for b in range(2):
+            total = add(
+                blocks + 2 * n + b, [weights[b * sources + k] for k in range(sources)], total
+            )
     step = blocks // PARTS
     for i, c in enumerate(copies):
         c.wait()
@@ -467,12 +473,17 @@
 
 
 def second_step_kernel(
-    mixed_hbm, edge_hbm, courant_ref, vertical_ref, sea_ref, coupled_ref,
-    out_hbm, mixed_ref, edge_ref, state, result, out_ref, in_sems, edge_sem, out_sems,
+    tiles, odd_ref, mixed_hbm, edge_hbm, courant_ref, vertical_ref, sea_ref, coupled_ref,
+    ocean_hbm, within_ref, across_ref, ocean_sea_ref, flux_ref, ocean_vertical_ref,
+    out_hbm, new_ocean_hbm,
+    mixed_ref, edge_ref, state, result, out_ref, ocean_ref, new_ocean_ref,
+    in_sems, edge_sem, ocean_sems, out_sems,
 ):
     edge_copy = pltpu.make_async_copy(edge_hbm, edge_ref, edge_sem)
     edge_copy.start()
     coming = start_all(groups(mixed_hbm, mixed_ref, in_sems))
+    ocean_coming = pltpu.make_async_copy(ocean_hbm, ocean_ref, ocean_sems.at[0])
+    ocean_coming.start()
     cells, height = mixed_ref.shape[0], mixed_ref.shape[1]
     top, low = height // 2 - 1, height - 1
     lateral = lateral_matrix(mixed_ref.shape[2])
@@ -480,35 +491,20 @@
     upper_column = vertical[:, top : top + 1].astype(F32)
     lower_column = vertical[:, low : low + 1].astype(F32)
     courant = courant_ref[...]
-
-    def complete(mixed, upper, lower):
-        return (mixed.astype(F32) + upper_column * upper + lower_column * lower).astype(BF16)
-
-    halo_ref = coupled_ref.at[3 * cells :]
-    upper_forced_ref = coupled_ref.at[cells : 2 * cells]
-    lower_forced_ref = coupled_ref.at[2 * cells : 3 * cells]
-    edge_copy.wait()
-    state[0] = complete(edge_ref[0], halo_ref[0:1, :], halo_ref[1:2, :])
-    state[1] = complete(edge_ref[1], upper_forced_ref[0:1, :], lower_forced_ref[0:1, :])
-    state[cells] = complete(
-        edge_ref[2], upper_forced_ref[cells - 1 : cells, :], lower_forced_ref[cells - 1 : cells, :]
-    )
-    state[cells + 1] = complete(edge_ref[3], halo_ref[2:3, :], halo_ref[3:4, :])
-
-    for g, c in enumerate(coming):
-        c.wait()
-        for x in range(max(1, g * GROUP), min(cells - 1, (g + 1) * GROUP)):
-            state[x + 1] = complete(
-                mixed_ref[x], upper_forced_ref[x : x + 1, :], lower_forced_ref[x : x + 1, :]
-            )
+    halo = 3 * cells
+
+    def complete(to, mixed, upper_at, lower_at):
+        upper = coupled_ref[upper_at : upper_at + 1, :]
+        lower = coupled_ref[lower_at : lower_at + 1, :]
+        done = mixed.astype(F32) + upper_column * upper + lower_column * lower
+        state[to] = done.astype(BF16)
 
     last = iota((8, mixed_ref.shape[2]), 0) == 7
 
-    @pl.loop(0, cells, unroll=GROUP)
-    def _(x):
+    def advance(x):
         updated = stencil(state[x], state[x + 1], state[x + 2], lateral, courant)
-        exchange = EXCHANGE_RATE * sea_ref[pl.ds(x, 1), :].astype(F32)
-        temp = coupled_ref[pl.ds(x, 1), :]
+        exchange = EXCHANGE_RATE * sea_ref[x : x + 1, :].astype(F32)
+        temp = coupled_ref[x : x + 1, :]
         upper = updated[top - 7 : top + 1]
         lower = updated[low - 7 : low + 1]
         upper = jnp.where(last, upper + exchange * (temp - upper), upper)
@@ -518,12 +514,44 @@
         ).astype(BF16)
         result[x] = jnp.dot(vertical, forced, preferred_element_type=F32).astype(BF16)
 
-    step = 32
+    edge_copy.wait()
+    coming[0].wait()
+    complete(0, edge_ref[0], halo, halo + 1)
+    complete(1, edge_ref[1], cells, 2 * cells)
     going = []
-    for i in range(height // step):
-        at = pl.ds(i * step, step)
-        out_ref[at] = jnp.swapaxes(result[:, i * step : (i + 1) * step, :], 0, 1)
-        going.append(pltpu.make_async_copy(out_ref.at[at], out_hbm.at[at], out_sems.at[i]))
+    step, half = 32, cells // 2
+    for x in range(cells):
+        ahead = x + 1
+        if ahead % GROUP == 0 and ahead < cells:
+            coming[ahead // GROUP].wait()
+        if ahead < cells - 1:
+            complete(ahead + 1, mixed_ref[ahead], cells + ahead, 2 * cells + ahead)
+        elif ahead == cells - 1:
+            complete(cells, edge_ref[2], 2 * cells - 1, 3 * cells - 1)
+        else:
+            complete(cells + 1, edge_ref[3], halo + 2, halo + 3)
+        advance(x)
+        if (x + 1) % half:
+            continue
+        across = slice(x + 1 - half, x + 1)
+        for i in range(height // step):
+            at = slice(i * step, (i + 1) * step)
+            out_ref[at, across, :] = jnp.swapaxes(result[across, at, :], 0, 1)
+        ends = out_ref.at[:, across], out_hbm.at[:, across]
+        going.append(pltpu.make_async_copy(*ends, out_sems.at[(x + 1) // half - 1]))
+        going[-1].start()
+        if x + 1 == cells:
+            break
+        ocean_coming.wait()
+        layers = ocean_ref.shape[0] // ocean_sea_ref.shape[0]
+        left, right = (
+            p[:layers]
+            for p in sides(odd_ref, unpack(within_ref[tiles:]), unpack(across_ref[tiles:]))
+        )
+        ocean_step(
+            ocean_ref, left, right, ocean_sea_ref, flux_ref, ocean_vertical_ref, new_ocean_ref
+        )
+        going.append(pltpu.make_async_copy(new_ocean_ref, new_ocean_hbm, ocean_sems.at[1]))
         going[-1].start()
     wait_all(going)
 
@@ -587,28 +615,26 @@
     )
     gathered = lax.all_to_all(head, BOTH, split_axis=0, concat_axis=0, tiled=True)
 
-    pair_of_columns = shape((2, height, width), BF16)
-    pair_of_blocks = shape((2, *remap_weight.shape[1:]), BF16)
-    pack = shape((layers + 16, ocean_width), F32)
-    state_a, state_b, weight_a, weight_b, pack_a, pack_b = call(
+    tiles = 2 * sources
+    columns_sent = shape((2, height, width), BF16)
+    load = shape((tiles + 2 * PACK // 128, 128, 128), BF16)
+    state_a, state_b, load_a, load_b, goal = call(
         edges_kernel,
-        (pair_of_columns, pair_of_columns, pair_of_blocks, pair_of_blocks, pack, pack),
-        odd, atm_state, ocean_state, remap_weight, owner, block, atm_sea,
+        (columns_sent, columns_sent, load, load, shape((8, 128), F32)),
+        odd, atm_state, ocean_state, remap_weight.reshape(pairs, 128, 128), owner, block, atm_sea,
         specs={
             0: SCALAR,
             1: pl.BlockSpec((levels, cells, width), lambda i: (i, 0, 0)),
             2: ANY,
             3: ANY,
         },
-        out_specs={2: ANY, 3: ANY},
         scratch=[pltpu.VMEM((layers, ocean_width), F32)] * 2 + [dma((4,))],
         grid=(height // levels,),
         limit=54,
         touched=6 << 20,
     )
     state_near = swap(state_a, state_b)
-    pack_near = swap(pack_a, pack_b)
-    weight_near = swap(weight_a, weight_b)
+    load_near = swap(load_a, load_b)
     mixed, rows = call(
         first_step_kernel,
         (shape((cells, height, width), BF16), shape((4, cells, width), F32)),
@@ -624,7 +650,7 @@
     mixed_edge, edge_rows = call(
         first_edges_kernel,
         (shape((4, height, width), BF16), shape((4, 8, width), F32)),
-        odd, *state_near, state_a, state_b, courant, atm_vertical, *pack_near,
+        odd, *state_near, state_a, state_b, courant, atm_vertical,
         specs={0: SCALAR},
         out_specs={0: ANY},
         scratch=[pltpu.VMEM((4, height, width), BF16), dma],
@@ -633,13 +659,13 @@
     )
 
     coupled, slots, outgoing = call(
-        couple_kernel,
+        functools.partial(couple_kernel, layers),
         (
             shape((3 * cells + 8, width), F32),
             shape((8, devices), F32),
             shape((devices * 8, 128), BF16),
         ),
-        odd, gathered, pack_a, *pack_near, remap_weight, *weight_near, atm_sea, place,
+        odd, gathered, goal, *load_near, remap_weight, atm_sea, place,
         rows, edge_rows, courant, atm_vertical,
         specs={0: SCALAR, 5: ANY},
         scratch=[
@@ -655,33 +681,28 @@
     incoming = lax.all_to_all(
         outgoing.reshape(devices, 8, 128), BOTH, split_axis=0, concat_axis=0, tiled=True
     )
-    state = call(
-        second_step_kernel,
-        shape(atm_state.shape, BF16),
-        mixed, mixed_edge, courant, atm_vertical, atm_sea, coupled,
-        specs={0: ANY, 1: ANY},
-        out_specs={0: ANY},
+    state, new_ocean = call(
+        functools.partial(second_step_kernel, tiles),
+        (shape(atm_state.shape, BF16), shape(ocean_rows.shape, F32)),
+        odd, mixed, mixed_edge, courant, atm_vertical, atm_sea, coupled,
+        ocean_rows, *load_near, ocean_sea, flux_in, ocean_vertical,
+        specs={0: SCALAR, 1: ANY, 2: ANY, 7: ANY},
+        out_specs={0: ANY, 1: ANY},
         scratch=[
             whole,
             pltpu.VMEM((4, height, width), BF16),
             pltpu.VMEM((cells + 2, height, width), BF16),
             whole,
             pltpu.VMEM(atm_state.shape, BF16),
+            pltpu.VMEM(ocean_rows.shape, F32),
+            pltpu.VMEM(ocean_rows.shape, F32),
             dma((cells // GROUP,)),
             dma,
-            dma((height // 32,)),
+            dma((2,)),
+            dma((2,)),
         ],
+        limit=52,
         touched=24 << 20,
-    )
-    new_ocean = call(
-        ocean_kernel,
-        shape(ocean_rows.shape, F32),
-        odd, ocean_rows, *pack_near, ocean_sea, flux_in, ocean_vertical,
-        specs={0: SCALAR, 1: ANY},
-        out_specs={0: ANY},
-        scratch=[pltpu.VMEM(ocean_rows.shape, F32), pltpu.VMEM(ocean_rows.shape, F32), dma],
-        limit=53,
-        touched=8 << 20,
     )
     ocean_flux = call(
         land_kernel,

time: 86 us -> 64.6 us (0.75)
  Pallas kernels: 51.2 us -> 33 us
  starting transfers between devices: 31.3 us -> 29.5 us
  local copies, waits for them, and re-layouts: 1.06 us -> 0.19 us
    pallas_call x8 -> x7, Pallas kernels: 51.2 us -> 33 us  [call(): pl.pallas_call(kernel, out_shape=outs, grid=grid, in_specs=[specs.get(i,...]
    ppermute x6 -> x4, starting transfers between devices: 10.7 us -> 8.57 us  [swap(): return (lax.ppermute(within, BOTH, pair), lax.ppermute(across, BOTH, other))]
    ppermute x6 -> x4, waiting for transfers between devices: 1.16 us -> 0.01 us  [swap(): return (lax.ppermute(within, BOTH, pair), lax.ppermute(across, BOTH, other))]
    unnamed x20, local copies, waits for them, and re-layouts: 0.93 us -> 0.06 us
  transfers between devices with their start and end apart: 8 -> 6, of which waited for: 1 -> 1; matrix products, arithmetic and copies ran while one was open for 0% -> 0% of each run, Pallas kernels for 47% -> 34%
where the time goes in v3:
time: 64.6 us; the launch traced here: 64.3 us
  Pallas kernels  33 us (51%)
  starting transfers between devices  29.5 us (46%)
  between operations  0.9 us (1%)
  waiting for transfers between devices  0.72 us (1%)
    pallas_call x7, Pallas kernels, call(): pl.pallas_call(kernel, out_shape=outs, grid=grid, in_specs=[specs.get(i,...  33 us
    all_to_all x1, starting transfers between devices, per_device(): lax.all_to_all(head, BOTH, split_axis=0, concat_axis=0, tiled=True)  11.5 us
    all_to_all x1, starting transfers between devices, per_device(): lax.all_to_all(outgoing.reshape(devices, 8, 128), BOTH, split_axis=0, con...  9.42 us
    ppermute x4, starting transfers between devices, swap(): return (lax.ppermute(within, BOTH, pair), lax.ppermute(across, BOTH, other))  8.57 us
  transfers between devices with their start and end apart: 6, of which 1 were waited for; matrix products, arithmetic and copies ran while one was open for 0% of the time, Pallas kernels for 34%

profile of v3, /device:TPU:1, one launch (start us, length us, event | category | flops | bytes accessed | tf_op | source)
XLA Modules:
  0.0 64.3 jit_solution(16363430993780403073)
XLA Ops:
  0.6 2.2 %shard_map.133 = (bf16[128,24,128]{2,1,0:T(8,128)(2,1)}, s32[8,256]{1,0:T(8,128)}) custom-call(s32[4,64]{1,0:T(4,128)} %bitcast.12, s32[4,64]{1,0:T(4,128)} %bitcast.14, f32[160,16,128]{2,1,0:T(8,128)} %ocean_hbm.3), custom_call_target="tpu_custom_call" | custom-call | bytes 1048576 | tf_op jit(solution)/shard_map/pallas_call | solution.py:28
  2.9 11.5 %all-to-all-start = ((bf16[128,24,128]{2,1,0:T(8,128)(2,1)}), bf16[128,24,128]{2,1,0:T(8,128)(2,1)S(1)}, u32[]{:S(2)}, u32[]{:S(2)}) async-start(bf16[128,24,128]{2,1,0:T(8,128)(2,1)} %get-tuple-element.23), calls=%async_computation | async-start | bytes 1572864 | tf_op jit(solution)/shard_map/all_to_all | solution.py:616
  14.4 0.0 copy-start.9
  14.4 0.0 copy-start
  14.4 4.3 %shard_map.131 = (bf16[2,256,256]{2,1,0:T(8,128)(2,1)}, bf16[2,256,256]{2,1,0:T(8,128)(2,1)}, bf16[11,128,128]{2,1,0:T(8,128)(2,1)}, bf16[11,128,128]{2,1,0:T(8,128)(2,1)}, f32[8,128]{1,0:T(8,128)}) custom-call(s32[1]{0:T(128)} %bitcast.odd_ref, bf16[256,32,256]{2,1,0:T(8,128)(2,1)} %state_ref.1, f32[160,16,128]{2,1,0:T(8,128)} %ocean_hbm.3, ...), custom_call_target="tpu_custom_call" | custom-call | bytes 6291456 | tf_op jit(solution)/shard_map/pallas_call | solution.py:28
  18.7 0.0 copy-start.2
  18.8 0.0 copy-start.3
  18.8 0.0 copy-start.1
  18.8 0.0 copy-start.7
  18.8 0.0 copy-start.8
  18.8 1.1 %collective-permute-start.2 = (bf16[11,128,128]{2,1,0:T(8,128)(2,1)}, bf16[11,128,128]{2,1,0:T(8,128)(2,1)S(1)}, u32[]{:S(2)}, u32[]{:S(2)}) collective-permute-start(bf16[11,128,128]{2,1,0:T(8,128)(2,1)} %get-tuple-element.25), channel_id=1, source_target_pairs={{0,1},{1,0},{2,3},{3,2},{4,5},{5,4},{6,7},{7,6},{8,9},{9,8},{10,11... | collective-permute-start | bytes 1081352 | tf_op jit(solution)/shard_map/ppermute | solution.py:579
  19.9 0.7 %collective-permute-start.3 = (bf16[11,128,128]{2,1,0:T(8,128)(2,1)}, bf16[11,128,128]{2,1,0:T(8,128)(2,1)S(1)}, u32[]{:S(2)}, u32[]{:S(2)}) collective-permute-start(bf16[11,128,128]{2,1,0:T(8,128)(2,1)} %get-tuple-element.26), channel_id=1, source_target_pairs={{0,127},{1,2},{2,1},{3,4},{4,3},{5,6},{6,5},{7,8},{8,7},{9,10},{10... | collective-permute-start | bytes 1081352 | tf_op jit(solution)/shard_map/ppermute | solution.py:579
  20.7 6.7 %collective-permute-start = (bf16[2,256,256]{2,1,0:T(8,128)(2,1)}, bf16[2,256,256]{2,1,0:T(8,128)(2,1)S(1)}, u32[]{:S(2)}, u32[]{:S(2)}) collective-permute-start(bf16[2,256,256]{2,1,0:T(8,128)(2,1)} %get-tuple-element.20.own_a_ref), channel_id=1, source_target_pairs={{0,1},{1,0},{2,3},{3,2},{4,5},{5,4},{6,7},{7,6},{8,9},{9,8},{10,11... | collective-permute-start | bytes 786440 | tf_op jit(solution)/shard_map/ppermute | solution.py:579
  27.4 0.0 collective-permute-start.1
  27.4 0.1 copy.14.courant_ref
  27.5 6.5 %shard_map.130 = (bf16[32,256,256]{2,1,0:T(8,128)(2,1)}, f32[4,32,256]{2,1,0:T(8,128)S(1)}) custom-call(bf16[256,32,256]{2,1,0:T(8,128)(2,1)} %state_ref.1, f32[256,1]{1,0:T(8,128)S(1)} %copy.14.courant_ref, bf16[256,256]{1,0:T(8,128)(2,1)S(1)} %copy-done), custom_call_target="tpu_custom_call" | custom-call | bytes 16777216 | tf_op jit(solution)/shard_map/pallas_call | solution.py:28
  34.1 0.0 collective-permute-done.within_ref
  34.1 0.0 collective-permute-done.1.across_ref
  34.1 0.0 copy-done.2
  34.1 0.0 copy-done.3
  34.1 0.8 %shard_map.132 = (bf16[4,256,256]{2,1,0:T(8,128)(2,1)S(1)}, f32[4,8,256]{2,1,0:T(8,128)S(1)}) custom-call(s32[1]{0:T(128)} %bitcast.odd_ref, bf16[2,256,256]{2,1,0:T(8,128)(2,1)S(1)} %collective-permute-done.within_ref, bf16[2,256,256]{2,1,0:T(8,128)(2,1)S(1)} %collective-permute-done.1.across_ref, bf16[2,256,256]{2,1,0:T(8,128)(2,1)S(1)} %copy-done.2, ...), custom_call_target="tpu_custom_call" | custom-call | bytes 2097152 | tf_op jit(solution)/shard_map/pallas_call | solution.py:28
  34.9 0.0 collective-permute-done.2.within_ref
  34.9 0.0 collective-permute-done.3.across_ref
  34.9 0.0 all-to-all-done.head_ref
  35.0 0.0 copy-start.4
  35.0 0.0 copy-start.5
  35.0 0.0 copy-start.6
  35.0 7.8 %shard_map.134 = (f32[104,256]{1,0:T(8,128)S(1)}, f32[8,128]{1,0:T(8,128)S(1)}, bf16[1024,128]{1,0:T(8,128)(2,1)}) custom-call(s32[1]{0:T(128)} %bitcast.odd_ref, bf16[128,24,128]{2,1,0:T(8,128)(2,1)S(1)} %all-to-all-done.head_ref, f32[8,128]{1,0:T(8,128)S(1)} %copy-done.8, bf16[11,128,128]{2,1,0:T(8,128)(2,1)S(1)} %collective-permute-done.2.within_ref, ...), custom_call_target="tpu_custom_call" | custom-call | bytes 16777216 | tf_op jit(solution)/shard_map/pallas_call | solution.py:28
  42.8 9.4 %all-to-all-start.1 = ((bf16[128,8,128]{2,1,0:T(8,128)(2,1)}), bf16[128,8,128]{2,1,0:T(8,128)(2,1)S(1)}, u32[]{:S(2)}, u32[]{:S(2)}) async-start(bf16[128,8,128]{2,1,0:T(8,128)(2,1)} %bitcast.7), calls=%async_computation.1 | async-start | bytes 524288 | tf_op jit(solution)/shard_map/all_to_all | solution.py:681
  52.3 10.5 %shard_map.135 = (bf16[256,32,256]{2,1,0:T(8,128)(2,1)}, f32[2560,128]{1,0:T(8,128)}) custom-call(s32[1]{0:T(128)} %bitcast.odd_ref, bf16[32,256,256]{2,1,0:T(8,128)(2,1)} %get-tuple-element.19.mixed_hbm, bf16[4,256,256]{2,1,0:T(8,128)(2,1)S(1)} %get-tuple-element.22.edge_hbm, f32[256,1]{1,0:T(8,128)S(1)} %copy.14.courant_ref, bf16[256,256]{1,0:T(8,128)(2,1)S(1)} %copy-done, ...), custom_call_target="tpu_custom_call" | custom-call | bytes 25165824 | tf_op jit(solution)/shard_map/pallas_call | solution.py:28
  62.8 0.7 %all-to-all-done.1 = bf16[128,8,128]{2,1,0:T(8,128)(2,1)S(1)} async-done(((bf16[128,8,128]{2,1,0:T(8,128)(2,1)}), bf16[128,8,128]{2,1,0:T(8,128)(2,1)S(1)}, u32[]{:S(2)}, u32[]{:S(2)}) %all-to-all-start.1) | async-done | bytes 262176 | tf_op jit(solution)/shard_map/all_to_all | solution.py:681
  63.5 0.8 %shard_map.136 = f32[2,16,128]{2,1,0:T(8,128)} custom-call(bf16[1024,128]{1,0:T(8,128)(2,1)S(1)} %bitcast.9, f32[8,128]{1,0:T(8,128)S(1)} %get-tuple-element.34.slots_ref, s32[16,128]{1,0:T(8,128)S(1)} %copy-done.5), custom_call_target="tpu_custom_call" | custom-call | bytes 1048576 | tf_op jit(solution)/shard_map/pallas_call | solution.py:28
  (8 shorter events, 0.0 us)
Async XLA Ops:
  2.9 32.1 %all-to-all-start = ((bf16[128,24,128]{2,1,0:T(8,128)(2,1)}), bf16[128,24,128]{2,1,0:T(8,128)(2,1)S(1)}, u32[]{:S(2)}, u32[]{:S(2)}) async-start(bf16[128,24,128]{2,1,0:T(8,128)(2,1)} %get-tuple-element.23), calls=%async_computation | async-start | bytes 1572864 | tf_op jit(solution)/shard_map/all_to_all | solution.py:616
  14.4 13.0 %copy-start.9 = (f32[256]{0:T(256)S(1)}, f32[256]{0:T(256)}, u32[]{:S(2)}) copy-start(f32[256]{0:T(256)} %param.13) | copy-start | bytes 3076
  14.4 13.1 %copy-start = (bf16[256,256]{1,0:T(8,128)(2,1)S(1)}, bf16[256,256]{1,0:T(8,128)(2,1)}, u32[]{:S(2)}) copy-start(bf16[256,256]{1,0:T(8,128)(2,1)} %vertical_ref.7) | copy-start | bytes 393220
  18.7 15.4 %copy-start.2 = (bf16[2,256,256]{2,1,0:T(8,128)(2,1)S(1)}, bf16[2,256,256]{2,1,0:T(8,128)(2,1)}, u32[]{:S(2)}) copy-start(bf16[2,256,256]{2,1,0:T(8,128)(2,1)} %get-tuple-element.20.own_a_ref) | copy-start | bytes 786436
  18.8 15.4 %copy-start.3 = (bf16[2,256,256]{2,1,0:T(8,128)(2,1)S(1)}, bf16[2,256,256]{2,1,0:T(8,128)(2,1)}, u32[]{:S(2)}) copy-start(bf16[2,256,256]{2,1,0:T(8,128)(2,1)} %get-tuple-element.21.own_b_ref) | copy-start | bytes 786436
  18.8 16.2 %copy-start.1 = (s32[32,256]{1,0:T(8,128)S(1)}, s32[32,256]{1,0:T(8,128)}, u32[]{:S(2)}) copy-start(s32[32,256]{1,0:T(8,128)} %sea_ref.6) | copy-start | bytes 98308
  18.8 16.2 %copy-start.7 = (s32[8,256]{1,0:T(8,128)S(1)}, s32[8,256]{1,0:T(8,128)}, u32[]{:S(2)}) copy-start(s32[8,256]{1,0:T(8,128)} %get-tuple-element.27.place_ref) | copy-start | bytes 24580
  18.8 16.2 %copy-start.8 = (f32[8,128]{1,0:T(8,128)S(1)}, f32[8,128]{1,0:T(8,128)}, u32[]{:S(2)}) copy-start(f32[8,128]{1,0:T(8,128)} %get-tuple-element.24.goal_ref) | copy-start | bytes 12292
  18.8 16.1 %collective-permute-start.2 = (bf16[11,128,128]{2,1,0:T(8,128)(2,1)}, bf16[11,128,128]{2,1,0:T(8,128)(2,1)S(1)}, u32[]{:S(2)}, u32[]{:S(2)}) collective-permute-start(bf16[11,128,128]{2,1,0:T(8,128)(2,1)} %get-tuple-element.25), channel_id=1, source_target_pairs={{0,1},{1,0},{2,3},{3,2},{4,5},{5,4},{6,7},{7,6},{8,9},{9,8},{10,11... | collective-permute-start | bytes 1081352 | tf_op jit(solution)/shard_map/ppermute | solution.py:579
  19.9 15.0 %collective-permute-start.3 = (bf16[11,128,128]{2,1,0:T(8,128)(2,1)}, bf16[11,128,128]{2,1,0:T(8,128)(2,1)S(1)}, u32[]{:S(2)}, u32[]{:S(2)}) collective-permute-start(bf16[11,128,128]{2,1,0:T(8,128)(2,1)} %get-tuple-element.26), channel_id=1, source_target_pairs={{0,127},{1,2},{2,1},{3,4},{4,3},{5,6},{6,5},{7,8},{8,7},{9,10},{10... | collective-permute-start | bytes 1081352 | tf_op jit(solution)/shard_map/ppermute | solution.py:579
  20.7 13.4 %collective-permute-start = (bf16[2,256,256]{2,1,0:T(8,128)(2,1)}, bf16[2,256,256]{2,1,0:T(8,128)(2,1)S(1)}, u32[]{:S(2)}, u32[]{:S(2)}) collective-permute-start(bf16[2,256,256]{2,1,0:T(8,128)(2,1)} %get-tuple-element.20.own_a_ref), channel_id=1, source_target_pairs={{0,1},{1,0},{2,3},{3,2},{4,5},{5,4},{6,7},{7,6},{8,9},{9,8},{10,11... | collective-permute-start | bytes 786440 | tf_op jit(solution)/shard_map/ppermute | solution.py:579
  27.4 6.7 %collective-permute-start.1 = (bf16[2,256,256]{2,1,0:T(8,128)(2,1)}, bf16[2,256,256]{2,1,0:T(8,128)(2,1)S(1)}, u32[]{:S(2)}, u32[]{:S(2)}) collective-permute-start(bf16[2,256,256]{2,1,0:T(8,128)(2,1)} %get-tuple-element.21.own_b_ref), channel_id=1, source_target_pairs={{0,127},{1,2},{2,1},{3,4},{4,3},{5,6},{6,5},{7,8},{8,7},{9,10},{10... | collective-permute-start | bytes 786440 | tf_op jit(solution)/shard_map/ppermute | solution.py:579
  35.0 17.3 %copy-start.4 = (f32[160,160]{1,0:T(8,128)S(1)}, f32[160,160]{1,0:T(8,128)}, u32[]{:S(2)}) copy-start(f32[160,160]{1,0:T(8,128)} %ocean_vertical_ref.1) | copy-start | bytes 307204
  35.0 17.3 %copy-start.5 = (s32[16,128]{1,0:T(8,128)S(1)}, s32[16,128]{1,0:T(8,128)}, u32[]{:S(2)}) copy-start(s32[16,128]{1,0:T(8,128)} %sea_ref.7) | copy-start | bytes 24580
  35.0 17.3 %copy-start.6 = (f32[2,16,128]{2,1,0:T(8,128)S(1)}, f32[2,16,128]{2,1,0:T(8,128)}, u32[]{:S(2)}) copy-start(f32[2,16,128]{2,1,0:T(8,128)} %flux_ref.1) | copy-start | bytes 49156
  42.8 20.6 %all-to-all-start.1 = ((bf16[128,8,128]{2,1,0:T(8,128)(2,1)}), bf16[128,8,128]{2,1,0:T(8,128)(2,1)S(1)}, u32[]{:S(2)}, u32[]{:S(2)}) async-start(bf16[128,8,128]{2,1,0:T(8,128)(2,1)} %bitcast.7), calls=%async_computation.1 | async-start | bytes 524288 | tf_op jit(solution)/shard_map/all_to_all | solution.py:681

commit v4 on v3

--- a/solution.py
+++ b/solution.py
@@ -19,7 +19,7 @@
 HEAD = 24
 
 
-def call(kernel, outs, *args, scratch=(), specs=None, out_specs=None, limit=50, touched=0, grid=()):
+def call(kernel, outs, *args, scratch=(), specs=None, out_specs=None, limit=50, touched=0, grid=(), aliases=None):
     specs, out_specs = specs or {}, out_specs or {}
     single = not isinstance(outs, tuple)
     placed = [
@@ -32,6 +32,7 @@
         in_specs=[specs.get(i, pl.BlockSpec(memory_space=VM)) for i in range(len(args))],
         out_specs=placed[0] if single else tuple(placed),
         scratch_shapes=list(scratch),
+        input_output_aliases=aliases or {},
         compiler_params=pltpu.CompilerParams(vmem_limit_bytes=limit << 20),
         cost_estimate=pl.CostEstimate(flops=0, bytes_accessed=touched, transcendentals=0),
     )(*args)
@@ -204,7 +205,8 @@
 
 
 def first_step_kernel(
-    state_hbm, courant_ref, vertical_ref, mixed_hbm, rows_ref, state, turned, mixed_out, in_sems, out_sems,
+    state_hbm, courant_ref, vertical_ref, ocean_hbm, ocean_sea_ref, flux_ref, ocean_vertical_ref,
+    mixed_hbm, rows_ref, new_ocean_hbm, ocean_ref, new_ocean_ref, ocean_sems, state, turned, mixed_out, in_sems, out_sems,
 ):
     levels = state.shape[0] // LEVEL_PARTS
     coming = start_all([
@@ -213,6 +215,8 @@
         )
         for n in range(LEVEL_PARTS)
     ])
+    ocean_coming = pltpu.make_async_copy(ocean_hbm, ocean_ref, ocean_sems.at[0])
+    ocean_coming.start()
     going = groups(mixed_hbm, mixed_out, out_sems, out=True)
     cells, height = turned.shape[0], turned.shape[1]
     lateral = lateral_matrix(turned.shape[2])
@@ -237,30 +241,41 @@
         for x in range(max(1, g * GROUP), min(cells - 1, (g + 1) * GROUP)):
             body(x)
         going[g].start()
+        if (g + 1) * GROUP != cells // 2:
+            continue
+        ocean_coming.wait()
+        ocean_cells = ocean_sea_ref.shape[0]
+        layers = ocean_ref.shape[0] // ocean_cells
+
+        def column(x):
+            return pl.ds(x, layers, stride=ocean_cells), slice(None)
+
+        def store(x, value):
+            new_ocean_ref[column(x)] = value
+
+        for x in (0, ocean_cells - 1):
+            store(x, jnp.zeros((layers, ocean_ref.shape[1]), F32))
+        ocean_step(
+            [(x, x + 1) for x in range(1, ocean_cells - 1, 2)],
+            lambda x: ocean_ref[column(x)],
+            ocean_sea_ref, flux_ref, ocean_vertical_ref, store,
+        )
+        going.append(pltpu.make_async_copy(new_ocean_ref, new_ocean_hbm, ocean_sems.at[1]))
+        going[-1].start()
     wait_all(going)
 
 
-def first_edges_kernel(
-    odd_ref, within_ref, across_ref, own_a_ref, own_b_ref, courant_ref, vertical_ref,
-    mixed_hbm, rows_ref, mixed_out, sem,
-):
-    height = own_a_ref.shape[1]
-    lateral = lateral_matrix(own_a_ref.shape[2])
-    vertical = without_forced(vertical_ref[...])
-    courant = courant_ref[...]
-    left, right = sides(odd_ref, within_ref[...], across_ref[...])
-    first, last = sides(odd_ref, own_a_ref[...], own_b_ref[...])
-    rows_ref[...] = jnp.zeros_like(rows_ref)
+def edge_columns(left, right, first, last, courant, vertical, keep, mixed_out):
+    lateral = lateral_matrix(first.shape[2])
+    vertical = without_forced(vertical)
     before = [left[0], left[1], first[0], first[1]]
     after = [last[0], last[1], right[0], right[1]]
+    keep[...] = jnp.zeros_like(keep)
     for i, columns_of in enumerate((before[:3], before[1:], after[:3], after[1:])):
         updated = stencil(*columns_of, lateral, courant)
         mixed = jnp.dot(vertical, updated.astype(BF16), preferred_element_type=F32)
-        keep_rows(rows_ref, i, updated, mixed)
+        keep_rows(keep, i, updated, mixed)
         mixed_out[i] = mixed.astype(BF16)
-    copy = pltpu.make_async_copy(mixed_out, mixed_hbm, sem)
-    copy.start()
-    copy.wait()
 
 
 def with_edges(main, edges):
@@ -269,9 +284,9 @@
     return jnp.where(at == 0, edges[1:2], jnp.where(at == cells - 1, edges[2:3], main))
 
 
-def ocean_step(ocean_ref, left, right, sea_ref, flux_ref, vertical_ref, out_ref):
-    cells, width = sea_ref.shape
-    height = ocean_ref.shape[0] // cells
+def ocean_step(pairs, column, sea_ref, flux_ref, vertical_ref, store):
+    width = sea_ref.shape[1]
+    height = vertical_ref.shape[0]
     vertical = vertical_ref[...]
     high = vertical.astype(BF16)
     low = (vertical - high.astype(F32)).astype(BF16)
@@ -279,15 +294,7 @@
     lane = iota((height, width), 1)
     row = iota((height, width), 0)
 
-    def column(x):
-        if x < 0:
-            return left
-        if x >= cells:
-            return right
-        return ocean_ref[pl.ds(x, height, stride=cells), :]
-
-    parts = []
-    for x in range(cells):
+    def forced(x):
         west, center, east = column(x - 1), column(x), column(x + 1)
         north = jnp.where(lane == width - 1, center, pltpu.roll(center, width - 1, 1))
         south = jnp.where(lane == 0, center, pltpu.roll(center, 1, 1))
@@ -296,19 +303,17 @@
         heat = FLUX_GAIN * wet * flux_ref[0, x : x + 1, :]
         fresh = FLUX_GAIN * wet * flux_ref[1, x : x + 1, :]
         added = jnp.where(row == 0, heat, jnp.where(row == height // 2, fresh, 0.0))
-        updated = (center + OCEAN_DIFFUSION * near) * wet + added
+        return (center + OCEAN_DIFFUSION * near) * wet + added
+
+    for pair in pairs:
+        updated = jnp.concatenate([forced(x) for x in pair], axis=1)
         upper = updated.astype(BF16)
         rest = (updated - upper.astype(F32)).astype(BF16)
-        parts.append((upper, rest))
-        if x % 2 == 0:
-            continue
-        upper, rest = (jnp.concatenate(p, axis=1) for p in zip(*parts))
-        parts = []
         mixed = jnp.dot(both, upper, preferred_element_type=F32)
         mixed = mixed[:height] + mixed[height:]
         mixed += jnp.dot(high, rest, preferred_element_type=F32)
-        out_ref[pl.ds(x - 1, height, stride=cells), :] = mixed[:, :width]
-        out_ref[pl.ds(x, height, stride=cells), :] = mixed[:, width:]
+        for n, x in enumerate(pair):
+            store(x, mixed[:, n * width : (n + 1) * width])
 
 
 PARTS = 8
@@ -327,10 +332,18 @@
 def couple_kernel(
     layers,
     odd_ref, head_ref, goal_ref, within_ref, across_ref, weight_hbm, sea_ref, place_ref,
-    rows_ref, edges_ref, courant_ref, vertical_ref, coupled_ref, slots_ref, out_ref,
-    slot_rows, by_block, flux_rows, shares, held, sems,
+    rows_ref, near_within_ref, near_across_ref, own_a_ref, own_b_ref, courant_ref, vertical_ref,
+    coupled_ref, slots_ref, out_ref, mixed_hbm,
+    slot_rows, by_block, flux_rows, shares, edges_ref, mixed_out, mixed_sem, held, sems,
 ):
     copies = weight_copies(weight_hbm, held, sems)
+    edge_columns(
+        *sides(odd_ref, near_within_ref[...], near_across_ref[...]),
+        *sides(odd_ref, own_a_ref[...], own_b_ref[...]),
+        courant_ref[...], vertical_ref[...], edges_ref, mixed_out,
+    )
+    mixed_going = pltpu.make_async_copy(mixed_out, mixed_hbm, mixed_sem)
+    mixed_going.start()
     devices = head_ref.shape[0]
     blocks, sources = held.shape[0], held.shape[1]
     surface = head_ref[:, 0:16, :].reshape(devices * 16, 128)
@@ -470,11 +483,12 @@
         ).astype(BF16)
         total += jnp.dot(pick, share, preferred_element_type=F32)
     out_ref[...] = total.astype(BF16)
+    mixed_going.wait()
 
 
 def second_step_kernel(
     tiles, odd_ref, mixed_hbm, edge_hbm, courant_ref, vertical_ref, sea_ref, coupled_ref,
-    ocean_hbm, within_ref, across_ref, ocean_sea_ref, flux_ref, ocean_vertical_ref,
+    ocean_hbm, _, within_ref, across_ref, ocean_sea_ref, flux_ref, ocean_vertical_ref,
     out_hbm, new_ocean_hbm,
     mixed_ref, edge_ref, state, result, out_ref, ocean_ref, new_ocean_ref,
     in_sems, edge_sem, ocean_sems, out_sems,
@@ -482,8 +496,12 @@
     edge_copy = pltpu.make_async_copy(edge_hbm, edge_ref, edge_sem)
     edge_copy.start()
     coming = start_all(groups(mixed_hbm, mixed_ref, in_sems))
-    ocean_coming = pltpu.make_async_copy(ocean_hbm, ocean_ref, ocean_sems.at[0])
-    ocean_coming.start()
+    ocean_cells = ocean_sea_ref.shape[0]
+    near_ends = (0, 1, ocean_cells - 2, ocean_cells - 1)
+    ocean_coming = start_all([
+        pltpu.make_async_copy(ocean_hbm.at[:, x], ocean_ref.at[n], ocean_sems.at[n])
+        for n, x in enumerate(near_ends)
+    ])
     cells, height = mixed_ref.shape[0], mixed_ref.shape[1]
     top, low = height // 2 - 1, height - 1
     lateral = lateral_matrix(mixed_ref.shape[2])
@@ -542,17 +560,25 @@
         going[-1].start()
         if x + 1 == cells:
             break
-        ocean_coming.wait()
-        layers = ocean_ref.shape[0] // ocean_sea_ref.shape[0]
+        wait_all(ocean_coming)
+        layers = ocean_ref.shape[1]
         left, right = (
             p[:layers]
             for p in sides(odd_ref, unpack(within_ref[tiles:]), unpack(across_ref[tiles:]))
         )
+        known = {-1: left, ocean_cells: right}
+        known.update((at, ocean_ref[n]) for n, at in enumerate(near_ends))
+
+        def store(x, value):
+            new_ocean_ref[min(x, 1)] = value
+
         ocean_step(
-            ocean_ref, left, right, ocean_sea_ref, flux_ref, ocean_vertical_ref, new_ocean_ref
+            [(0, ocean_cells - 1)], known.get, ocean_sea_ref, flux_ref, ocean_vertical_ref, store
         )
-        going.append(pltpu.make_async_copy(new_ocean_ref, new_ocean_hbm, ocean_sems.at[1]))
-        going[-1].start()
+        for n, at in enumerate((0, ocean_cells - 1)):
+            ends = new_ocean_ref.at[n], new_ocean_hbm.at[:, at]
+            going.append(pltpu.make_async_copy(*ends, ocean_sems.at[4 + n]))
+            going[-1].start()
     wait_all(going)
 
 
@@ -635,44 +661,46 @@
     )
     state_near = swap(state_a, state_b)
     load_near = swap(load_a, load_b)
-    mixed, rows = call(
+    mixed, rows, ocean_inside = call(
         first_step_kernel,
-        (shape((cells, height, width), BF16), shape((4, cells, width), F32)),
-        atm_state, courant, atm_vertical,
-        specs={0: ANY},
-        out_specs={0: ANY},
+        (
+            shape((cells, height, width), BF16),
+            shape((4, cells, width), F32),
+            shape(ocean_rows.shape, F32),
+        ),
+        atm_state, courant, atm_vertical, ocean_rows, ocean_sea, flux_in, ocean_vertical,
+        specs={0: ANY, 3: ANY},
+        out_specs={0: ANY, 2: ANY},
         scratch=[
+            pltpu.VMEM(ocean_rows.shape, F32),
+            pltpu.VMEM(ocean_rows.shape, F32),
+            dma((2,)),
             pltpu.VMEM(atm_state.shape, BF16), whole, whole,
             dma((LEVEL_PARTS,)), dma((cells // GROUP,)),
         ],
+        limit=53,
         touched=16 << 20,
     )
-    mixed_edge, edge_rows = call(
-        first_edges_kernel,
-        (shape((4, height, width), BF16), shape((4, 8, width), F32)),
-        odd, *state_near, state_a, state_b, courant, atm_vertical,
-        specs={0: SCALAR},
-        out_specs={0: ANY},
-        scratch=[pltpu.VMEM((4, height, width), BF16), dma],
-        limit=50,
-        touched=2 << 20,
-    )
-
-    coupled, slots, outgoing = call(
+    coupled, slots, outgoing, mixed_edge = call(
         functools.partial(couple_kernel, layers),
         (
             shape((3 * cells + 8, width), F32),
             shape((8, devices), F32),
             shape((devices * 8, 128), BF16),
+            shape((4, height, width), BF16),
         ),
         odd, gathered, goal, *load_near, remap_weight, atm_sea, place,
-        rows, edge_rows, courant, atm_vertical,
+        rows, *state_near, state_a, state_b, courant, atm_vertical,
         specs={0: SCALAR, 5: ANY},
+        out_specs={3: ANY},
         scratch=[
             pltpu.VMEM((devices * 8, 128), F32),
             pltpu.VMEM((128, 128), F32),
             pltpu.VMEM((blocks * 8, 128), F32),
             pltpu.VMEM((pairs * 4, 128), F32),
+            pltpu.VMEM((4, 8, width), F32),
+            pltpu.VMEM((4, height, width), BF16),
+            dma,
             *held,
         ],
         limit=50,
@@ -683,25 +711,26 @@
     )
     state, new_ocean = call(
         functools.partial(second_step_kernel, tiles),
-        (shape(atm_state.shape, BF16), shape(ocean_rows.shape, F32)),
+        (shape(atm_state.shape, BF16), shape(ocean_state.shape, F32)),
         odd, mixed, mixed_edge, courant, atm_vertical, atm_sea, coupled,
-        ocean_rows, *load_near, ocean_sea, flux_in, ocean_vertical,
-        specs={0: SCALAR, 1: ANY, 2: ANY, 7: ANY},
+        ocean_state, ocean_inside.reshape(ocean_state.shape), *load_near, ocean_sea, flux_in, ocean_vertical,
+        specs={0: SCALAR, 1: ANY, 2: ANY, 7: ANY, 8: ANY},
         out_specs={0: ANY, 1: ANY},
+        aliases={8: 1},
         scratch=[
             whole,
             pltpu.VMEM((4, height, width), BF16),
             pltpu.VMEM((cells + 2, height, width), BF16),
             whole,
             pltpu.VMEM(atm_state.shape, BF16),
-            pltpu.VMEM(ocean_rows.shape, F32),
-            pltpu.VMEM(ocean_rows.shape, F32),
+            pltpu.VMEM((4, layers, ocean_width), F32),
+            pltpu.VMEM((2, layers, ocean_width), F32),
             dma((cells // GROUP,)),
             dma,
-            dma((2,)),
+            dma((6,)),
             dma((2,)),
         ],
-        limit=52,
+        limit=53,
         touched=24 << 20,
     )
     ocean_flux = call(
@@ -711,7 +740,7 @@
         scratch=[pltpu.VMEM((devices * 8, 128), F32)],
         touched=1 << 20,
     )
-    return state, new_ocean.reshape(ocean_state.shape), ocean_flux
+    return state, new_ocean, ocean_flux
 
 
 def solution(mesh):

time: 64.6 us -> 65.5 us (1.014)
  Pallas kernels: 33 us -> 34.5 us
  starting transfers between devices: 29.5 us -> 28.1 us
  local copies, waits for them, and re-layouts: 0.19 us -> 0.99 us
    pallas_call x7 -> x6, Pallas kernels: 33 us -> 34.5 us  [call(): pl.pallas_call(kernel, out_shape=outs, grid=grid, in_specs=[specs.get(i,...]
    all_to_all x1, starting transfers between devices: 9.42 us -> 8.04 us  [per_device(): lax.all_to_all(outgoing.reshape(devices, 8, 128), BOTH, split_axis=0, con...]
    unnamed x20 -> x24, local copies, waits for them, and re-layouts: 0.06 us -> 0.86 us
  transfers between devices with their start and end apart: 6 -> 6, of which waited for: 1 -> 1; matrix products, arithmetic and copies ran while one was open for 0% -> 0% of each run, Pallas kernels for 34% -> 35%
where the time goes in v4:
time: 65.5 us; the launch traced here: 65.2 us
  Pallas kernels  34.5 us (53%)
  starting transfers between devices  28.1 us (43%)
  local copies, waits for them, and re-layouts  0.99 us (2%)
  between operations  0.91 us (1%)
  waiting for transfers between devices  0.72 us (1%)
    pallas_call x6, Pallas kernels, call(): pl.pallas_call(kernel, out_shape=outs, grid=grid, in_specs=[specs.get(i,...  34.5 us
    all_to_all x1, starting transfers between devices, per_device(): lax.all_to_all(head, BOTH, split_axis=0, concat_axis=0, tiled=True)  11.5 us
    ppermute x4, starting transfers between devices, swap(): return (lax.ppermute(within, BOTH, pair), lax.ppermute(across, BOTH, other))  8.57 us
    all_to_all x1, starting transfers between devices, per_device(): lax.all_to_all(outgoing.reshape(devices, 8, 128), BOTH, split_axis=0, con...  8.04 us
  transfers between devices with their start and end apart: 6, of which 1 were waited for; matrix products, arithmetic and copies ran while one was open for 0% of the time, Pallas kernels for 35%

profile of v4, /device:TPU:1, one launch (start us, length us, event | category | flops | bytes accessed | tf_op | source)
XLA Modules:
  0.0 65.2 jit_solution(9153744816698162586)
XLA Ops:
  0.6 2.2 %shard_map.131 = (bf16[128,24,128]{2,1,0:T(8,128)(2,1)}, s32[8,256]{1,0:T(8,128)}) custom-call(s32[4,64]{1,0:T(4,128)} %bitcast.13, s32[4,64]{1,0:T(4,128)} %bitcast.15, f32[160,16,128]{2,1,0:T(8,128)} %ocean_hbm.5), custom_call_target="tpu_custom_call" | custom-call | bytes 1048576 | tf_op jit(solution)/shard_map/pallas_call | solution.py:28
  2.9 11.5 %all-to-all-start = ((bf16[128,24,128]{2,1,0:T(8,128)(2,1)}), bf16[128,24,128]{2,1,0:T(8,128)(2,1)S(1)}, u32[]{:S(2)}, u32[]{:S(2)}) async-start(bf16[128,24,128]{2,1,0:T(8,128)(2,1)} %get-tuple-element.20), calls=%async_computation | async-start | bytes 1572864 | tf_op jit(solution)/shard_map/all_to_all | solution.py:642
  14.4 0.0 copy-start.11
  14.4 0.0 copy-start.1
  14.4 0.0 copy-start.2
  14.4 0.0 copy-start.7
  14.4 0.0 copy-start.8
  14.4 4.5 %shard_map.132 = (bf16[2,256,256]{2,1,0:T(8,128)(2,1)}, bf16[2,256,256]{2,1,0:T(8,128)(2,1)}, bf16[11,128,128]{2,1,0:T(8,128)(2,1)}, bf16[11,128,128]{2,1,0:T(8,128)(2,1)}, f32[8,128]{1,0:T(8,128)}) custom-call(s32[1]{0:T(128)} %bitcast.odd_ref, bf16[256,32,256]{2,1,0:T(8,128)(2,1)} %state_ref.1, f32[160,16,128]{2,1,0:T(8,128)} %ocean_hbm.5, ...), custom_call_target="tpu_custom_call" | custom-call | bytes 6291456 | tf_op jit(solution)/shard_map/pallas_call | solution.py:28
  18.9 0.0 copy-start.4
  18.9 0.0 copy-start.5
  18.9 0.0 copy-start.6
  18.9 0.0 copy-start.9
  19.0 0.0 copy-start.10
  19.0 1.1 %collective-permute-start = (bf16[11,128,128]{2,1,0:T(8,128)(2,1)}, bf16[11,128,128]{2,1,0:T(8,128)(2,1)S(1)}, u32[]{:S(2)}, u32[]{:S(2)}) collective-permute-start(bf16[11,128,128]{2,1,0:T(8,128)(2,1)} %get-tuple-element.22), channel_id=1, source_target_pairs={{0,1},{1,0},{2,3},{3,2},{4,5},{5,4},{6,7},{7,6},{8,9},{9,8},{10,11... | collective-permute-start | bytes 1081352 | tf_op jit(solution)/shard_map/ppermute | solution.py:605
  20.1 0.7 %collective-permute-start.1 = (bf16[11,128,128]{2,1,0:T(8,128)(2,1)}, bf16[11,128,128]{2,1,0:T(8,128)(2,1)S(1)}, u32[]{:S(2)}, u32[]{:S(2)}) collective-permute-start(bf16[11,128,128]{2,1,0:T(8,128)(2,1)} %get-tuple-element.23), channel_id=1, source_target_pairs={{0,127},{1,2},{2,1},{3,4},{4,3},{5,6},{6,5},{7,8},{8,7},{9,10},{10... | collective-permute-start | bytes 1081352 | tf_op jit(solution)/shard_map/ppermute | solution.py:605
  20.8 6.7 %collective-permute-start.2 = (bf16[2,256,256]{2,1,0:T(8,128)(2,1)}, bf16[2,256,256]{2,1,0:T(8,128)(2,1)S(1)}, u32[]{:S(2)}, u32[]{:S(2)}) collective-permute-start(bf16[2,256,256]{2,1,0:T(8,128)(2,1)} %get-tuple-element.26.own_a_ref), channel_id=1, source_target_pairs={{0,1},{1,0},{2,3},{3,2},{4,5},{5,4},{6,7},{7,6},{8,9},{9,8},{10,11... | collective-permute-start | bytes 786440 | tf_op jit(solution)/shard_map/ppermute | solution.py:605
  27.5 0.0 collective-permute-start.3
  27.5 0.0 copy-done.11
  27.5 0.1 copy.15.courant_ref
  27.7 0.0 copy-done.1
  27.7 8.0 %shard_map.130 = (bf16[32,256,256]{2,1,0:T(8,128)(2,1)}, f32[4,32,256]{2,1,0:T(8,128)S(1)}, f32[2560,128]{1,0:T(8,128)}) custom-call(bf16[256,32,256]{2,1,0:T(8,128)(2,1)} %state_ref.1, f32[256,1]{1,0:T(8,128)S(1)} %copy.15.courant_ref, bf16[256,256]{1,0:T(8,128)(2,1)S(1)} %copy-done.1, f32[2560,128]{1,0:T(8,128)} %bitcast.11, s32[16,128]{1,0:T(8,128)S(1)} %copy-done.7, ...), custom_call_target="tpu_custom_call" | custom-call | bytes 16777216 | tf_op jit(solution)/shard_map/pallas_call | solution.py:28
  35.7 0.0 collective-permute-done.2.near_within_ref
  35.7 0.0 collective-permute-done.3.near_across_ref
  35.7 0.0 collective-permute-done.within_ref
  35.7 0.0 collective-permute-done.1.across_ref
  35.7 0.0 all-to-all-done.head_ref
  35.8 8.5 %shard_map.133 = (f32[104,256]{1,0:T(8,128)S(1)}, f32[8,128]{1,0:T(8,128)S(1)}, bf16[1024,128]{1,0:T(8,128)(2,1)}, bf16[4,256,256]{2,1,0:T(8,128)(2,1)S(1)}) custom-call(s32[1]{0:T(128)} %bitcast.odd_ref, bf16[128,24,128]{2,1,0:T(8,128)(2,1)S(1)} %all-to-all-done.head_ref, f32[8,128]{1,0:T(8,128)S(1)} %copy-done.10, ...), custom_call_target="tpu_custom_call" | custom-call | bytes 16777216 | tf_op jit(solution)/shard_map/pallas_call | solution.py:28
  44.3 0.8 %copy-done.3 = bf16[4,256,256]{2,1,0:T(8,128)(2,1)} copy-done((bf16[4,256,256]{2,1,0:T(8,128)(2,1)}, bf16[4,256,256]{2,1,0:T(8,128)(2,1)S(1)}, u32[]{:S(2)}) %copy-start.3) | copy-done | bytes 524312
  45.1 8.0 %all-to-all-start.1 = ((bf16[128,8,128]{2,1,0:T(8,128)(2,1)}), bf16[128,8,128]{2,1,0:T(8,128)(2,1)S(1)}, u32[]{:S(2)}, u32[]{:S(2)}) async-start(bf16[128,8,128]{2,1,0:T(8,128)(2,1)} %bitcast.7), calls=%async_computation.1 | async-start | bytes 524288 | tf_op jit(solution)/shard_map/all_to_all | solution.py:709
  53.1 10.5 %shard_map.134 = (bf16[256,32,256]{2,1,0:T(8,128)(2,1)}, f32[160,16,128]{2,1,0:T(8,128)}) custom-call(s32[1]{0:T(128)} %bitcast.odd_ref, bf16[32,256,256]{2,1,0:T(8,128)(2,1)} %get-tuple-element.19.mixed_hbm, bf16[4,256,256]{2,1,0:T(8,128)(2,1)} %copy-done.3, f32[256,1]{1,0:T(8,128)S(1)} %copy.15.courant_ref, ...), custom_call_target="tpu_custom_call", output_to_operand_aliasing={{1}: (8, {})} | custom-call | bytes 25165824 | tf_op jit(solution)/shard_map/pallas_call | solution.py:28
  63.6 0.7 %all-to-all-done.1 = bf16[128,8,128]{2,1,0:T(8,128)(2,1)S(1)} async-done(((bf16[128,8,128]{2,1,0:T(8,128)(2,1)}), bf16[128,8,128]{2,1,0:T(8,128)(2,1)S(1)}, u32[]{:S(2)}, u32[]{:S(2)}) %all-to-all-start.1) | async-done | bytes 262176 | tf_op jit(solution)/shard_map/all_to_all | solution.py:709
  64.4 0.8 %shard_map.135 = f32[2,16,128]{2,1,0:T(8,128)} custom-call(bf16[1024,128]{1,0:T(8,128)(2,1)S(1)} %bitcast.9, f32[8,128]{1,0:T(8,128)S(1)} %get-tuple-element.34.slots_ref, s32[16,128]{1,0:T(8,128)S(1)} %copy-done.7), custom_call_target="tpu_custom_call" | custom-call | bytes 1048576 | tf_op jit(solution)/shard_map/pallas_call | solution.py:28
  (11 shorter events, 0.0 us)
Async XLA Ops:
  2.9 32.9 %all-to-all-start = ((bf16[128,24,128]{2,1,0:T(8,128)(2,1)}), bf16[128,24,128]{2,1,0:T(8,128)(2,1)S(1)}, u32[]{:S(2)}, u32[]{:S(2)}) async-start(bf16[128,24,128]{2,1,0:T(8,128)(2,1)} %get-tuple-element.20), calls=%async_computation | async-start | bytes 1572864 | tf_op jit(solution)/shard_map/all_to_all | solution.py:642
  14.4 13.2 %copy-start.11 = (f32[256]{0:T(256)S(1)}, f32[256]{0:T(256)}, u32[]{:S(2)}) copy-start(f32[256]{0:T(256)} %param.13) | copy-start | bytes 3076
  14.4 13.3 %copy-start.1 = (bf16[256,256]{1,0:T(8,128)(2,1)S(1)}, bf16[256,256]{1,0:T(8,128)(2,1)}, u32[]{:S(2)}) copy-start(bf16[256,256]{1,0:T(8,128)(2,1)} %vertical_ref.5) | copy-start | bytes 393220
  14.4 13.3 %copy-start.2 = (f32[160,160]{1,0:T(8,128)S(1)}, f32[160,160]{1,0:T(8,128)}, u32[]{:S(2)}) copy-start(f32[160,160]{1,0:T(8,128)} %ocean_vertical_ref.3) | copy-start | bytes 307204
  14.4 13.3 %copy-start.7 = (s32[16,128]{1,0:T(8,128)S(1)}, s32[16,128]{1,0:T(8,128)}, u32[]{:S(2)}) copy-start(s32[16,128]{1,0:T(8,128)} %sea_ref.7) | copy-start | bytes 24580
  14.4 13.3 %copy-start.8 = (f32[2,16,128]{2,1,0:T(8,128)S(1)}, f32[2,16,128]{2,1,0:T(8,128)}, u32[]{:S(2)}) copy-start(f32[2,16,128]{2,1,0:T(8,128)} %flux_ref.3) | copy-start | bytes 49156
  18.9 16.8 %copy-start.4 = (s32[32,256]{1,0:T(8,128)S(1)}, s32[32,256]{1,0:T(8,128)}, u32[]{:S(2)}) copy-start(s32[32,256]{1,0:T(8,128)} %sea_ref.6) | copy-start | bytes 98308
  18.9 16.8 %copy-start.5 = (bf16[2,256,256]{2,1,0:T(8,128)(2,1)S(1)}, bf16[2,256,256]{2,1,0:T(8,128)(2,1)}, u32[]{:S(2)}) copy-start(bf16[2,256,256]{2,1,0:T(8,128)(2,1)} %get-tuple-element.26.own_a_ref) | copy-start | bytes 786436
  18.9 16.8 %copy-start.6 = (bf16[2,256,256]{2,1,0:T(8,128)(2,1)S(1)}, bf16[2,256,256]{2,1,0:T(8,128)(2,1)}, u32[]{:S(2)}) copy-start(bf16[2,256,256]{2,1,0:T(8,128)(2,1)} %get-tuple-element.27.own_b_ref) | copy-start | bytes 786436
  18.9 16.8 %copy-start.9 = (s32[8,256]{1,0:T(8,128)S(1)}, s32[8,256]{1,0:T(8,128)}, u32[]{:S(2)}) copy-start(s32[8,256]{1,0:T(8,128)} %get-tuple-element.24.place_ref) | copy-start | bytes 24580
  19.0 16.8 %copy-start.10 = (f32[8,128]{1,0:T(8,128)S(1)}, f32[8,128]{1,0:T(8,128)}, u32[]{:S(2)}) copy-start(f32[8,128]{1,0:T(8,128)} %get-tuple-element.21.goal_ref) | copy-start | bytes 12292
  19.0 16.7 %collective-permute-start = (bf16[11,128,128]{2,1,0:T(8,128)(2,1)}, bf16[11,128,128]{2,1,0:T(8,128)(2,1)S(1)}, u32[]{:S(2)}, u32[]{:S(2)}) collective-permute-start(bf16[11,128,128]{2,1,0:T(8,128)(2,1)} %get-tuple-element.22), channel_id=1, source_target_pairs={{0,1},{1,0},{2,3},{3,2},{4,5},{5,4},{6,7},{7,6},{8,9},{9,8},{10,11... | collective-permute-start | bytes 1081352 | tf_op jit(solution)/shard_map/ppermute | solution.py:605
  20.1 15.6 %collective-permute-start.1 = (bf16[11,128,128]{2,1,0:T(8,128)(2,1)}, bf16[11,128,128]{2,1,0:T(8,128)(2,1)S(1)}, u32[]{:S(2)}, u32[]{:S(2)}) collective-permute-start(bf16[11,128,128]{2,1,0:T(8,128)(2,1)} %get-tuple-element.23), channel_id=1, source_target_pairs={{0,127},{1,2},{2,1},{3,4},{4,3},{5,6},{6,5},{7,8},{8,7},{9,10},{10... | collective-permute-start | bytes 1081352 | tf_op jit(solution)/shard_map/ppermute | solution.py:605
  20.8 14.9 %collective-permute-start.2 = (bf16[2,256,256]{2,1,0:T(8,128)(2,1)}, bf16[2,256,256]{2,1,0:T(8,128)(2,1)S(1)}, u32[]{:S(2)}, u32[]{:S(2)}) collective-permute-start(bf16[2,256,256]{2,1,0:T(8,128)(2,1)} %get-tuple-element.26.own_a_ref), channel_id=1, source_target_pairs={{0,1},{1,0},{2,3},{3,2},{4,5},{5,4},{6,7},{7,6},{8,9},{9,8},{10,11... | collective-permute-start | bytes 786440 | tf_op jit(solution)/shard_map/ppermute | solution.py:605
  27.5 8.2 %collective-permute-start.3 = (bf16[2,256,256]{2,1,0:T(8,128)(2,1)}, bf16[2,256,256]{2,1,0:T(8,128)(2,1)S(1)}, u32[]{:S(2)}, u32[]{:S(2)}) collective-permute-start(bf16[2,256,256]{2,1,0:T(8,128)(2,1)} %get-tuple-element.27.own_b_ref), channel_id=1, source_target_pairs={{0,127},{1,2},{2,1},{3,4},{4,3},{5,6},{6,5},{7,8},{8,7},{9,10},{10... | collective-permute-start | bytes 786440 | tf_op jit(solution)/shard_map/ppermute | solution.py:605
  35.7 8.5 %copy-start = (bf16[11,128,128]{2,1,0:T(8,128)(2,1)}, bf16[11,128,128]{2,1,0:T(8,128)(2,1)S(1)}, u32[]{:S(2)}) copy-start(bf16[11,128,128]{2,1,0:T(8,128)(2,1)S(1)} %collective-permute-done.1.across_ref) | copy-start | bytes 1081348
  44.3 0.8 %copy-start.3 = (bf16[4,256,256]{2,1,0:T(8,128)(2,1)}, bf16[4,256,256]{2,1,0:T(8,128)(2,1)S(1)}, u32[]{:S(2)}) copy-start(bf16[4,256,256]{2,1,0:T(8,128)(2,1)S(1)} %get-tuple-element.28.edge_hbm) | copy-start | bytes 1572868
  45.1 19.3 %all-to-all-start.1 = ((bf16[128,8,128]{2,1,0:T(8,128)(2,1)}), bf16[128,8,128]{2,1,0:T(8,128)(2,1)S(1)}, u32[]{:S(2)}, u32[]{:S(2)}) async-start(bf16[128,8,128]{2,1,0:T(8,128)(2,1)} %bitcast.7), calls=%async_computation.1 | async-start | bytes 524288 | tf_op jit(solution)/shard_map/all_to_all | solution.py:709

commit v5 on v4

--- a/solution.py
+++ b/solution.py
@@ -105,15 +105,25 @@
     head_ref[:, 16:24, :] = slot_rows[...].reshape(devices, 8, 128).astype(BF16)
 
 
+EDGE_PARTS = 8
 PACK = 192
 
 
 def edges_kernel(
-    odd_ref, state_ref, ocean_hbm, weight_hbm, owner_ref, block_ref, sea_ref,
+    odd_ref, state_hbm, ocean_hbm, weight_hbm, owner_ref, block_ref, sea_ref,
     state_a_ref, state_b_ref, load_a_ref, load_b_ref, goal_ref,
-    ocean_first, ocean_last, sems,
+    state_ref, ocean_first, ocean_last, state_sems, sems,
 ):
-    i, odd = pl.program_id(0), odd_ref[0]
+    odd = odd_ref[0]
+    levels = state_ref.shape[0] // EDGE_PARTS
+    coming = start_all([
+        pltpu.make_async_copy(
+            state_hbm.at[pl.ds(n * levels, levels)],
+            state_ref.at[pl.ds(n * levels, levels)],
+            state_sems.at[n],
+        )
+        for n in range(EDGE_PARTS)
+    ])
     tiles = 2 * owner_ref.shape[0]
     at_a = (1 - odd) * (weight_hbm.shape[0] - tiles)
     at_b = odd * (weight_hbm.shape[0] - tiles)
@@ -123,34 +133,33 @@
         pltpu.make_async_copy(ocean_hbm.at[:, 0], ocean_first, sems.at[2]),
         pltpu.make_async_copy(ocean_hbm.at[:, ocean_hbm.shape[1] - 1], ocean_last, sems.at[3]),
     ]
-    pl.when(i == 0)(lambda: (start_all(copies), None)[1])
-    rows, cells = state_ref.shape[0], state_ref.shape[1]
-    first = jnp.swapaxes(state_ref[:, 0:8, :], 0, 1)[0:2]
-    last = jnp.swapaxes(state_ref[:, cells - 8 : cells, :], 0, 1)[6:8]
-    at = pl.ds(pl.multiple_of(i * rows, rows), rows)
-    state_a_ref[:, at, :], state_b_ref[:, at, :] = sides(odd_ref, first, last)
-
-    @pl.when(i == pl.num_programs(0) - 1)
-    def _():
-        layers = ocean_first.shape[0]
-        goal = (owner_ref[...] * 16 + block_ref[...]).astype(F32)
-        goal_ref[...] = jnp.zeros_like(goal_ref)
-        goal_ref[0 : goal.shape[0], 0 : goal.shape[1]] = goal
-        sea = sea_ref[...].astype(F32)
-        width = sea.shape[1] // 2
-        row = iota((8, width), 0)
-        wait_all(copies)
-        oceans = sides(odd_ref, ocean_first[...], ocean_last[...])
-        lines = sides(odd_ref, sea[0:1], sea[cells - 1 : cells])
-        for ref, ocean, line in zip((load_a_ref, load_b_ref), oceans, lines):
-            halves = jnp.where(row == 0, line[:, :width], jnp.where(row == 1, line[:, width:], 0.0))
-            empty = jnp.zeros((PACK - layers - 16, width), F32)
-            pack = jnp.concatenate([ocean, halves, goal_ref[...], empty], axis=0)
-            high = pack.astype(BF16)
-            low = (pack - high.astype(F32)).astype(BF16)
-            ref[tiles:] = jnp.concatenate([high, low], axis=0).reshape(
-                2 * PACK // width, width, width
-            )
+    start_all(copies)
+    cells = state_ref.shape[1]
+    layers = ocean_first.shape[0]
+    goal = (owner_ref[...] * 16 + block_ref[...]).astype(F32)
+    goal_ref[...] = jnp.zeros_like(goal_ref)
+    goal_ref[0 : goal.shape[0], 0 : goal.shape[1]] = goal
+    sea = sea_ref[...].astype(F32)
+    width = sea.shape[1] // 2
+    row = iota((8, width), 0)
+    for n, c in enumerate(coming):
+        c.wait()
+        at = slice(n * levels, (n + 1) * levels)
+        first = jnp.swapaxes(state_ref[at, 0:8, :], 0, 1)[0:2]
+        last = jnp.swapaxes(state_ref[at, cells - 8 : cells, :], 0, 1)[6:8]
+        state_a_ref[:, at, :], state_b_ref[:, at, :] = sides(odd_ref, first, last)
+    wait_all(copies)
+    oceans = sides(odd_ref, ocean_first[...], ocean_last[...])
+    lines = sides(odd_ref, sea[0:1], sea[cells - 1 : cells])
+    for ref, ocean, line in zip((load_a_ref, load_b_ref), oceans, lines):
+        halves = jnp.where(row == 0, line[:, :width], jnp.where(row == 1, line[:, width:], 0.0))
+        empty = jnp.zeros((PACK - layers - 16, width), F32)
+        pack = jnp.concatenate([ocean, halves, goal_ref[...], empty], axis=0)
+        high = pack.astype(BF16)
+        low = (pack - high.astype(F32)).astype(BF16)
+        ref[tiles:] = jnp.concatenate([high, low], axis=0).reshape(
+            2 * PACK // width, width, width
+        )
 
 
 def unpack(load):
@@ -332,9 +341,9 @@
 def couple_kernel(
     layers,
     odd_ref, head_ref, goal_ref, within_ref, across_ref, weight_hbm, sea_ref, place_ref,
-    rows_ref, near_within_ref, near_across_ref, own_a_ref, own_b_ref, courant_ref, vertical_ref,
-    coupled_ref, slots_ref, out_ref, mixed_hbm,
-    slot_rows, by_block, flux_rows, shares, edges_ref, mixed_out, mixed_sem, held, sems,
+    rows_ref, near_within_ref, near_across_ref, own_a_ref, own_b_ref, courant_ref, vertical_ref, _,
+    coupled_ref, slots_ref, out_ref, mixed_hbm, ocean_hbm,
+    slot_rows, by_block, flux_rows, shares, edges_ref, mixed_out, ocean_out, out_sems, held, sems,
 ):
     copies = weight_copies(weight_hbm, held, sems)
     edge_columns(
@@ -342,8 +351,10 @@
         *sides(odd_ref, own_a_ref[...], own_b_ref[...]),
         courant_ref[...], vertical_ref[...], edges_ref, mixed_out,
     )
-    mixed_going = pltpu.make_async_copy(mixed_out, mixed_hbm, mixed_sem)
-    mixed_going.start()
+    going = [pltpu.make_async_copy(
+        mixed_out, mixed_hbm.at[pl.ds(sea_ref.shape[0], 4)], out_sems.at[0]
+    )]
+    going[0].start()
     devices = head_ref.shape[0]
     blocks, sources = held.shape[0], held.shape[1]
     surface = head_ref[:, 0:16, :].reshape(devices * 16, 128)
@@ -351,10 +362,12 @@
     slots_ref[...] = jnp.transpose(slot_rows[pl.ds(0, devices, stride=8), :])[:8]
 
     tiles = 2 * sources
-    left_pack, right_pack = (
-        p[layers : layers + 16]
-        for p in sides(odd_ref, unpack(within_ref[tiles:]), unpack(across_ref[tiles:]))
-    )
+    packs = sides(odd_ref, unpack(within_ref[tiles:]), unpack(across_ref[tiles:]))
+    for n in range(2):
+        ocean_out[n] = packs[n][:layers]
+    going.append(pltpu.make_async_copy(ocean_out, ocean_hbm, out_sems.at[1]))
+    going[1].start()
+    left_pack, right_pack = (p[layers : layers + 16] for p in packs)
     lane = iota((8, 128), 1)
     goals = jnp.where(
         lane < blocks,
@@ -483,17 +496,19 @@
         ).astype(BF16)
         total += jnp.dot(pick, share, preferred_element_type=F32)
     out_ref[...] = total.astype(BF16)
-    mixed_going.wait()
+    wait_all(going)
 
 
 def second_step_kernel(
-    tiles, odd_ref, mixed_hbm, edge_hbm, courant_ref, vertical_ref, sea_ref, coupled_ref,
-    ocean_hbm, _, within_ref, across_ref, ocean_sea_ref, flux_ref, ocean_vertical_ref,
+    mixed_hbm, courant_ref, vertical_ref, sea_ref, coupled_ref,
+    ocean_hbm, _, ocean_halo_hbm, ocean_sea_ref, flux_ref, ocean_vertical_ref,
     out_hbm, new_ocean_hbm,
-    mixed_ref, edge_ref, state, result, out_ref, ocean_ref, new_ocean_ref,
+    mixed_ref, edge_ref, state, result, out_ref, ocean_ref, ocean_halo_ref, new_ocean_ref,
     in_sems, edge_sem, ocean_sems, out_sems,
 ):
-    edge_copy = pltpu.make_async_copy(edge_hbm, edge_ref, edge_sem)
+    edge_copy = pltpu.make_async_copy(
+        mixed_hbm.at[pl.ds(mixed_ref.shape[0], 4)], edge_ref, edge_sem
+    )
     edge_copy.start()
     coming = start_all(groups(mixed_hbm, mixed_ref, in_sems))
     ocean_cells = ocean_sea_ref.shape[0]
@@ -501,7 +516,7 @@
     ocean_coming = start_all([
         pltpu.make_async_copy(ocean_hbm.at[:, x], ocean_ref.at[n], ocean_sems.at[n])
         for n, x in enumerate(near_ends)
-    ])
+    ] + [pltpu.make_async_copy(ocean_halo_hbm, ocean_halo_ref, ocean_sems.at[6])])
     cells, height = mixed_ref.shape[0], mixed_ref.shape[1]
     top, low = height // 2 - 1, height - 1
     lateral = lateral_matrix(mixed_ref.shape[2])
@@ -561,12 +576,7 @@
         if x + 1 == cells:
             break
         wait_all(ocean_coming)
-        layers = ocean_ref.shape[1]
-        left, right = (
-            p[:layers]
-            for p in sides(odd_ref, unpack(within_ref[tiles:]), unpack(across_ref[tiles:]))
-        )
-        known = {-1: left, ocean_cells: right}
+        known = {-1: ocean_halo_ref[0], ocean_cells: ocean_halo_ref[1]}
         known.update((at, ocean_ref[n]) for n, at in enumerate(near_ends))
 
         def store(x, value):
@@ -621,7 +631,6 @@
     dma = pltpu.SemaphoreType.DMA
     held = [pltpu.VMEM(remap_weight.shape, BF16), dma((PARTS,))]
     whole = pltpu.VMEM((cells, height, width), BF16)
-    levels = 64
 
     head, place = call(
         plan_kernel,
@@ -650,12 +659,17 @@
         odd, atm_state, ocean_state, remap_weight.reshape(pairs, 128, 128), owner, block, atm_sea,
         specs={
             0: SCALAR,
-            1: pl.BlockSpec((levels, cells, width), lambda i: (i, 0, 0)),
+            1: ANY,
             2: ANY,
             3: ANY,
         },
-        scratch=[pltpu.VMEM((layers, ocean_width), F32)] * 2 + [dma((4,))],
-        grid=(height // levels,),
+        scratch=[
+            pltpu.VMEM(atm_state.shape, BF16),
+            pltpu.VMEM((layers, ocean_width), F32),
+            pltpu.VMEM((layers, ocean_width), F32),
+            dma((EDGE_PARTS,)),
+            dma((4,)),
+        ],
         limit=54,
         touched=6 << 20,
     )
@@ -664,7 +678,7 @@
     mixed, rows, ocean_inside = call(
         first_step_kernel,
         (
-            shape((cells, height, width), BF16),
+            shape((cells + 4, height, width), BF16),
             shape((4, cells, width), F32),
             shape(ocean_rows.shape, F32),
         ),
@@ -681,18 +695,20 @@
         limit=53,
         touched=16 << 20,
     )
-    coupled, slots, outgoing, mixed_edge = call(
+    coupled, slots, outgoing, mixed, ocean_halo = call(
         functools.partial(couple_kernel, layers),
         (
             shape((3 * cells + 8, width), F32),
             shape((8, devices), F32),
             shape((devices * 8, 128), BF16),
-            shape((4, height, width), BF16),
+            shape(mixed.shape, BF16),
+            shape((2, layers, ocean_width), F32),
         ),
         odd, gathered, goal, *load_near, remap_weight, atm_sea, place,
-        rows, *state_near, state_a, state_b, courant, atm_vertical,
-        specs={0: SCALAR, 5: ANY},
-        out_specs={3: ANY},
+        rows, *state_near, state_a, state_b, courant, atm_vertical, mixed,
+        specs={0: SCALAR, 5: ANY, 15: ANY},
+        aliases={15: 3},
+        out_specs={3: ANY, 4: ANY},
         scratch=[
             pltpu.VMEM((devices * 8, 128), F32),
             pltpu.VMEM((128, 128), F32),
@@ -700,7 +716,8 @@
             pltpu.VMEM((pairs * 4, 128), F32),
             pltpu.VMEM((4, 8, width), F32),
             pltpu.VMEM((4, height, width), BF16),
-            dma,
+            pltpu.VMEM((2, layers, ocean_width), F32),
+            dma((2,)),
             *held,
         ],
         limit=50,
@@ -710,13 +727,13 @@
         outgoing.reshape(devices, 8, 128), BOTH, split_axis=0, concat_axis=0, tiled=True
     )
     state, new_ocean = call(
-        functools.partial(second_step_kernel, tiles),
+        second_step_kernel,
         (shape(atm_state.shape, BF16), shape(ocean_state.shape, F32)),
-        odd, mixed, mixed_edge, courant, atm_vertical, atm_sea, coupled,
-        ocean_state, ocean_inside.reshape(ocean_state.shape), *load_near, ocean_sea, flux_in, ocean_vertical,
-        specs={0: SCALAR, 1: ANY, 2: ANY, 7: ANY, 8: ANY},
+        mixed, courant, atm_vertical, atm_sea, coupled,
+        ocean_state, ocean_inside.reshape(ocean_state.shape), ocean_halo, ocean_sea, flux_in, ocean_vertical,
+        specs={0: ANY, 5: ANY, 6: ANY, 7: ANY},
         out_specs={0: ANY, 1: ANY},
-        aliases={8: 1},
+        aliases={6: 1},
         scratch=[
             whole,
             pltpu.VMEM((4, height, width), BF16),
@@ -725,9 +742,10 @@
             pltpu.VMEM(atm_state.shape, BF16),
             pltpu.VMEM((4, layers, ocean_width), F32),
             pltpu.VMEM((2, layers, ocean_width), F32),
+            pltpu.VMEM((2, layers, ocean_width), F32),
             dma((cells // GROUP,)),
             dma,
-            dma((6,)),
+            dma((7,)),
             dma((2,)),
         ],
         limit=53,

time: 65.5 us -> 64.8 us (0.989)
  local copies, waits for them, and re-layouts: 0.99 us -> 0.19 us
    unnamed x24 -> x20, local copies, waits for them, and re-layouts: 0.86 us -> 0.06 us
where the time goes in v5:
time: 64.8 us; the launch traced here: 64.5 us
  Pallas kernels  34.4 us (53%)
  starting transfers between devices  28.1 us (43%)
  waiting for transfers between devices  0.99 us (2%)
  between operations  0.89 us (1%)
    pallas_call x6, Pallas kernels, call(): pl.pallas_call(kernel, out_shape=outs, grid=grid, in_specs=[specs.get(i,...  34.4 us
    all_to_all x1, starting transfers between devices, per_device(): lax.all_to_all(head, BOTH, split_axis=0, concat_axis=0, tiled=True)  11.5 us
    ppermute x4, starting transfers between devices, swap(): return (lax.ppermute(within, BOTH, pair), lax.ppermute(across, BOTH, other))  8.57 us
    all_to_all x1, starting transfers between devices, per_device(): lax.all_to_all(outgoing.reshape(devices, 8, 128), BOTH, split_axis=0, con...  8.04 us
  transfers between devices with their start and end apart: 6, of which 1 were waited for; matrix products, arithmetic and copies ran while one was open for 0% of the time, Pallas kernels for 35%

profile of v5, /device:TPU:1, one launch (start us, length us, event | category | flops | bytes accessed | tf_op | source)
XLA Modules:
  0.0 64.5 jit_solution(13126068000490299408)
XLA Ops:
  0.6 2.2 %shard_map.130 = (bf16[128,24,128]{2,1,0:T(8,128)(2,1)}, s32[8,256]{1,0:T(8,128)}) custom-call(s32[4,64]{1,0:T(4,128)} %bitcast.13, s32[4,64]{1,0:T(4,128)} %bitcast.15, f32[160,16,128]{2,1,0:T(8,128)} %ocean_hbm.5), custom_call_target="tpu_custom_call" | custom-call | bytes 1048576 | tf_op jit(solution)/shard_map/pallas_call | solution.py:28
  2.9 11.5 %all-to-all-start = ((bf16[128,24,128]{2,1,0:T(8,128)(2,1)}), bf16[128,24,128]{2,1,0:T(8,128)(2,1)S(1)}, u32[]{:S(2)}, u32[]{:S(2)}) async-start(bf16[128,24,128]{2,1,0:T(8,128)(2,1)} %get-tuple-element.20), calls=%async_computation | async-start | bytes 1572864 | tf_op jit(solution)/shard_map/all_to_all | solution.py:651
  14.4 0.0 copy-start.9
  14.4 0.0 copy-start
  14.4 0.0 copy-start.1
  14.4 0.0 copy-start.5
  14.4 0.0 copy-start.6
  14.4 4.4 %shard_map.131 = (bf16[2,256,256]{2,1,0:T(8,128)(2,1)}, bf16[2,256,256]{2,1,0:T(8,128)(2,1)}, bf16[11,128,128]{2,1,0:T(8,128)(2,1)}, bf16[11,128,128]{2,1,0:T(8,128)(2,1)}, f32[8,128]{1,0:T(8,128)}) custom-call(s32[1]{0:T(128)} %bitcast.odd_ref, bf16[256,32,256]{2,1,0:T(8,128)(2,1)} %state_hbm.3, f32[160,16,128]{2,1,0:T(8,128)} %ocean_hbm.5, ...), custom_call_target="tpu_custom_call" | custom-call | bytes 6291456 | tf_op jit(solution)/shard_map/pallas_call | solution.py:28
  18.9 0.0 copy-start.2
  18.9 0.0 copy-start.3
  18.9 0.0 copy-start.7
  18.9 1.1 %collective-permute-start = (bf16[11,128,128]{2,1,0:T(8,128)(2,1)}, bf16[11,128,128]{2,1,0:T(8,128)(2,1)S(1)}, u32[]{:S(2)}, u32[]{:S(2)}) collective-permute-start(bf16[11,128,128]{2,1,0:T(8,128)(2,1)} %get-tuple-element.22), channel_id=1, source_target_pairs={{0,1},{1,0},{2,3},{3,2},{4,5},{5,4},{6,7},{7,6},{8,9},{9,8},{10,11... | collective-permute-start | bytes 1081352 | tf_op jit(solution)/shard_map/ppermute | solution.py:615
  20.1 0.7 %collective-permute-start.1 = (bf16[11,128,128]{2,1,0:T(8,128)(2,1)}, bf16[11,128,128]{2,1,0:T(8,128)(2,1)S(1)}, u32[]{:S(2)}, u32[]{:S(2)}) collective-permute-start(bf16[11,128,128]{2,1,0:T(8,128)(2,1)} %get-tuple-element.23), channel_id=1, source_target_pairs={{0,127},{1,2},{2,1},{3,4},{4,3},{5,6},{6,5},{7,8},{8,7},{9,10},{10... | collective-permute-start | bytes 1081352 | tf_op jit(solution)/shard_map/ppermute | solution.py:615
  20.8 6.7 %collective-permute-start.2 = (bf16[2,256,256]{2,1,0:T(8,128)(2,1)}, bf16[2,256,256]{2,1,0:T(8,128)(2,1)S(1)}, u32[]{:S(2)}, u32[]{:S(2)}) collective-permute-start(bf16[2,256,256]{2,1,0:T(8,128)(2,1)} %get-tuple-element.26.own_a_ref), channel_id=1, source_target_pairs={{0,1},{1,0},{2,3},{3,2},{4,5},{5,4},{6,7},{7,6},{8,9},{9,8},{10,11... | collective-permute-start | bytes 786440 | tf_op jit(solution)/shard_map/ppermute | solution.py:615
  27.5 0.0 collective-permute-start.3
  27.5 0.1 copy.16.courant_ref
  27.7 8.0 %shard_map.132 = (bf16[36,256,256]{2,1,0:T(8,128)(2,1)}, f32[4,32,256]{2,1,0:T(8,128)S(1)}, f32[2560,128]{1,0:T(8,128)}) custom-call(bf16[256,32,256]{2,1,0:T(8,128)(2,1)} %state_hbm.3, f32[256,1]{1,0:T(8,128)S(1)} %copy.16.courant_ref, bf16[256,256]{1,0:T(8,128)(2,1)S(1)} %copy-done, f32[2560,128]{1,0:T(8,128)} %bitcast.11, s32[16,128]{1,0:T(8,128)S(1)} %copy-done.5, ...), custom_call_target="tpu_custom_call" | custom-call | bytes 16777216 | tf_op jit(solution)/shard_map/pallas_call | solution.py:28
  35.6 0.0 collective-permute-done.2.near_within_ref
  35.7 0.0 collective-permute-done.3.near_across_ref
  35.7 0.0 collective-permute-done.within_ref
  35.7 0.0 collective-permute-done.1.across_ref
  35.7 0.0 all-to-all-done.head_ref
  35.7 0.0 copy-done.2
  35.7 0.0 copy-done.3
  35.7 0.0 copy-done.4
  35.7 0.0 copy-done.7
  35.7 0.0 copy-done.8
  35.7 8.7 %shard_map.133 = (f32[104,256]{1,0:T(8,128)S(1)}, f32[8,128]{1,0:T(8,128)S(1)}, bf16[1024,128]{1,0:T(8,128)(2,1)}, bf16[36,256,256]{2,1,0:T(8,128)(2,1)}, f32[2,160,128]{2,1,0:T(8,128)S(1)}) custom-call(s32[1]{0:T(128)} %bitcast.odd_ref, bf16[128,24,128]{2,1,0:T(8,128)(2,1)S(1)} %all-to-all-done.head_ref, ...), custom_call_target="tpu_custom_call", output_to_operand_aliasing={{3}: (15, {})} | custom-call | bytes 16777216 | tf_op jit(solution)/shard_map/pallas_call | solution.py:28
  44.4 8.0 %all-to-all-start.1 = ((bf16[128,8,128]{2,1,0:T(8,128)(2,1)}), bf16[128,8,128]{2,1,0:T(8,128)(2,1)S(1)}, u32[]{:S(2)}, u32[]{:S(2)}) async-start(bf16[128,8,128]{2,1,0:T(8,128)(2,1)} %bitcast.7), calls=%async_computation.1 | async-start | bytes 524288 | tf_op jit(solution)/shard_map/all_to_all | solution.py:726
  52.5 10.2 %shard_map.134 = (bf16[256,32,256]{2,1,0:T(8,128)(2,1)}, f32[160,16,128]{2,1,0:T(8,128)}) custom-call(bf16[36,256,256]{2,1,0:T(8,128)(2,1)} %get-tuple-element.29.mixed_hbm, f32[256,1]{1,0:T(8,128)S(1)} %copy.16.courant_ref, bf16[256,256]{1,0:T(8,128)(2,1)S(1)} %copy-done, s32[32,256]{1,0:T(8,128)S(1)} %copy-done.2, ...), custom_call_target="tpu_custom_call", output_to_operand_aliasing={{1}: (6, {})} | custom-call | bytes 25165824 | tf_op jit(solution)/shard_map/pallas_call | solution.py:28
  62.7 1.0 %all-to-all-done.1 = bf16[128,8,128]{2,1,0:T(8,128)(2,1)S(1)} async-done(((bf16[128,8,128]{2,1,0:T(8,128)(2,1)}), bf16[128,8,128]{2,1,0:T(8,128)(2,1)S(1)}, u32[]{:S(2)}, u32[]{:S(2)}) %all-to-all-start.1) | async-done | bytes 262176 | tf_op jit(solution)/shard_map/all_to_all | solution.py:726
  63.7 0.8 %shard_map.135 = f32[2,16,128]{2,1,0:T(8,128)} custom-call(bf16[1024,128]{1,0:T(8,128)(2,1)S(1)} %bitcast.9, f32[8,128]{1,0:T(8,128)S(1)} %get-tuple-element.36.slots_ref, s32[16,128]{1,0:T(8,128)S(1)} %copy-done.5), custom_call_target="tpu_custom_call" | custom-call | bytes 1048576 | tf_op jit(solution)/shard_map/pallas_call | solution.py:28
  (7 shorter events, 0.0 us)
Async XLA Ops:
  2.9 32.8 %all-to-all-start = ((bf16[128,24,128]{2,1,0:T(8,128)(2,1)}), bf16[128,24,128]{2,1,0:T(8,128)(2,1)S(1)}, u32[]{:S(2)}, u32[]{:S(2)}) async-start(bf16[128,24,128]{2,1,0:T(8,128)(2,1)} %get-tuple-element.20), calls=%async_computation | async-start | bytes 1572864 | tf_op jit(solution)/shard_map/all_to_all | solution.py:651
  14.4 13.1 %copy-start.9 = (f32[256]{0:T(256)S(1)}, f32[256]{0:T(256)}, u32[]{:S(2)}) copy-start(f32[256]{0:T(256)} %param.13) | copy-start | bytes 3076
  14.4 13.2 %copy-start = (bf16[256,256]{1,0:T(8,128)(2,1)S(1)}, bf16[256,256]{1,0:T(8,128)(2,1)}, u32[]{:S(2)}) copy-start(bf16[256,256]{1,0:T(8,128)(2,1)} %vertical_ref.5) | copy-start | bytes 393220
  14.4 13.2 %copy-start.1 = (f32[160,160]{1,0:T(8,128)S(1)}, f32[160,160]{1,0:T(8,128)}, u32[]{:S(2)}) copy-start(f32[160,160]{1,0:T(8,128)} %ocean_vertical_ref.3) | copy-start | bytes 307204
  14.4 13.2 %copy-start.5 = (s32[16,128]{1,0:T(8,128)S(1)}, s32[16,128]{1,0:T(8,128)}, u32[]{:S(2)}) copy-start(s32[16,128]{1,0:T(8,128)} %sea_ref.7) | copy-start | bytes 24580
  14.4 13.2 %copy-start.6 = (f32[2,16,128]{2,1,0:T(8,128)S(1)}, f32[2,16,128]{2,1,0:T(8,128)}, u32[]{:S(2)}) copy-start(f32[2,16,128]{2,1,0:T(8,128)} %flux_ref.3) | copy-start | bytes 49156
  18.9 16.8 %copy-start.2 = (s32[32,256]{1,0:T(8,128)S(1)}, s32[32,256]{1,0:T(8,128)}, u32[]{:S(2)}) copy-start(s32[32,256]{1,0:T(8,128)} %sea_ref.6) | copy-start | bytes 98308
  18.9 16.8 %copy-start.3 = (bf16[2,256,256]{2,1,0:T(8,128)(2,1)S(1)}, bf16[2,256,256]{2,1,0:T(8,128)(2,1)}, u32[]{:S(2)}) copy-start(bf16[2,256,256]{2,1,0:T(8,128)(2,1)} %get-tuple-element.26.own_a_ref) | copy-start | bytes 786436
  18.9 16.8 %copy-start.4 = (bf16[2,256,256]{2,1,0:T(8,128)(2,1)S(1)}, bf16[2,256,256]{2,1,0:T(8,128)(2,1)}, u32[]{:S(2)}) copy-start(bf16[2,256,256]{2,1,0:T(8,128)(2,1)} %get-tuple-element.27.own_b_ref) | copy-start | bytes 786436
  18.9 16.8 %copy-start.7 = (s32[8,256]{1,0:T(8,128)S(1)}, s32[8,256]{1,0:T(8,128)}, u32[]{:S(2)}) copy-start(s32[8,256]{1,0:T(8,128)} %get-tuple-element.24.place_ref) | copy-start | bytes 24580
  18.9 16.8 %copy-start.8 = (f32[8,128]{1,0:T(8,128)S(1)}, f32[8,128]{1,0:T(8,128)}, u32[]{:S(2)}) copy-start(f32[8,128]{1,0:T(8,128)} %get-tuple-element.21.goal_ref) | copy-start | bytes 12292
  18.9 16.7 %collective-permute-start = (bf16[11,128,128]{2,1,0:T(8,128)(2,1)}, bf16[11,128,128]{2,1,0:T(8,128)(2,1)S(1)}, u32[]{:S(2)}, u32[]{:S(2)}) collective-permute-start(bf16[11,128,128]{2,1,0:T(8,128)(2,1)} %get-tuple-element.22), channel_id=1, source_target_pairs={{0,1},{1,0},{2,3},{3,2},{4,5},{5,4},{6,7},{7,6},{8,9},{9,8},{10,11... | collective-permute-start | bytes 1081352 | tf_op jit(solution)/shard_map/ppermute | solution.py:615
  20.1 15.6 %collective-permute-start.1 = (bf16[11,128,128]{2,1,0:T(8,128)(2,1)}, bf16[11,128,128]{2,1,0:T(8,128)(2,1)S(1)}, u32[]{:S(2)}, u32[]{:S(2)}) collective-permute-start(bf16[11,128,128]{2,1,0:T(8,128)(2,1)} %get-tuple-element.23), channel_id=1, source_target_pairs={{0,127},{1,2},{2,1},{3,4},{4,3},{5,6},{6,5},{7,8},{8,7},{9,10},{10... | collective-permute-start | bytes 1081352 | tf_op jit(solution)/shard_map/ppermute | solution.py:615
  20.8 14.9 %collective-permute-start.2 = (bf16[2,256,256]{2,1,0:T(8,128)(2,1)}, bf16[2,256,256]{2,1,0:T(8,128)(2,1)S(1)}, u32[]{:S(2)}, u32[]{:S(2)}) collective-permute-start(bf16[2,256,256]{2,1,0:T(8,128)(2,1)} %get-tuple-element.26.own_a_ref), channel_id=1, source_target_pairs={{0,1},{1,0},{2,3},{3,2},{4,5},{5,4},{6,7},{7,6},{8,9},{9,8},{10,11... | collective-permute-start | bytes 786440 | tf_op jit(solution)/shard_map/ppermute | solution.py:615
  27.5 8.2 %collective-permute-start.3 = (bf16[2,256,256]{2,1,0:T(8,128)(2,1)}, bf16[2,256,256]{2,1,0:T(8,128)(2,1)S(1)}, u32[]{:S(2)}, u32[]{:S(2)}) collective-permute-start(bf16[2,256,256]{2,1,0:T(8,128)(2,1)} %get-tuple-element.27.own_b_ref), channel_id=1, source_target_pairs={{0,127},{1,2},{2,1},{3,4},{4,3},{5,6},{6,5},{7,8},{8,7},{9,10},{10... | collective-permute-start | bytes 786440 | tf_op jit(solution)/shard_map/ppermute | solution.py:615
  44.4 19.3 %all-to-all-start.1 = ((bf16[128,8,128]{2,1,0:T(8,128)(2,1)}), bf16[128,8,128]{2,1,0:T(8,128)(2,1)S(1)}, u32[]{:S(2)}, u32[]{:S(2)}) async-start(bf16[128,8,128]{2,1,0:T(8,128)(2,1)} %bitcast.7), calls=%async_computation.1 | async-start | bytes 524288 | tf_op jit(solution)/shard_map/all_to_all | solution.py:726

commit v6 on v5

--- a/solution.py
+++ b/solution.py
@@ -106,13 +106,12 @@
 
 
 EDGE_PARTS = 8
-PACK = 192
 
 
 def edges_kernel(
     odd_ref, state_hbm, ocean_hbm, weight_hbm, owner_ref, block_ref, sea_ref,
     state_a_ref, state_b_ref, load_a_ref, load_b_ref, goal_ref,
-    state_ref, ocean_first, ocean_last, state_sems, sems,
+    state_ref, ocean_first, ocean_last, names, state_sems, sems,
 ):
     odd = odd_ref[0]
     levels = state_ref.shape[0] // EDGE_PARTS
@@ -124,21 +123,22 @@
         )
         for n in range(EDGE_PARTS)
     ])
-    tiles = 2 * owner_ref.shape[0]
-    at_a = (1 - odd) * (weight_hbm.shape[0] - tiles)
-    at_b = odd * (weight_hbm.shape[0] - tiles)
+    size = 2 * owner_ref.shape[0] * 128
+    at_a = pl.multiple_of((1 - odd) * (weight_hbm.shape[0] - size), 128)
+    at_b = pl.multiple_of(odd * (weight_hbm.shape[0] - size), 128)
     copies = [
-        pltpu.make_async_copy(weight_hbm.at[pl.ds(at_a, tiles)], load_a_ref.at[0:tiles], sems.at[0]),
-        pltpu.make_async_copy(weight_hbm.at[pl.ds(at_b, tiles)], load_b_ref.at[0:tiles], sems.at[1]),
+        pltpu.make_async_copy(weight_hbm.at[pl.ds(at_a, size)], load_a_ref.at[0:size], sems.at[0]),
+        pltpu.make_async_copy(weight_hbm.at[pl.ds(at_b, size)], load_b_ref.at[0:size], sems.at[1]),
         pltpu.make_async_copy(ocean_hbm.at[:, 0], ocean_first, sems.at[2]),
         pltpu.make_async_copy(ocean_hbm.at[:, ocean_hbm.shape[1] - 1], ocean_last, sems.at[3]),
     ]
     start_all(copies)
     cells = state_ref.shape[1]
-    layers = ocean_first.shape[0]
-    goal = (owner_ref[...] * 16 + block_ref[...]).astype(F32)
-    goal_ref[...] = jnp.zeros_like(goal_ref)
-    goal_ref[0 : goal.shape[0], 0 : goal.shape[1]] = goal
+    count, blocks = owner_ref.shape
+    names[...] = jnp.zeros_like(names)
+    names[0:count, 0:blocks] = owner_ref[...].astype(F32)
+    names[count : 2 * count, 0:blocks] = block_ref[...].astype(F32)
+    goal_ref[...] = goal_of(names[...])
     sea = sea_ref[...].astype(F32)
     width = sea.shape[1] // 2
     row = iota((8, width), 0)
@@ -153,18 +153,12 @@
     lines = sides(odd_ref, sea[0:1], sea[cells - 1 : cells])
     for ref, ocean, line in zip((load_a_ref, load_b_ref), oceans, lines):
         halves = jnp.where(row == 0, line[:, :width], jnp.where(row == 1, line[:, width:], 0.0))
-        empty = jnp.zeros((PACK - layers - 16, width), F32)
-        pack = jnp.concatenate([ocean, halves, goal_ref[...], empty], axis=0)
-        high = pack.astype(BF16)
-        low = (pack - high.astype(F32)).astype(BF16)
-        ref[tiles:] = jnp.concatenate([high, low], axis=0).reshape(
-            2 * PACK // width, width, width
-        )
-
-
-def unpack(load):
-    both = load.reshape(2 * PACK, load.shape[2]).astype(F32)
-    return both[:PACK] + both[PACK:]
+        pack = jnp.concatenate([ocean, halves, names[...]], axis=0)
+        ref[size:, :] = pack.astype(BF16)
+
+
+def goal_of(names):
+    return 16.0 * names + pltpu.roll(names, names.shape[0] // 2, 0)
 
 
 def sides(odd_ref, within, across):
@@ -361,8 +355,10 @@
     slot_rows[...] = head_ref[:, 16:24, :].astype(F32).reshape(devices * 8, 128)
     slots_ref[...] = jnp.transpose(slot_rows[pl.ds(0, devices, stride=8), :])[:8]
 
-    tiles = 2 * sources
-    packs = sides(odd_ref, unpack(within_ref[tiles:]), unpack(across_ref[tiles:]))
+    size = 2 * sources * 128
+    packs = sides(
+        odd_ref, within_ref[size:, :].astype(F32), across_ref[size:, :].astype(F32)
+    )
     for n in range(2):
         ocean_out[n] = packs[n][:layers]
     going.append(pltpu.make_async_copy(ocean_out, ocean_hbm, out_sems.at[1]))
@@ -374,8 +370,8 @@
         goal_ref[...],
         jnp.where(
             lane < blocks + 2,
-            pltpu.roll(left_pack[8:], 2, 1),
-            jnp.where(lane < blocks + 4, pltpu.roll(right_pack[8:], blocks + 2, 1), -1.0),
+            pltpu.roll(goal_of(left_pack[8:]), 2, 1),
+            jnp.where(lane < blocks + 4, pltpu.roll(goal_of(right_pack[8:]), blocks + 2, 1), -1.0),
         ),
     )
     count = blocks + 8
@@ -403,11 +399,10 @@
         return jnp.where(lane == j, jnp.dot(rows, wanted, preferred_element_type=F32), total)
 
     total = jnp.zeros((128, 128), F32)
-    for n, weights in enumerate(sides(odd_ref, within_ref[0:tiles], across_ref[0:tiles])):
+    for n, weights in enumerate(sides(odd_ref, within_ref[0:size, :], across_ref[0:size, :])):
+        tiles = [weights[t * 128 : (t + 1) * 128] for t in range(2 * sources)]
         for b in range(2):
-            total = add(
-                blocks + 2 * n + b, [weights[b * sources + k] for k in range(sources)], total
-            )
+            total = add(blocks + 2 * n + b, tiles[b * sources : (b + 1) * sources], total)
     step = blocks // PARTS
     for i, c in enumerate(copies):
         c.wait()
@@ -650,13 +645,12 @@
     )
     gathered = lax.all_to_all(head, BOTH, split_axis=0, concat_axis=0, tiled=True)
 
-    tiles = 2 * sources
     columns_sent = shape((2, height, width), BF16)
-    load = shape((tiles + 2 * PACK // 128, 128, 128), BF16)
+    load = shape((2 * sources * 128 + layers + 16, 128), BF16)
     state_a, state_b, load_a, load_b, goal = call(
         edges_kernel,
         (columns_sent, columns_sent, load, load, shape((8, 128), F32)),
-        odd, atm_state, ocean_state, remap_weight.reshape(pairs, 128, 128), owner, block, atm_sea,
+        odd, atm_state, ocean_state, remap_weight.reshape(pairs * 128, 128), owner, block, atm_sea,
         specs={
             0: SCALAR,
             1: ANY,
@@ -667,6 +661,7 @@
             pltpu.VMEM(atm_state.shape, BF16),
             pltpu.VMEM((layers, ocean_width), F32),
             pltpu.VMEM((layers, ocean_width), F32),
+            pltpu.VMEM((8, 128), F32),
             dma((EDGE_PARTS,)),
             dma((4,)),
         ],

time: 64.8 us -> 64.8 us (level)
  no operation moved by 1% of the time
where the time goes in v6:
time: 64.8 us; the launch traced here: 64.5 us
  Pallas kernels  34.3 us (53%)
  starting transfers between devices  28.1 us (43%)
  waiting for transfers between devices  1.04 us (2%)
  between operations  0.89 us (1%)
    pallas_call x6, Pallas kernels, call(): pl.pallas_call(kernel, out_shape=outs, grid=grid, in_specs=[specs.get(i,...  34.3 us
    all_to_all x1, starting transfers between devices, per_device(): lax.all_to_all(head, BOTH, split_axis=0, concat_axis=0, tiled=True)  11.5 us
    ppermute x4, starting transfers between devices, swap(): return (lax.ppermute(within, BOTH, pair), lax.ppermute(across, BOTH, other))  8.57 us
    all_to_all x1, starting transfers between devices, per_device(): lax.all_to_all(outgoing.reshape(devices, 8, 128), BOTH, split_axis=0, con...  8.05 us
  transfers between devices with their start and end apart: 6, of which 1 were waited for; matrix products, arithmetic and copies ran while one was open for 0% of the time, Pallas kernels for 35%

profile of v6, /device:TPU:1, one launch (start us, length us, event | category | flops | bytes accessed | tf_op | source)
XLA Modules:
  0.0 64.5 jit_solution(645650991503362158)
XLA Ops:
  0.6 2.2 %shard_map.130 = (bf16[128,24,128]{2,1,0:T(8,128)(2,1)}, s32[8,256]{1,0:T(8,128)}) custom-call(s32[4,64]{1,0:T(4,128)} %bitcast.13, s32[4,64]{1,0:T(4,128)} %bitcast.15, f32[160,16,128]{2,1,0:T(8,128)} %ocean_hbm.5), custom_call_target="tpu_custom_call" | custom-call | bytes 1048576 | tf_op jit(solution)/shard_map/pallas_call | solution.py:28
  2.9 11.5 %all-to-all-start = ((bf16[128,24,128]{2,1,0:T(8,128)(2,1)}), bf16[128,24,128]{2,1,0:T(8,128)(2,1)S(1)}, u32[]{:S(2)}, u32[]{:S(2)}) async-start(bf16[128,24,128]{2,1,0:T(8,128)(2,1)} %get-tuple-element.20), calls=%async_computation | async-start | bytes 1572864 | tf_op jit(solution)/shard_map/all_to_all | solution.py:646
  14.4 0.0 copy-start.9
  14.4 0.0 copy-start
  14.4 0.0 copy-start.1
  14.4 0.0 copy-start.5
  14.4 0.0 copy-start.6
  14.4 4.4 %shard_map.131 = (bf16[2,256,256]{2,1,0:T(8,128)(2,1)}, bf16[2,256,256]{2,1,0:T(8,128)(2,1)}, bf16[1200,128]{1,0:T(8,128)(2,1)}, bf16[1200,128]{1,0:T(8,128)(2,1)}, f32[8,128]{1,0:T(8,128)}) custom-call(s32[1]{0:T(128)} %bitcast.odd_ref, bf16[256,32,256]{2,1,0:T(8,128)(2,1)} %state_hbm.3, f32[160,16,128]{2,1,0:T(8,128)} %ocean_hbm.5, ...), custom_call_target="tpu_custom_call" | custom-call | bytes 6291456 | tf_op jit(solution)/shard_map/pallas_call | solution.py:28
  18.9 0.0 copy-start.2
  18.9 0.0 copy-start.3
  18.9 0.0 copy-start.7
  18.9 1.1 %collective-permute-start = (bf16[1200,128]{1,0:T(8,128)(2,1)}, bf16[1200,128]{1,0:T(8,128)(2,1)S(1)}, u32[]{:S(2)}, u32[]{:S(2)}) collective-permute-start(bf16[1200,128]{1,0:T(8,128)(2,1)} %get-tuple-element.22), channel_id=1, source_target_pairs={{0,1},{1,0},{2,3},{3,2},{4,5},{5,4},{6,7},{7,6},{8,9},{9,8},{10,11... | collective-permute-start | bytes 921608 | tf_op jit(solution)/shard_map/ppermute | solution.py:610
  20.1 0.7 %collective-permute-start.1 = (bf16[1200,128]{1,0:T(8,128)(2,1)}, bf16[1200,128]{1,0:T(8,128)(2,1)S(1)}, u32[]{:S(2)}, u32[]{:S(2)}) collective-permute-start(bf16[1200,128]{1,0:T(8,128)(2,1)} %get-tuple-element.23), channel_id=1, source_target_pairs={{0,127},{1,2},{2,1},{3,4},{4,3},{5,6},{6,5},{7,8},{8,7},{9,10},{10... | collective-permute-start | bytes 921608 | tf_op jit(solution)/shard_map/ppermute | solution.py:610
  20.8 6.7 %collective-permute-start.2 = (bf16[2,256,256]{2,1,0:T(8,128)(2,1)}, bf16[2,256,256]{2,1,0:T(8,128)(2,1)S(1)}, u32[]{:S(2)}, u32[]{:S(2)}) collective-permute-start(bf16[2,256,256]{2,1,0:T(8,128)(2,1)} %get-tuple-element.26.own_a_ref), channel_id=1, source_target_pairs={{0,1},{1,0},{2,3},{3,2},{4,5},{5,4},{6,7},{7,6},{8,9},{9,8},{10,11... | collective-permute-start | bytes 786440 | tf_op jit(solution)/shard_map/ppermute | solution.py:610
  27.5 0.0 collective-permute-start.3
  27.5 0.1 copy.16.courant_ref
  27.7 8.0 %shard_map.132 = (bf16[36,256,256]{2,1,0:T(8,128)(2,1)}, f32[4,32,256]{2,1,0:T(8,128)S(1)}, f32[2560,128]{1,0:T(8,128)}) custom-call(bf16[256,32,256]{2,1,0:T(8,128)(2,1)} %state_hbm.3, f32[256,1]{1,0:T(8,128)S(1)} %copy.16.courant_ref, bf16[256,256]{1,0:T(8,128)(2,1)S(1)} %copy-done, f32[2560,128]{1,0:T(8,128)} %bitcast.11, s32[16,128]{1,0:T(8,128)S(1)} %copy-done.5, ...), custom_call_target="tpu_custom_call" | custom-call | bytes 16777216 | tf_op jit(solution)/shard_map/pallas_call | solution.py:28
  35.6 0.0 collective-permute-done.2.near_within_ref
  35.6 0.0 collective-permute-done.3.near_across_ref
  35.7 0.0 collective-permute-done.within_ref
  35.7 0.0 collective-permute-done.1.across_ref
  35.7 0.0 all-to-all-done.head_ref
  35.7 0.0 copy-done.2
  35.7 0.0 copy-done.3
  35.7 0.0 copy-done.4
  35.7 0.0 copy-done.7
  35.7 0.0 copy-done.8
  35.7 8.7 %shard_map.133 = (f32[104,256]{1,0:T(8,128)S(1)}, f32[8,128]{1,0:T(8,128)S(1)}, bf16[1024,128]{1,0:T(8,128)(2,1)}, bf16[36,256,256]{2,1,0:T(8,128)(2,1)}, f32[2,160,128]{2,1,0:T(8,128)S(1)}) custom-call(s32[1]{0:T(128)} %bitcast.odd_ref, bf16[128,24,128]{2,1,0:T(8,128)(2,1)S(1)} %all-to-all-done.head_ref, ...), custom_call_target="tpu_custom_call", output_to_operand_aliasing={{3}: (15, {})} | custom-call | bytes 16777216 | tf_op jit(solution)/shard_map/pallas_call | solution.py:28
  44.4 8.1 %all-to-all-start.1 = ((bf16[128,8,128]{2,1,0:T(8,128)(2,1)}), bf16[128,8,128]{2,1,0:T(8,128)(2,1)S(1)}, u32[]{:S(2)}, u32[]{:S(2)}) async-start(bf16[128,8,128]{2,1,0:T(8,128)(2,1)} %bitcast.7), calls=%async_computation.1 | async-start | bytes 524288 | tf_op jit(solution)/shard_map/all_to_all | solution.py:721
  52.5 10.2 %shard_map.134 = (bf16[256,32,256]{2,1,0:T(8,128)(2,1)}, f32[160,16,128]{2,1,0:T(8,128)}) custom-call(bf16[36,256,256]{2,1,0:T(8,128)(2,1)} %get-tuple-element.29.mixed_hbm, f32[256,1]{1,0:T(8,128)S(1)} %copy.16.courant_ref, bf16[256,256]{1,0:T(8,128)(2,1)S(1)} %copy-done, s32[32,256]{1,0:T(8,128)S(1)} %copy-done.2, ...), custom_call_target="tpu_custom_call", output_to_operand_aliasing={{1}: (6, {})} | custom-call | bytes 25165824 | tf_op jit(solution)/shard_map/pallas_call | solution.py:28
  62.7 1.0 %all-to-all-done.1 = bf16[128,8,128]{2,1,0:T(8,128)(2,1)S(1)} async-done(((bf16[128,8,128]{2,1,0:T(8,128)(2,1)}), bf16[128,8,128]{2,1,0:T(8,128)(2,1)S(1)}, u32[]{:S(2)}, u32[]{:S(2)}) %all-to-all-start.1) | async-done | bytes 262176 | tf_op jit(solution)/shard_map/all_to_all | solution.py:721
  63.7 0.8 %shard_map.135 = f32[2,16,128]{2,1,0:T(8,128)} custom-call(bf16[1024,128]{1,0:T(8,128)(2,1)S(1)} %bitcast.9, f32[8,128]{1,0:T(8,128)S(1)} %get-tuple-element.36.slots_ref, s32[16,128]{1,0:T(8,128)S(1)} %copy-done.5), custom_call_target="tpu_custom_call" | custom-call | bytes 1048576 | tf_op jit(solution)/shard_map/pallas_call | solution.py:28
  (7 shorter events, 0.0 us)
Async XLA Ops:
  2.9 32.8 %all-to-all-start = ((bf16[128,24,128]{2,1,0:T(8,128)(2,1)}), bf16[128,24,128]{2,1,0:T(8,128)(2,1)S(1)}, u32[]{:S(2)}, u32[]{:S(2)}) async-start(bf16[128,24,128]{2,1,0:T(8,128)(2,1)} %get-tuple-element.20), calls=%async_computation | async-start | bytes 1572864 | tf_op jit(solution)/shard_map/all_to_all | solution.py:646
  14.4 13.1 %copy-start.9 = (f32[256]{0:T(256)S(1)}, f32[256]{0:T(256)}, u32[]{:S(2)}) copy-start(f32[256]{0:T(256)} %param.13) | copy-start | bytes 3076
  14.4 13.2 %copy-start = (bf16[256,256]{1,0:T(8,128)(2,1)S(1)}, bf16[256,256]{1,0:T(8,128)(2,1)}, u32[]{:S(2)}) copy-start(bf16[256,256]{1,0:T(8,128)(2,1)} %vertical_ref.5) | copy-start | bytes 393220
  14.4 13.2 %copy-start.1 = (f32[160,160]{1,0:T(8,128)S(1)}, f32[160,160]{1,0:T(8,128)}, u32[]{:S(2)}) copy-start(f32[160,160]{1,0:T(8,128)} %ocean_vertical_ref.3) | copy-start | bytes 307204
  14.4 13.2 %copy-start.5 = (s32[16,128]{1,0:T(8,128)S(1)}, s32[16,128]{1,0:T(8,128)}, u32[]{:S(2)}) copy-start(s32[16,128]{1,0:T(8,128)} %sea_ref.7) | copy-start | bytes 24580
  14.4 13.2 %copy-start.6 = (f32[2,16,128]{2,1,0:T(8,128)S(1)}, f32[2,16,128]{2,1,0:T(8,128)}, u32[]{:S(2)}) copy-start(f32[2,16,128]{2,1,0:T(8,128)} %flux_ref.3) | copy-start | bytes 49156
  18.9 16.8 %copy-start.2 = (s32[32,256]{1,0:T(8,128)S(1)}, s32[32,256]{1,0:T(8,128)}, u32[]{:S(2)}) copy-start(s32[32,256]{1,0:T(8,128)} %sea_ref.6) | copy-start | bytes 98308
  18.9 16.8 %copy-start.3 = (bf16[2,256,256]{2,1,0:T(8,128)(2,1)S(1)}, bf16[2,256,256]{2,1,0:T(8,128)(2,1)}, u32[]{:S(2)}) copy-start(bf16[2,256,256]{2,1,0:T(8,128)(2,1)} %get-tuple-element.26.own_a_ref) | copy-start | bytes 786436
  18.9 16.8 %copy-start.4 = (bf16[2,256,256]{2,1,0:T(8,128)(2,1)S(1)}, bf16[2,256,256]{2,1,0:T(8,128)(2,1)}, u32[]{:S(2)}) copy-start(bf16[2,256,256]{2,1,0:T(8,128)(2,1)} %get-tuple-element.27.own_b_ref) | copy-start | bytes 786436
  18.9 16.8 %copy-start.7 = (s32[8,256]{1,0:T(8,128)S(1)}, s32[8,256]{1,0:T(8,128)}, u32[]{:S(2)}) copy-start(s32[8,256]{1,0:T(8,128)} %get-tuple-element.24.place_ref) | copy-start | bytes 24580
  18.9 16.8 %copy-start.8 = (f32[8,128]{1,0:T(8,128)S(1)}, f32[8,128]{1,0:T(8,128)}, u32[]{:S(2)}) copy-start(f32[8,128]{1,0:T(8,128)} %get-tuple-element.21.goal_ref) | copy-start | bytes 12292
  18.9 16.7 %collective-permute-start = (bf16[1200,128]{1,0:T(8,128)(2,1)}, bf16[1200,128]{1,0:T(8,128)(2,1)S(1)}, u32[]{:S(2)}, u32[]{:S(2)}) collective-permute-start(bf16[1200,128]{1,0:T(8,128)(2,1)} %get-tuple-element.22), channel_id=1, source_target_pairs={{0,1},{1,0},{2,3},{3,2},{4,5},{5,4},{6,7},{7,6},{8,9},{9,8},{10,11... | collective-permute-start | bytes 921608 | tf_op jit(solution)/shard_map/ppermute | solution.py:610
  20.1 15.6 %collective-permute-start.1 = (bf16[1200,128]{1,0:T(8,128)(2,1)}, bf16[1200,128]{1,0:T(8,128)(2,1)S(1)}, u32[]{:S(2)}, u32[]{:S(2)}) collective-permute-start(bf16[1200,128]{1,0:T(8,128)(2,1)} %get-tuple-element.23), channel_id=1, source_target_pairs={{0,127},{1,2},{2,1},{3,4},{4,3},{5,6},{6,5},{7,8},{8,7},{9,10},{10... | collective-permute-start | bytes 921608 | tf_op jit(solution)/shard_map/ppermute | solution.py:610
  20.8 14.9 %collective-permute-start.2 = (bf16[2,256,256]{2,1,0:T(8,128)(2,1)}, bf16[2,256,256]{2,1,0:T(8,128)(2,1)S(1)}, u32[]{:S(2)}, u32[]{:S(2)}) collective-permute-start(bf16[2,256,256]{2,1,0:T(8,128)(2,1)} %get-tuple-element.26.own_a_ref), channel_id=1, source_target_pairs={{0,1},{1,0},{2,3},{3,2},{4,5},{5,4},{6,7},{7,6},{8,9},{9,8},{10,11... | collective-permute-start | bytes 786440 | tf_op jit(solution)/shard_map/ppermute | solution.py:610
  27.5 8.2 %collective-permute-start.3 = (bf16[2,256,256]{2,1,0:T(8,128)(2,1)}, bf16[2,256,256]{2,1,0:T(8,128)(2,1)S(1)}, u32[]{:S(2)}, u32[]{:S(2)}) collective-permute-start(bf16[2,256,256]{2,1,0:T(8,128)(2,1)} %get-tuple-element.27.own_b_ref), channel_id=1, source_target_pairs={{0,127},{1,2},{2,1},{3,4},{4,3},{5,6},{6,5},{7,8},{8,7},{9,10},{10... | collective-permute-start | bytes 786440 | tf_op jit(solution)/shard_map/ppermute | solution.py:610
  44.4 19.3 %all-to-all-start.1 = ((bf16[128,8,128]{2,1,0:T(8,128)(2,1)}), bf16[128,8,128]{2,1,0:T(8,128)(2,1)S(1)}, u32[]{:S(2)}, u32[]{:S(2)}) async-start(bf16[128,8,128]{2,1,0:T(8,128)(2,1)} %bitcast.7), calls=%async_computation.1 | async-start | bytes 524288 | tf_op jit(solution)/shard_map/all_to_all | solution.py:721

commit v7 on v3

--- a/solution.py
+++ b/solution.py
@@ -595,7 +595,7 @@
     dma = pltpu.SemaphoreType.DMA
     held = [pltpu.VMEM(remap_weight.shape, BF16), dma((PARTS,))]
     whole = pltpu.VMEM((cells, height, width), BF16)
-    levels = 64
+    levels = 128
 
     head, place = call(
         plan_kernel,

time: 64.6 us -> 64.3 us (level)
  no operation moved by 1% of the time
where the time goes in v7:
time: 64.3 us; the launch traced here: 64 us
  Pallas kernels  32.7 us (51%)
  starting transfers between devices  29.5 us (46%)
  between operations  0.9 us (1%)
  waiting for transfers between devices  0.72 us (1%)
    pallas_call x7, Pallas kernels, call(): pl.pallas_call(kernel, out_shape=outs, grid=grid, in_specs=[specs.get(i,...  32.7 us
    all_to_all x1, starting transfers between devices, per_device(): lax.all_to_all(head, BOTH, split_axis=0, concat_axis=0, tiled=True)  11.5 us
    all_to_all x1, starting transfers between devices, per_device(): lax.all_to_all(outgoing.reshape(devices, 8, 128), BOTH, split_axis=0, con...  9.44 us
    ppermute x4, starting transfers between devices, swap(): return (lax.ppermute(within, BOTH, pair), lax.ppermute(across, BOTH, other))  8.57 us
  transfers between devices with their start and end apart: 6, of which 1 were waited for; matrix products, arithmetic and copies ran while one was open for 0% of the time, Pallas kernels for 34%

profile of v7, /device:TPU:1, one launch (start us, length us, event | category | flops | bytes accessed | tf_op | source)
XLA Modules:
  0.0 64.0 jit_solution(17158305196922583571)
XLA Ops:
  0.6 2.2 %shard_map.133 = (bf16[128,24,128]{2,1,0:T(8,128)(2,1)}, s32[8,256]{1,0:T(8,128)}) custom-call(s32[4,64]{1,0:T(4,128)} %bitcast.12, s32[4,64]{1,0:T(4,128)} %bitcast.14, f32[160,16,128]{2,1,0:T(8,128)} %ocean_hbm.3), custom_call_target="tpu_custom_call" | custom-call | bytes 1048576 | tf_op jit(solution)/shard_map/pallas_call | solution.py:28
  2.9 11.5 %all-to-all-start = ((bf16[128,24,128]{2,1,0:T(8,128)(2,1)}), bf16[128,24,128]{2,1,0:T(8,128)(2,1)S(1)}, u32[]{:S(2)}, u32[]{:S(2)}) async-start(bf16[128,24,128]{2,1,0:T(8,128)(2,1)} %get-tuple-element.23), calls=%async_computation | async-start | bytes 1572864 | tf_op jit(solution)/shard_map/all_to_all | solution.py:616
  14.4 0.0 copy-start.9
  14.4 0.0 copy-start
  14.4 4.0 %shard_map.131 = (bf16[2,256,256]{2,1,0:T(8,128)(2,1)}, bf16[2,256,256]{2,1,0:T(8,128)(2,1)}, bf16[11,128,128]{2,1,0:T(8,128)(2,1)}, bf16[11,128,128]{2,1,0:T(8,128)(2,1)}, f32[8,128]{1,0:T(8,128)}) custom-call(s32[1]{0:T(128)} %bitcast.odd_ref, bf16[256,32,256]{2,1,0:T(8,128)(2,1)} %state_ref.1, f32[160,16,128]{2,1,0:T(8,128)} %ocean_hbm.3, ...), custom_call_target="tpu_custom_call" | custom-call | bytes 6291456 | tf_op jit(solution)/shard_map/pallas_call | solution.py:28
  18.4 0.0 copy-start.2
  18.4 0.0 copy-start.3
  18.4 0.0 copy-start.1
  18.4 0.0 copy-start.7
  18.5 1.1 %collective-permute-start.2 = (bf16[11,128,128]{2,1,0:T(8,128)(2,1)}, bf16[11,128,128]{2,1,0:T(8,128)(2,1)S(1)}, u32[]{:S(2)}, u32[]{:S(2)}) collective-permute-start(bf16[11,128,128]{2,1,0:T(8,128)(2,1)} %get-tuple-element.25), channel_id=1, source_target_pairs={{0,1},{1,0},{2,3},{3,2},{4,5},{5,4},{6,7},{7,6},{8,9},{9,8},{10,11... | collective-permute-start | bytes 1081352 | tf_op jit(solution)/shard_map/ppermute | solution.py:579
  19.6 0.7 %collective-permute-start.3 = (bf16[11,128,128]{2,1,0:T(8,128)(2,1)}, bf16[11,128,128]{2,1,0:T(8,128)(2,1)S(1)}, u32[]{:S(2)}, u32[]{:S(2)}) collective-permute-start(bf16[11,128,128]{2,1,0:T(8,128)(2,1)} %get-tuple-element.26), channel_id=1, source_target_pairs={{0,127},{1,2},{2,1},{3,4},{4,3},{5,6},{6,5},{7,8},{8,7},{9,10},{10... | collective-permute-start | bytes 1081352 | tf_op jit(solution)/shard_map/ppermute | solution.py:579
  20.3 6.7 %collective-permute-start = (bf16[2,256,256]{2,1,0:T(8,128)(2,1)}, bf16[2,256,256]{2,1,0:T(8,128)(2,1)S(1)}, u32[]{:S(2)}, u32[]{:S(2)}) collective-permute-start(bf16[2,256,256]{2,1,0:T(8,128)(2,1)} %get-tuple-element.20.own_a_ref), channel_id=1, source_target_pairs={{0,1},{1,0},{2,3},{3,2},{4,5},{5,4},{6,7},{7,6},{8,9},{9,8},{10,11... | collective-permute-start | bytes 786440 | tf_op jit(solution)/shard_map/ppermute | solution.py:579
  27.0 0.0 collective-permute-start.1
  27.0 0.1 copy.14.courant_ref
  27.2 6.5 %shard_map.130 = (bf16[32,256,256]{2,1,0:T(8,128)(2,1)}, f32[4,32,256]{2,1,0:T(8,128)S(1)}) custom-call(bf16[256,32,256]{2,1,0:T(8,128)(2,1)} %state_ref.1, f32[256,1]{1,0:T(8,128)S(1)} %copy.14.courant_ref, bf16[256,256]{1,0:T(8,128)(2,1)S(1)} %copy-done), custom_call_target="tpu_custom_call" | custom-call | bytes 16777216 | tf_op jit(solution)/shard_map/pallas_call | solution.py:28
  33.7 0.0 collective-permute-done.within_ref
  33.7 0.0 collective-permute-done.1.across_ref
  33.8 0.8 %shard_map.132 = (bf16[4,256,256]{2,1,0:T(8,128)(2,1)S(1)}, f32[4,8,256]{2,1,0:T(8,128)S(1)}) custom-call(s32[1]{0:T(128)} %bitcast.odd_ref, bf16[2,256,256]{2,1,0:T(8,128)(2,1)S(1)} %collective-permute-done.within_ref, bf16[2,256,256]{2,1,0:T(8,128)(2,1)S(1)} %collective-permute-done.1.across_ref, bf16[2,256,256]{2,1,0:T(8,128)(2,1)S(1)} %copy-done.2, ...), custom_call_target="tpu_custom_call" | custom-call | bytes 2097152 | tf_op jit(solution)/shard_map/pallas_call | solution.py:28
  34.6 0.0 collective-permute-done.2.within_ref
  34.6 0.0 collective-permute-done.3.across_ref
  34.6 0.0 all-to-all-done.head_ref
  34.6 0.0 copy-done.1
  34.6 0.0 copy-done.7
  34.6 0.0 copy-done.8
  34.6 0.0 copy-start.4
  34.7 0.0 copy-start.5
  34.7 0.0 copy-start.6
  34.7 7.8 %shard_map.134 = (f32[104,256]{1,0:T(8,128)S(1)}, f32[8,128]{1,0:T(8,128)S(1)}, bf16[1024,128]{1,0:T(8,128)(2,1)}) custom-call(s32[1]{0:T(128)} %bitcast.odd_ref, bf16[128,24,128]{2,1,0:T(8,128)(2,1)S(1)} %all-to-all-done.head_ref, f32[8,128]{1,0:T(8,128)S(1)} %copy-done.8, bf16[11,128,128]{2,1,0:T(8,128)(2,1)S(1)} %collective-permute-done.2.within_ref, ...), custom_call_target="tpu_custom_call" | custom-call | bytes 16777216 | tf_op jit(solution)/shard_map/pallas_call | solution.py:28
  42.5 9.4 %all-to-all-start.1 = ((bf16[128,8,128]{2,1,0:T(8,128)(2,1)}), bf16[128,8,128]{2,1,0:T(8,128)(2,1)S(1)}, u32[]{:S(2)}, u32[]{:S(2)}) async-start(bf16[128,8,128]{2,1,0:T(8,128)(2,1)} %bitcast.7), calls=%async_computation.1 | async-start | bytes 524288 | tf_op jit(solution)/shard_map/all_to_all | solution.py:681
  52.0 10.5 %shard_map.135 = (bf16[256,32,256]{2,1,0:T(8,128)(2,1)}, f32[2560,128]{1,0:T(8,128)}) custom-call(s32[1]{0:T(128)} %bitcast.odd_ref, bf16[32,256,256]{2,1,0:T(8,128)(2,1)} %get-tuple-element.19.mixed_hbm, bf16[4,256,256]{2,1,0:T(8,128)(2,1)S(1)} %get-tuple-element.22.edge_hbm, f32[256,1]{1,0:T(8,128)S(1)} %copy.14.courant_ref, bf16[256,256]{1,0:T(8,128)(2,1)S(1)} %copy-done, ...), custom_call_target="tpu_custom_call" | custom-call | bytes 25165824 | tf_op jit(solution)/shard_map/pallas_call | solution.py:28
  62.4 0.7 %all-to-all-done.1 = bf16[128,8,128]{2,1,0:T(8,128)(2,1)S(1)} async-done(((bf16[128,8,128]{2,1,0:T(8,128)(2,1)}), bf16[128,8,128]{2,1,0:T(8,128)(2,1)S(1)}, u32[]{:S(2)}, u32[]{:S(2)}) %all-to-all-start.1) | async-done | bytes 262176 | tf_op jit(solution)/shard_map/all_to_all | solution.py:681
  63.2 0.8 %shard_map.136 = f32[2,16,128]{2,1,0:T(8,128)} custom-call(bf16[1024,128]{1,0:T(8,128)(2,1)S(1)} %bitcast.9, f32[8,128]{1,0:T(8,128)S(1)} %get-tuple-element.34.slots_ref, s32[16,128]{1,0:T(8,128)S(1)} %copy-done.5), custom_call_target="tpu_custom_call" | custom-call | bytes 1048576 | tf_op jit(solution)/shard_map/pallas_call | solution.py:28
  (8 shorter events, 0.0 us)
Async XLA Ops:
  2.9 31.7 %all-to-all-start = ((bf16[128,24,128]{2,1,0:T(8,128)(2,1)}), bf16[128,24,128]{2,1,0:T(8,128)(2,1)S(1)}, u32[]{:S(2)}, u32[]{:S(2)}) async-start(bf16[128,24,128]{2,1,0:T(8,128)(2,1)} %get-tuple-element.23), calls=%async_computation | async-start | bytes 1572864 | tf_op jit(solution)/shard_map/all_to_all | solution.py:616
  14.4 12.6 %copy-start.9 = (f32[256]{0:T(256)S(1)}, f32[256]{0:T(256)}, u32[]{:S(2)}) copy-start(f32[256]{0:T(256)} %param.13) | copy-start | bytes 3076
  14.4 12.8 %copy-start = (bf16[256,256]{1,0:T(8,128)(2,1)S(1)}, bf16[256,256]{1,0:T(8,128)(2,1)}, u32[]{:S(2)}) copy-start(bf16[256,256]{1,0:T(8,128)(2,1)} %vertical_ref.7) | copy-start | bytes 393220
  18.4 15.4 %copy-start.2 = (bf16[2,256,256]{2,1,0:T(8,128)(2,1)S(1)}, bf16[2,256,256]{2,1,0:T(8,128)(2,1)}, u32[]{:S(2)}) copy-start(bf16[2,256,256]{2,1,0:T(8,128)(2,1)} %get-tuple-element.20.own_a_ref) | copy-start | bytes 786436
  18.4 15.4 %copy-start.3 = (bf16[2,256,256]{2,1,0:T(8,128)(2,1)S(1)}, bf16[2,256,256]{2,1,0:T(8,128)(2,1)}, u32[]{:S(2)}) copy-start(bf16[2,256,256]{2,1,0:T(8,128)(2,1)} %get-tuple-element.21.own_b_ref) | copy-start | bytes 786436
  18.4 16.2 %copy-start.1 = (s32[32,256]{1,0:T(8,128)S(1)}, s32[32,256]{1,0:T(8,128)}, u32[]{:S(2)}) copy-start(s32[32,256]{1,0:T(8,128)} %sea_ref.6) | copy-start | bytes 98308
  18.4 16.2 %copy-start.7 = (s32[8,256]{1,0:T(8,128)S(1)}, s32[8,256]{1,0:T(8,128)}, u32[]{:S(2)}) copy-start(s32[8,256]{1,0:T(8,128)} %get-tuple-element.27.place_ref) | copy-start | bytes 24580
  18.5 16.2 %copy-start.8 = (f32[8,128]{1,0:T(8,128)S(1)}, f32[8,128]{1,0:T(8,128)}, u32[]{:S(2)}) copy-start(f32[8,128]{1,0:T(8,128)} %get-tuple-element.24.goal_ref) | copy-start | bytes 12292
  18.5 16.1 %collective-permute-start.2 = (bf16[11,128,128]{2,1,0:T(8,128)(2,1)}, bf16[11,128,128]{2,1,0:T(8,128)(2,1)S(1)}, u32[]{:S(2)}, u32[]{:S(2)}) collective-permute-start(bf16[11,128,128]{2,1,0:T(8,128)(2,1)} %get-tuple-element.25), channel_id=1, source_target_pairs={{0,1},{1,0},{2,3},{3,2},{4,5},{5,4},{6,7},{7,6},{8,9},{9,8},{10,11... | collective-permute-start | bytes 1081352 | tf_op jit(solution)/shard_map/ppermute | solution.py:579
  19.6 15.0 %collective-permute-start.3 = (bf16[11,128,128]{2,1,0:T(8,128)(2,1)}, bf16[11,128,128]{2,1,0:T(8,128)(2,1)S(1)}, u32[]{:S(2)}, u32[]{:S(2)}) collective-permute-start(bf16[11,128,128]{2,1,0:T(8,128)(2,1)} %get-tuple-element.26), channel_id=1, source_target_pairs={{0,127},{1,2},{2,1},{3,4},{4,3},{5,6},{6,5},{7,8},{8,7},{9,10},{10... | collective-permute-start | bytes 1081352 | tf_op jit(solution)/shard_map/ppermute | solution.py:579
  20.3 13.4 %collective-permute-start = (bf16[2,256,256]{2,1,0:T(8,128)(2,1)}, bf16[2,256,256]{2,1,0:T(8,128)(2,1)S(1)}, u32[]{:S(2)}, u32[]{:S(2)}) collective-permute-start(bf16[2,256,256]{2,1,0:T(8,128)(2,1)} %get-tuple-element.20.own_a_ref), channel_id=1, source_target_pairs={{0,1},{1,0},{2,3},{3,2},{4,5},{5,4},{6,7},{7,6},{8,9},{9,8},{10,11... | collective-permute-start | bytes 786440 | tf_op jit(solution)/shard_map/ppermute | solution.py:579
  27.0 6.7 %collective-permute-start.1 = (bf16[2,256,256]{2,1,0:T(8,128)(2,1)}, bf16[2,256,256]{2,1,0:T(8,128)(2,1)S(1)}, u32[]{:S(2)}, u32[]{:S(2)}) collective-permute-start(bf16[2,256,256]{2,1,0:T(8,128)(2,1)} %get-tuple-element.21.own_b_ref), channel_id=1, source_target_pairs={{0,127},{1,2},{2,1},{3,4},{4,3},{5,6},{6,5},{7,8},{8,7},{9,10},{10... | collective-permute-start | bytes 786440 | tf_op jit(solution)/shard_map/ppermute | solution.py:579
  34.6 17.3 %copy-start.4 = (f32[160,160]{1,0:T(8,128)S(1)}, f32[160,160]{1,0:T(8,128)}, u32[]{:S(2)}) copy-start(f32[160,160]{1,0:T(8,128)} %ocean_vertical_ref.1) | copy-start | bytes 307204
  34.7 17.3 %copy-start.5 = (s32[16,128]{1,0:T(8,128)S(1)}, s32[16,128]{1,0:T(8,128)}, u32[]{:S(2)}) copy-start(s32[16,128]{1,0:T(8,128)} %sea_ref.7) | copy-start | bytes 24580
  34.7 17.3 %copy-start.6 = (f32[2,16,128]{2,1,0:T(8,128)S(1)}, f32[2,16,128]{2,1,0:T(8,128)}, u32[]{:S(2)}) copy-start(f32[2,16,128]{2,1,0:T(8,128)} %flux_ref.1) | copy-start | bytes 49156
  42.5 20.7 %all-to-all-start.1 = ((bf16[128,8,128]{2,1,0:T(8,128)(2,1)}), bf16[128,8,128]{2,1,0:T(8,128)(2,1)S(1)}, u32[]{:S(2)}, u32[]{:S(2)}) async-start(bf16[128,8,128]{2,1,0:T(8,128)(2,1)} %bitcast.7), calls=%async_computation.1 | async-start | bytes 524288 | tf_op jit(solution)/shard_map/all_to_all | solution.py:681
